TPU v7x, 256 devices: a whole 4x4x8 slice. The times are simulated.
256 devices in a mesh: dp: 64 (over x, z, core), rep: 4 (over y).
Axes of the slice: x: 4, y: 4, z: 8, core: 2. Of those that a mesh axis runs over, the one named last changes fastest.
Arguments:
- query_hidden: bfloat16 [512, 32, 768], P(('dp', 'rep')), may hold values from -6 to 6
- passage_hidden: bfloat16 [2048, 180, 768], P(('dp', 'rep')), may hold values from -6 to 6
- projection: bfloat16 [768, 128], replicated, may hold values from -0.21875 to 0.21875
- negatives: int32 [512, 128], P(('dp', 'rep')), may hold values from 0 to 2047, as said below
- positions: int32 [512, 128, 32], P(('dp', 'rep')), may hold values from 0 to 179
- teacher: float32 [512, 128], P(('dp', 'rep')), may hold values from -8 to 8
Outputs:
- grad_passages: bfloat16 [2048, 180, 128], P(('dp', 'rep'))
- grad_projection: float32 [768, 128], replicated
Inputs may be any that keep to these rules, and one draw needn't show every extreme that they name: `negatives`: queries and passages lie in blocks of 2 queries and 8 passages per device of dp+rep, device number dp index * (size of rep) + rep index. Every listed passage belongs to a device with the same rep index as the query's and another dp index. Of the 256 pairs of one device, every other dp index owns the passages of at most 5 pairs, and some dp index owns exactly 5.
All inputs are finite; a program needn't handle non-finite values.
Results may differ from a plain program's by a relative error of at most 0.015.
Values may be sent and summed in bfloat16 or wider, within the bound.
No kernel may reach another device: no remote copies, remote signals or barrier semaphores. Data moves between devices by JAX's collectives and lax.ppermute only.
A program may use at most 64 MiB of HBM per device.

v0:
```python
import math

import jax
import jax.numpy as jnp
from jax import lax
from jax.sharding import PartitionSpec as P

slot_block = 64


def unit_rows(raw):
    length = jnp.sqrt(jnp.sum(raw * raw, axis=-1, keepdims=True) + 1e-06)
    return (raw / length, length)


def unit_back(grad, unit, length):
    return (grad - unit * jnp.sum(unit * grad, axis=-1, keepdims=True)) / length


def pair_weights(scores, teacher):
    student = jnp.exp(scores)
    student = student / jnp.sum(student, axis=-1, keepdims=True)
    target = jnp.exp(teacher)
    target = target / jnp.sum(target, axis=-1, keepdims=True)
    return (scores.shape[-1] * (student - target)).astype(jnp.bfloat16)


def padded_blocks(within, picks):
    slot_total = within.shape[0]
    block_count = (slot_total + slot_block - 1) // slot_block
    extra = block_count * slot_block - slot_total
    within_pad = within.reshape(block_count, slot_block)
    picks_pad = picks.reshape(block_count, slot_block, picks.shape[1])
    return (within_pad, picks_pad, extra)


def select_tokens(passage_emb, pass_count, pass_len, within, picks):
    emb_dim = passage_emb.shape[1]
    slot_total = within.shape[0]
    whole_rows = passage_emb.reshape(pass_count, pass_len * emb_dim)
    within_pad, picks_pad, extra = padded_blocks(within, picks)

    def pick_block(block):
        block_within, block_picks = block
        which = (block_within[:, None] == jnp.arange(pass_count, dtype=jnp.int32)[None, :]).astype(
            jnp.bfloat16
        )
        chosen = jnp.dot(which, whole_rows, preferred_element_type=jnp.float32).astype(jnp.bfloat16)
        chosen = chosen.reshape(slot_block, pass_len, emb_dim)
        where = (
            block_picks[:, :, None] == jnp.arange(pass_len, dtype=jnp.int32)[None, None, :]
        ).astype(jnp.bfloat16)
        return jnp.einsum("bip,bpe->bie", where, chosen, preferred_element_type=jnp.float32).astype(
            jnp.bfloat16
        )

    picked = lax.map(pick_block, (within_pad, picks_pad))
    return picked.reshape(-1, picks.shape[1], emb_dim)


def spread_grads(grads, pass_count, pass_len, within, picks):
    emb_dim = grads.shape[2]
    query_len = grads.shape[1]
    within_pad, picks_pad, extra = padded_blocks(within, picks)
    grads_pad = grads.reshape(-1, slot_block, query_len, emb_dim)

    def add_block(total, block):
        block_within, block_picks, block_grads = block
        where = (
            block_picks[:, :, None] == jnp.arange(pass_len, dtype=jnp.int32)[None, None, :]
        ).astype(jnp.bfloat16)
        placed = jnp.einsum("bip,bie->bpe", where, block_grads, preferred_element_type=jnp.float32)
        which = (block_within[:, None] == jnp.arange(pass_count, dtype=jnp.int32)[None, :]).astype(
            jnp.float32
        )
        total = total + jnp.dot(
            which.T, placed.reshape(slot_block, pass_len * emb_dim), precision=lax.Precision.HIGHEST
        )
        return (total, None)

    start = jnp.zeros((pass_count, pass_len * emb_dim), jnp.float32)
    total, _ = lax.scan(add_block, start, (within_pad, picks_pad, grads_pad))
    return total.reshape(pass_count * pass_len, emb_dim)


def per_device(query_hidden, passage_hidden, projection, negatives, positions, teacher):
    query_count, query_len, hidden_dim = query_hidden.shape
    pass_count, pass_len, _ = passage_hidden.shape
    emb_dim = projection.shape[1]
    neg_count = negatives.shape[1]
    owners = lax.axis_size("dp")
    rep_count = lax.axis_size("rep")
    pair_count = query_count * neg_count
    capacity = (pair_count + owners - 2) // (owners - 1)
    slot_total = owners * capacity
    query_flat = query_hidden.reshape(-1, hidden_dim)
    passage_flat = passage_hidden.reshape(-1, hidden_dim)
    query_unit, query_length = unit_rows(
        jnp.dot(query_flat, projection, preferred_element_type=jnp.float32)
    )
    query_emb = query_unit.astype(jnp.bfloat16).reshape(query_count, query_len, emb_dim)
    passage_unit, passage_length = unit_rows(
        jnp.dot(passage_flat, projection, preferred_element_type=jnp.float32)
    )
    passage_emb = passage_unit.astype(jnp.bfloat16)
    flat_ids = negatives.reshape(-1)
    owner_of = flat_ids // (rep_count * pass_count)
    within = flat_ids % pass_count
    owner_table = (owner_of[:, None] == jnp.arange(owners, dtype=jnp.int32)[None, :]).astype(
        jnp.int32
    )
    slot_rank = jnp.sum((jnp.cumsum(owner_table, axis=0) - owner_table) * owner_table, axis=1)
    slot_index = owner_of * capacity + slot_rank
    query_slot = jnp.arange(pair_count, dtype=jnp.int32) // neg_count
    slot_match = slot_index[:, None] == jnp.arange(slot_total, dtype=jnp.int32)[None, :]
    slot_exact = slot_match.astype(jnp.float32)
    slot_table = slot_match.astype(jnp.bfloat16)
    request_fields = jnp.concatenate(
        [within[:, None], query_slot[:, None], positions.reshape(pair_count, query_len)], axis=1
    ).astype(jnp.float32)
    placed_fields = jnp.dot(slot_exact.T, request_fields, precision=lax.Precision.HIGHEST).astype(
        jnp.int32
    )
    request_meta = placed_fields[:, 0:2]
    request_pos = placed_fields[:, 2:]
    arrived_meta, arrived_pos = (
        lax.all_to_all(
            request_meta.reshape(owners, capacity, 2), "dp", split_axis=0, concat_axis=0, tiled=True
        ),
        lax.all_to_all(
            request_pos.reshape(owners, capacity, query_len),
            "dp",
            split_axis=0,
            concat_axis=0,
            tiled=True,
        ),
    )
    arrived_within = arrived_meta[:, :, 0].reshape(-1)
    arrived_picks = arrived_pos.reshape(slot_total, query_len)
    picked = select_tokens(passage_emb, pass_count, pass_len, arrived_within, arrived_picks)
    returned = lax.all_to_all(
        picked.reshape(owners, capacity, query_len, emb_dim),
        "dp",
        split_axis=0,
        concat_axis=0,
        tiled=True,
    )
    tokens = jnp.dot(
        slot_table,
        returned.reshape(slot_total, query_len * emb_dim),
        preferred_element_type=jnp.float32,
    ).astype(jnp.bfloat16)
    tokens = tokens.reshape(query_count, neg_count, query_len, emb_dim)
    scores = jnp.einsum("qnie,qie->qn", tokens, query_emb, preferred_element_type=jnp.float32)
    weights = pair_weights(scores, teacher)
    query_grad = jnp.einsum("qn,qnie->qie", weights, tokens, preferred_element_type=jnp.float32)
    token_grad = (
        weights.astype(jnp.float32)[:, :, None, None] * query_emb.astype(jnp.float32)[:, None]
    ).astype(jnp.bfloat16)
    outgoing = jnp.dot(
        slot_table.T,
        token_grad.reshape(pair_count, query_len * emb_dim),
        preferred_element_type=jnp.float32,
    ).astype(jnp.bfloat16)
    arrived_grad = lax.all_to_all(
        outgoing.reshape(owners, capacity, query_len, emb_dim),
        "dp",
        split_axis=0,
        concat_axis=0,
        tiled=True,
    )
    passage_grad = spread_grads(
        arrived_grad.reshape(slot_total, query_len, emb_dim),
        pass_count,
        pass_len,
        arrived_within,
        arrived_picks,
    )
    query_raw_grad = unit_back(query_grad.reshape(-1, emb_dim), query_unit, query_length).astype(
        jnp.bfloat16
    )
    passage_raw_grad = unit_back(passage_grad, passage_unit, passage_length).astype(jnp.bfloat16)
    local_sum = jnp.dot(query_flat.T, query_raw_grad, preferred_element_type=jnp.float32)
    local_sum = local_sum + jnp.dot(
        passage_flat.T, passage_raw_grad, preferred_element_type=jnp.float32
    )
    total = lax.psum(local_sum, ("dp", "rep"))
    scale = 1.0 / math.sqrt(owners * rep_count * (query_count * query_len + pass_count * pass_len))
    return (passage_raw_grad.reshape(pass_count, pass_len, emb_dim), total * scale)


def solution(mesh):
    in_specs = (
        P(("dp", "rep"), None, None),
        P(("dp", "rep"), None, None),
        P(),
        P(("dp", "rep"), None),
        P(("dp", "rep"), None, None),
        P(("dp", "rep"), None),
    )
    out_specs = (P(("dp", "rep"), None, None), P())
    return jax.shard_map(
        per_device, mesh=mesh, in_specs=in_specs, out_specs=out_specs, check_vma=False
    )
```

profile of v0, /device:TPU:1, one launch (start us, length us, event | category | flops | bytes accessed | tf_op | source)
XLA Modules:
  0.0 539.5 jit_solution(11385705560953658447)
XLA Ops:
  12.8 13.0 %all-to-all-start = ((s32[64,5,2]{1,2,0:T(2,128)}), s32[64,5,2]{1,2,0:T(2,128)S(1)}, u32[]{:S(2)}, u32[]{:S(2)}) async-start(s32[64,5,2]{1,2,0:T(2,128)} %copy.21), calls=%async_computation | async-start | bytes 131072 | tf_op jit(solution)/shard_map/all_to_all | solution.py:127
  25.8 3.4 copy.23
  36.5 10.3 %all-to-all-start.1 = ((s32[64,1,160]{2,1,0:T(1,128)}), s32[64,1,160]{2,1,0:T(1,128)S(1)}, u32[]{:S(2)}, u32[]{:S(2)}) async-start(s32[64,1,160]{2,1,0:T(1,128)} %reshape.262), calls=%async_computation.1 | async-start | bytes 131072 | tf_op jit(solution)/shard_map/all_to_all | solution.py:130
  47.1 9.6 %all-to-all-done.1 = s32[64,1,160]{2,1,0:T(1,128)S(1)} async-done(((s32[64,1,160]{2,1,0:T(1,128)}), s32[64,1,160]{2,1,0:T(1,128)S(1)}, u32[]{:S(2)}, u32[]{:S(2)}) %all-to-all-start.1) | async-done | bytes 40992 | tf_op jit(solution)/shard_map/all_to_all | solution.py:130
  58.1 43.6 %while.21 = (s32[]{:T(128)}, bf16[5,64,32,128]{3,2,1,0:T(8,128)(2,1)}, s32[5,64,32]{2,1,0:T(8,128)S(1)}, s32[5,64]{1,0:T(8,128)S(1)}, bf16[8,23040]{1,0:T(8,128)(2,1)}, /*index=5*/s32[]{:T(128)}) while((s32[]{:T(128)}, bf16[5,64,32,128]{3,2,1,0:T(8,128)(2,1)}, s32[5,64,32]{2,1,0:T(8,128)S(1)}, s32[5,64]{1,0:T(8,128)S(1)}, ...), condition=%wide.region_5.6_spmd, body=%wide.region_4.5_spmd.sunk | while | flops 120070656 | bytes 12714841 | solution.py:57
  58.1 3.5 convolution_convert_fusion.5
  61.7 3.4 reshape.265
  66.8 3.5 convolution_convert_fusion.5
  70.4 3.4 reshape.265
  75.6 3.5 convolution_convert_fusion.5
  79.1 3.4 reshape.265
  84.3 3.5 convolution_convert_fusion.5
  87.8 3.4 reshape.265
  93.0 3.5 convolution_convert_fusion.5
  96.6 3.4 reshape.265
  102.4 4.5 all-to-all-start.2
  108.1 61.2 %all-to-all-done.2 = bf16[64,5,32,128]{3,2,1,0:T(8,128)(2,1)S(1)} async-done(((bf16[64,5,32,128]{3,2,1,0:T(8,128)(2,1)}), bf16[64,5,32,128]{3,2,1,0:T(8,128)(2,1)S(1)}, u32[]{:S(2)}, u32[]{:S(2)}) %all-to-all-start.2) | async-done | bytes 2621472 | tf_op jit(solution)/shard_map/all_to_all | solution.py:141
  173.5 2.9 fusion.25
  178.4 5.9 %all-to-all-start.3 = ((bf16[64,5,32,128]{3,2,1,0:T(8,128)(2,1)}), bf16[64,5,32,128]{3,2,1,0:T(8,128)(2,1)S(1)}, u32[]{:S(2)}, u32[]{:S(2)}) async-start(bf16[64,5,32,128]{3,2,1,0:T(8,128)(2,1)} %bitcast.44), calls=%async_computation.3 | async-start | bytes 5242880 | tf_op jit(solution)/shard_map/all_to_all | solution.py:165
  189.1 57.6 %all-to-all-done.3 = bf16[64,5,32,128]{3,2,1,0:T(8,128)(2,1)S(1)} async-done(((bf16[64,5,32,128]{3,2,1,0:T(8,128)(2,1)}), bf16[64,5,32,128]{3,2,1,0:T(8,128)(2,1)S(1)}, u32[]{:S(2)}, u32[]{:S(2)}) %all-to-all-start.3) | async-done | bytes 2621472 | tf_op jit(solution)/shard_map/all_to_all | solution.py:165
  246.6 32.9 %while.22 = (s32[]{:T(128)}, f32[8,23040]{1,0:T(8,128)S(1)}, s32[5,64]{1,0:T(8,128)}, s32[5,64,32]{2,1,0:T(8,128)}, bf16[5,64,32,128]{3,2,1,0:T(8,128)(2,1)S(1)}, /*index=5*/s32[]{:T(128)}, s32[]{:T(128)}) while((s32[]{:T(128)}, f32[8,23040]{1,0:T(8,128)S(1)}, s32[5,64]{1,0:T(8,128)}, s32[5,64,32]{2,1,0:T(8,128)}, ...), condition=%wide.region_10.11_spmd.clone, body=%wide.region_9.10_spmd.clone.sunk | while | flops 236667392 | bytes 13845355 | solution.py:82
  254.6 2.6 fusion.76
  274.4 2.6 fusion.76
  286.7 244.0 %all-reduce.2.cloned.1.call-done = f32[768,128]{0,1:T(8,128)} async-done(((f32[768,128]{0,1:T(8,128)}), f32[768,128]{0,1:T(8,128)}) %all-reduce.2.cloned.1.call-update) | async-done | bytes 393232 | tf_op jit(solution)/shard_map/psum | solution.py:187
  (128 shorter events, 72.5 us)
Async XLA Ops:
  7.2 24.7 %copy-start = (bf16[768,128]{1,0:T(8,128)(2,1)S(1)}, bf16[768,128]{1,0:T(8,128)(2,1)}, u32[]{:S(2)}) copy-start(bf16[768,128]{1,0:T(8,128)(2,1)} %param.12) | copy-start | bytes 589828
  12.8 23.7 %all-to-all-start = ((s32[64,5,2]{1,2,0:T(2,128)}), s32[64,5,2]{1,2,0:T(2,128)S(1)}, u32[]{:S(2)}, u32[]{:S(2)}) async-start(s32[64,5,2]{1,2,0:T(2,128)} %copy.21), calls=%async_computation | async-start | bytes 131072 | tf_op jit(solution)/shard_map/all_to_all | solution.py:127
  31.9 1.4 copy-start.1
  33.2 0.9 copy-start.3
  33.3 1.1 copy-start.12
  36.5 20.1 %all-to-all-start.1 = ((s32[64,1,160]{2,1,0:T(1,128)}), s32[64,1,160]{2,1,0:T(1,128)S(1)}, u32[]{:S(2)}, u32[]{:S(2)}) async-start(s32[64,1,160]{2,1,0:T(1,128)} %reshape.262), calls=%async_computation.1 | async-start | bytes 131072 | tf_op jit(solution)/shard_map/all_to_all | solution.py:130
  101.7 0.7 copy-start.5
  101.7 0.7 copy-start.16
  101.7 5.2 copy-start.18
  101.7 5.3 copy-start.8
  102.4 66.9 %all-to-all-start.2 = ((bf16[64,5,32,128]{3,2,1,0:T(8,128)(2,1)}), bf16[64,5,32,128]{3,2,1,0:T(8,128)(2,1)S(1)}, u32[]{:S(2)}, u32[]{:S(2)}) async-start(bf16[64,5,32,128]{3,2,1,0:T(8,128)(2,1)} %bitcast.134), calls=%async_computation.2 | async-start | bytes 5242880 | tf_op jit(solution)/shard_map/all_to_all | solution.py:141
  107.3 0.6 copy-start.6
  107.4 63.8 %copy-start.14 = (f32[64]{0:T(128)}, f32[64]{0:T(128)S(1)}, u32[]{:S(2)}) copy-start(f32[64]{0:T(128)S(1)} %add_sqrt_fusion.1) | copy-start | bytes 772
  171.2 1.8 copy-start.4
  178.4 68.2 %all-to-all-start.3 = ((bf16[64,5,32,128]{3,2,1,0:T(8,128)(2,1)}), bf16[64,5,32,128]{3,2,1,0:T(8,128)(2,1)S(1)}, u32[]{:S(2)}, u32[]{:S(2)}) async-start(bf16[64,5,32,128]{3,2,1,0:T(8,128)(2,1)} %bitcast.44), calls=%async_computation.3 | async-start | bytes 5242880 | tf_op jit(solution)/shard_map/all_to_all | solution.py:165
  184.4 346.3 %all-reduce.2.cloned.1.call-start = ((), (), s32[]{:S(2)}) async-start(), calls=%async_computation.4 | async-start | bytes 786432 | tf_op jit(solution)/shard_map/psum | solution.py:187
  186.9 0.6 copy-start.10
  279.5 2.8 copy-start.13
  279.5 4.7 copy-start.2
  282.3 2.4 copy-start.7
  282.3 2.4 copy-start.9
  282.3 2.4 copy-start.11
  282.3 2.4 copy-start.15
  282.4 2.4 copy-start.17
Sparse Core Ops, SparseCore 0:
  286.0 244.6 all-reduce.1
where the time goes:
time: 541 us; the launch traced here: 539 us
  waiting for transfers between devices  372 us (69%)
  matrix products  62.6 us (12%)
  local copies, waits for them, and re-layouts  44 us (8%)
  starting transfers between devices  34 us (6%)
  between operations  14.5 us (3%)
  other arithmetic  11.8 us (2%)
    psum x1, waiting for transfers between devices, per_device(): total = lax.psum(local_sum, ('dp', 'rep'))  244 us
    all_to_all x1, waiting for transfers between devices, per_device(): lax.all_to_all(picked.reshape(owners, capacity, query_len, emb_dim), 'dp'...  61.2 us
    all_to_all x1, waiting for transfers between devices, per_device(): lax.all_to_all(outgoing.reshape(owners, capacity, query_len, emb_dim), 'd...  57.6 us
    dot_general x5, matrix products, pick_block(): jnp.dot(which, whole_rows, preferred_element_type=jnp.float32)  17.7 us
    reshape x5, local copies, waits for them, and re-layouts, pick_block(): chosen = chosen.reshape(slot_block, pass_len, emb_dim)  17 us
    all_to_all x1, starting transfers between devices, per_device(): lax.all_to_all(request_meta.reshape(owners, capacity, 2), 'dp', split_axi...  13 us
    dot_general x5, matrix products, add_block(): jnp.einsum('bip,bie->bpe', where, block_grads, preferred_element_type=jnp...  12.9 us
    dot_general x5, matrix products, add_block(): jnp.dot(which.T, placed.reshape(slot_block, pass_len * emb_dim), precisio...  12.6 us
  transfers between devices with their start and end apart: 5, of which 4 were waited for; matrix products, arithmetic and copies ran while one was open for 3% of the time, Pallas kernels for 0%

commit v1 on v0

--- a/solution.py
+++ b/solution.py
@@ -81,6 +81,21 @@
     start = jnp.zeros((pass_count, pass_len * emb_dim), jnp.float32)
     total, _ = lax.scan(add_block, start, (within_pad, picks_pad, grads_pad))
     return total.reshape(pass_count * pass_len, emb_dim)
+
+
+def reduce_all(term):
+    owners = lax.axis_size("dp")
+    reps = lax.axis_size("rep")
+    rows, cols = term.shape
+    pieces = term.astype(jnp.bfloat16).reshape(owners, rows // owners, cols)
+    pieces = lax.all_to_all(pieces, "dp", split_axis=0, concat_axis=0, tiled=True)
+    mine = jnp.sum(pieces.astype(jnp.float32), axis=0)
+    copies = jnp.broadcast_to(mine[None], (reps,) + mine.shape)
+    copies = lax.all_to_all(copies, "rep", split_axis=0, concat_axis=0, tiled=True)
+    mine = jnp.sum(copies, axis=0).astype(jnp.bfloat16)
+    copies = jnp.broadcast_to(mine[None], (owners,) + mine.shape)
+    copies = lax.all_to_all(copies, "dp", split_axis=0, concat_axis=0, tiled=True)
+    return copies.reshape(rows, cols).astype(jnp.float32)
 
 
 def per_device(query_hidden, passage_hidden, projection, negatives, positions, teacher):
@@ -184,7 +199,7 @@
     local_sum = local_sum + jnp.dot(
         passage_flat.T, passage_raw_grad, preferred_element_type=jnp.float32
     )
-    total = lax.psum(local_sum, ("dp", "rep"))
+    total = reduce_all(local_sum)
     scale = 1.0 / math.sqrt(owners * rep_count * (query_count * query_len + pass_count * pass_len))
     return (passage_raw_grad.reshape(pass_count, pass_len, emb_dim), total * scale)
 

time: 541 us -> 328 us (0.61)
  waiting for transfers between devices: 372 us -> 140 us
  blocking collectives: 0 us -> 25.9 us
  between operations: 14.5 us -> 1.11 us
  starting transfers between devices: 34 us -> 41.2 us
    psum x1 -> x0, waiting for transfers between devices: 244 us -> none  [per_device(): total = lax.psum(local_sum, ('dp', 'rep'))]
    all_to_all x0 -> x2, blocking collectives: none -> 25.9 us  [the longest x1 17.6 us: reduce_all(): lax.all_to_all(pieces, 'dp', split_axis=0, concat_axis=0, tiled=True)]
    all_to_all x0 -> x1, waiting for transfers between devices: none -> 11.1 us  [reduce_all(): lax.all_to_all(copies, 'dp', split_axis=0, concat_axis=0, tiled=True)]
    all_to_all x0 -> x1, starting transfers between devices: none -> 7.46 us  [reduce_all(): lax.all_to_all(copies, 'dp', split_axis=0, concat_axis=0, tiled=True)]
    unnamed x45 -> x44, local copies, waits for them, and re-layouts: 11.9 us -> 11 us
  transfers between devices with their start and end apart: 5 -> 5, of which waited for: 4 -> 4; matrix products, arithmetic and copies ran while one was open for 3% -> 4% of each run, Pallas kernels for 0% -> 0%
where the time goes in v1:
time: 328 us; the launch traced here: 326 us
  waiting for transfers between devices  140 us (43%)
  matrix products  61.9 us (19%)
  local copies, waits for them, and re-layouts  44.9 us (14%)
  starting transfers between devices  41.2 us (13%)
  blocking collectives  25.9 us (8%)
  other arithmetic  10.9 us (3%)
    all_to_all x1, waiting for transfers between devices, per_device(): lax.all_to_all(picked.reshape(owners, capacity, query_len, emb_dim), 'dp'...  61.2 us
    all_to_all x1, waiting for transfers between devices, per_device(): lax.all_to_all(outgoing.reshape(owners, capacity, query_len, emb_dim), 'd...  57.8 us
    dot_general x5, matrix products, pick_block(): jnp.dot(which, whole_rows, preferred_element_type=jnp.float32)  17.7 us
    all_to_all x1, blocking collectives, reduce_all(): lax.all_to_all(pieces, 'dp', split_axis=0, concat_axis=0, tiled=True)  17.6 us
    reshape x5, local copies, waits for them, and re-layouts, pick_block(): chosen = chosen.reshape(slot_block, pass_len, emb_dim)  17 us
    all_to_all x1, starting transfers between devices, per_device(): lax.all_to_all(request_meta.reshape(owners, capacity, 2), 'dp', split_axi...  13 us
    dot_general x5, matrix products, add_block(): jnp.einsum('bip,bie->bpe', where, block_grads, preferred_element_type=jnp...  12.9 us
    dot_general x5, matrix products, add_block(): jnp.dot(which.T, placed.reshape(slot_block, pass_len * emb_dim), precisio...  12.6 us
  transfers between devices with their start and end apart: 5, of which 4 were waited for; matrix products, arithmetic and copies ran while one was open for 4% of the time, Pallas kernels for 0%

profile of v1, /device:TPU:1, one launch (start us, length us, event | category | flops | bytes accessed | tf_op | source)
XLA Modules:
  0.0 325.8 jit_solution(14731990958096904919)
XLA Ops:
  6.3 13.0 %all-to-all-start = ((s32[64,5,2]{1,2,0:T(2,128)}), s32[64,5,2]{1,2,0:T(2,128)S(1)}, u32[]{:S(2)}, u32[]{:S(2)}) async-start(s32[64,5,2]{1,2,0:T(2,128)} %copy.34), calls=%async_computation | async-start | bytes 131072 | tf_op jit(solution)/shard_map/all_to_all | solution.py:142
  19.3 3.4 %copy.36 = bf16[8,180,768]{2,1,0:T(8,128)(2,1)} copy(bf16[8,180,768]{2,0,1:T(8,128)(2,1)} %param.11) | data formatting | bytes 4423680 | tf_op args[1]
  30.0 10.3 %all-to-all-start.1 = ((s32[64,1,160]{2,1,0:T(1,128)}), s32[64,1,160]{2,1,0:T(1,128)S(1)}, u32[]{:S(2)}, u32[]{:S(2)}) async-start(s32[64,1,160]{2,1,0:T(1,128)} %reshape.274), calls=%async_computation.1 | async-start | bytes 131072 | tf_op jit(solution)/shard_map/all_to_all | solution.py:145
  40.5 9.6 %all-to-all-done.1 = s32[64,1,160]{2,1,0:T(1,128)S(1)} async-done(((s32[64,1,160]{2,1,0:T(1,128)}), s32[64,1,160]{2,1,0:T(1,128)S(1)}, u32[]{:S(2)}, u32[]{:S(2)}) %all-to-all-start.1) | async-done | bytes 40992 | tf_op jit(solution)/shard_map/all_to_all | solution.py:145
  51.5 43.6 %while.21 = (s32[]{:T(128)}, bf16[5,64,32,128]{3,2,1,0:T(8,128)(2,1)}, s32[5,64,32]{2,1,0:T(8,128)S(1)}, s32[5,64]{1,0:T(8,128)S(1)}, bf16[8,23040]{1,0:T(8,128)(2,1)}, /*index=5*/s32[]{:T(128)}) while((s32[]{:T(128)}, bf16[5,64,32,128]{3,2,1,0:T(8,128)(2,1)}, s32[5,64,32]{2,1,0:T(8,128)S(1)}, s32[5,64]{1,0:T(8,128)S(1)}, ...), condition=%wide.region_5.6_spmd, body=%wide.region_4.5_spmd.sunk | while | flops 120070656 | bytes 12714841 | solution.py:57
  51.6 3.5 %convolution_convert_fusion.5 = bf16[64,23040]{1,0:T(8,128)(2,1)} fusion(bf16[8,23040]{1,0:T(8,128)(2,1)} %get-tuple-element.192, s32[64]{0:T(128)S(1)} %fusion.73), kind=kOutput, calls=%fused_computation.clone.1 | convolution fusion | flops 25068032 | bytes 3318016 | tf_op jit(solution)/shard_map/while/body/eval_jaxpr/dot_general | solution.py:48
  55.1 3.4 %reshape.277 = bf16[64,180,128]{2,1,0:T(8,128)(2,1)S(1)} reshape(bf16[64,23040]{1,0:T(8,128)(2,1)} %convolution_convert_fusion.5) | data formatting | bytes 5898240 | tf_op jit(solution)/shard_map/while/body/eval_jaxpr/reshape | solution.py:49
  60.3 3.5 %convolution_convert_fusion.5 = bf16[64,23040]{1,0:T(8,128)(2,1)} fusion(bf16[8,23040]{1,0:T(8,128)(2,1)} %get-tuple-element.192, s32[64]{0:T(128)S(1)} %fusion.73), kind=kOutput, calls=%fused_computation.clone.1 | convolution fusion | flops 25068032 | bytes 3318016 | tf_op jit(solution)/shard_map/while/body/eval_jaxpr/dot_general | solution.py:48
  63.9 3.4 %reshape.277 = bf16[64,180,128]{2,1,0:T(8,128)(2,1)S(1)} reshape(bf16[64,23040]{1,0:T(8,128)(2,1)} %convolution_convert_fusion.5) | data formatting | bytes 5898240 | tf_op jit(solution)/shard_map/while/body/eval_jaxpr/reshape | solution.py:49
  69.0 3.5 %convolution_convert_fusion.5 = bf16[64,23040]{1,0:T(8,128)(2,1)} fusion(bf16[8,23040]{1,0:T(8,128)(2,1)} %get-tuple-element.192, s32[64]{0:T(128)S(1)} %fusion.73), kind=kOutput, calls=%fused_computation.clone.1 | convolution fusion | flops 25068032 | bytes 3318016 | tf_op jit(solution)/shard_map/while/body/eval_jaxpr/dot_general | solution.py:48
  72.6 3.4 %reshape.277 = bf16[64,180,128]{2,1,0:T(8,128)(2,1)S(1)} reshape(bf16[64,23040]{1,0:T(8,128)(2,1)} %convolution_convert_fusion.5) | data formatting | bytes 5898240 | tf_op jit(solution)/shard_map/while/body/eval_jaxpr/reshape | solution.py:49
  77.7 3.5 %convolution_convert_fusion.5 = bf16[64,23040]{1,0:T(8,128)(2,1)} fusion(bf16[8,23040]{1,0:T(8,128)(2,1)} %get-tuple-element.192, s32[64]{0:T(128)S(1)} %fusion.73), kind=kOutput, calls=%fused_computation.clone.1 | convolution fusion | flops 25068032 | bytes 3318016 | tf_op jit(solution)/shard_map/while/body/eval_jaxpr/dot_general | solution.py:48
  81.3 3.4 %reshape.277 = bf16[64,180,128]{2,1,0:T(8,128)(2,1)S(1)} reshape(bf16[64,23040]{1,0:T(8,128)(2,1)} %convolution_convert_fusion.5) | data formatting | bytes 5898240 | tf_op jit(solution)/shard_map/while/body/eval_jaxpr/reshape | solution.py:49
  86.5 3.5 %convolution_convert_fusion.5 = bf16[64,23040]{1,0:T(8,128)(2,1)} fusion(bf16[8,23040]{1,0:T(8,128)(2,1)} %get-tuple-element.192, s32[64]{0:T(128)S(1)} %fusion.73), kind=kOutput, calls=%fused_computation.clone.1 | convolution fusion | flops 25068032 | bytes 3318016 | tf_op jit(solution)/shard_map/while/body/eval_jaxpr/dot_general | solution.py:48
  90.0 3.4 %reshape.277 = bf16[64,180,128]{2,1,0:T(8,128)(2,1)S(1)} reshape(bf16[64,23040]{1,0:T(8,128)(2,1)} %convolution_convert_fusion.5) | data formatting | bytes 5898240 | tf_op jit(solution)/shard_map/while/body/eval_jaxpr/reshape | solution.py:49
  95.9 4.5 %all-to-all-start.2 = ((bf16[64,5,32,128]{3,2,1,0:T(8,128)(2,1)}), bf16[64,5,32,128]{3,2,1,0:T(8,128)(2,1)S(1)}, u32[]{:S(2)}, u32[]{:S(2)}) async-start(bf16[64,5,32,128]{3,2,1,0:T(8,128)(2,1)} %bitcast.134), calls=%async_computation.2 | async-start | bytes 5242880 | tf_op jit(solution)/shard_map/all_to_all | solution.py:156
  101.5 61.2 %all-to-all-done.2 = bf16[64,5,32,128]{3,2,1,0:T(8,128)(2,1)S(1)} async-done(((bf16[64,5,32,128]{3,2,1,0:T(8,128)(2,1)}), bf16[64,5,32,128]{3,2,1,0:T(8,128)(2,1)S(1)}, u32[]{:S(2)}, u32[]{:S(2)}) %all-to-all-start.2) | async-done | bytes 2621472 | tf_op jit(solution)/shard_map/all_to_all | solution.py:156
  171.9 5.9 %all-to-all-start.3 = ((bf16[64,5,32,128]{3,2,1,0:T(8,128)(2,1)}), bf16[64,5,32,128]{3,2,1,0:T(8,128)(2,1)S(1)}, u32[]{:S(2)}, u32[]{:S(2)}) async-start(bf16[64,5,32,128]{3,2,1,0:T(8,128)(2,1)} %bitcast.44), calls=%async_computation.3 | async-start | bytes 5242880 | tf_op jit(solution)/shard_map/all_to_all | solution.py:180
  182.3 57.8 %all-to-all-done.3 = bf16[64,5,32,128]{3,2,1,0:T(8,128)(2,1)S(1)} async-done(((bf16[64,5,32,128]{3,2,1,0:T(8,128)(2,1)}), bf16[64,5,32,128]{3,2,1,0:T(8,128)(2,1)S(1)}, u32[]{:S(2)}, u32[]{:S(2)}) %all-to-all-start.3) | async-done | bytes 2621472 | tf_op jit(solution)/shard_map/all_to_all | solution.py:180
  240.1 32.9 %while.22 = (s32[]{:T(128)}, f32[8,23040]{1,0:T(8,128)S(1)}, s32[5,64]{1,0:T(8,128)}, s32[5,64,32]{2,1,0:T(8,128)}, bf16[5,64,32,128]{3,2,1,0:T(8,128)(2,1)S(1)}, /*index=5*/s32[]{:T(128)}, s32[]{:T(128)}) while((s32[]{:T(128)}, f32[8,23040]{1,0:T(8,128)S(1)}, s32[5,64]{1,0:T(8,128)}, s32[5,64,32]{2,1,0:T(8,128)}, ...), condition=%wide.region_10.11_spmd.clone, body=%wide.region_9.10_spmd.clone.sunk | while | flops 236667392 | bytes 13845355 | solution.py:82
  278.8 17.6 %all_to_all.35 = bf16[64,12,128]{2,1,0:T(8,128)(2,1)S(1)} all-to-all(bf16[64,12,128]{2,1,0:T(8,128)(2,1)S(1)} %reshape.259), channel_id=1, replica_groups=mesh['dp'=64,'rep'=4] {'dp'}, dimensions={0} | all-to-all | bytes 393216 | tf_op jit(solution)/shard_map/all_to_all | solution.py:91
  296.5 8.3 %all_to_all.36 = f32[4,12,128]{2,1,0:T(8,128)S(1)} all-to-all(f32[4,12,128]{2,1,0:T(8,128)S(1)} %broadcast_in_dim.13), channel_id=1, replica_groups=mesh['dp'=64,'rep'=4] {'rep'}, dimensions={0} | all-to-all | bytes 49152 | tf_op jit(solution)/shard_map/all_to_all | solution.py:94
  305.5 7.5 %all-to-all-start.6 = ((bf16[64,12,128]{2,1,0:T(8,128)(2,1)}), bf16[64,12,128]{2,1,0:T(8,128)(2,1)S(1)}, u32[]{:S(2)}, u32[]{:S(2)}) async-start(bf16[64,12,128]{2,1,0:T(8,128)(2,1)} %broadcast_in_dim.14), calls=%async_computation.6 | async-start | bytes 524288 | tf_op jit(solution)/shard_map/all_to_all | solution.py:97
  313.9 11.1 %all-to-all-done.6 = bf16[64,12,128]{2,1,0:T(8,128)(2,1)S(1)} async-done(((bf16[64,12,128]{2,1,0:T(8,128)(2,1)}), bf16[64,12,128]{2,1,0:T(8,128)(2,1)S(1)}, u32[]{:S(2)}, u32[]{:S(2)}) %all-to-all-start.6) | async-done | bytes 196640 | tf_op jit(solution)/shard_map/all_to_all | solution.py:97
  (135 shorter events, 79.5 us)
Async XLA Ops:
  0.6 24.7 %copy-start = (bf16[768,128]{1,0:T(8,128)(2,1)S(1)}, bf16[768,128]{1,0:T(8,128)(2,1)}, u32[]{:S(2)}) copy-start(bf16[768,128]{1,0:T(8,128)(2,1)} %param.12) | copy-start | bytes 589828
  6.3 23.7 %all-to-all-start = ((s32[64,5,2]{1,2,0:T(2,128)}), s32[64,5,2]{1,2,0:T(2,128)S(1)}, u32[]{:S(2)}, u32[]{:S(2)}) async-start(s32[64,5,2]{1,2,0:T(2,128)} %copy.34), calls=%async_computation | async-start | bytes 131072 | tf_op jit(solution)/shard_map/all_to_all | solution.py:142
  25.3 1.4 copy-start.1
  26.7 0.9 copy-start.3
  26.7 1.1 copy-start.12
  30.0 20.1 %all-to-all-start.1 = ((s32[64,1,160]{2,1,0:T(1,128)}), s32[64,1,160]{2,1,0:T(1,128)S(1)}, u32[]{:S(2)}, u32[]{:S(2)}) async-start(s32[64,1,160]{2,1,0:T(1,128)} %reshape.274), calls=%async_computation.1 | async-start | bytes 131072 | tf_op jit(solution)/shard_map/all_to_all | solution.py:145
  95.2 0.7 copy-start.5
  95.2 0.7 copy-start.16
  95.2 5.2 %copy-start.18 = (f32[2,128]{1,0:T(2,128)S(1)}, f32[2,128]{1,0:T(2,128)}, u32[]{:S(2)}) copy-start(f32[2,128]{1,0:T(2,128)} %param.15) | copy-start | bytes 3076
  95.2 5.3 %copy-start.8 = (bf16[2,32,768]{2,1,0:T(8,128)(2,1)S(1)}, bf16[2,32,768]{2,1,0:T(8,128)(2,1)}, u32[]{:S(2)}) copy-start(bf16[2,32,768]{2,1,0:T(8,128)(2,1)} %param.10) | copy-start | bytes 294916
  95.9 66.9 %all-to-all-start.2 = ((bf16[64,5,32,128]{3,2,1,0:T(8,128)(2,1)}), bf16[64,5,32,128]{3,2,1,0:T(8,128)(2,1)S(1)}, u32[]{:S(2)}, u32[]{:S(2)}) async-start(bf16[64,5,32,128]{3,2,1,0:T(8,128)(2,1)} %bitcast.134), calls=%async_computation.2 | async-start | bytes 5242880 | tf_op jit(solution)/shard_map/all_to_all | solution.py:156
  100.8 0.6 copy-start.6
  100.8 63.8 %copy-start.14 = (f32[64]{0:T(128)}, f32[64]{0:T(128)S(1)}, u32[]{:S(2)}) copy-start(f32[64]{0:T(128)S(1)} %add_sqrt_fusion.1) | copy-start | bytes 772
  164.6 1.8 copy-start.4
  171.9 68.2 %all-to-all-start.3 = ((bf16[64,5,32,128]{3,2,1,0:T(8,128)(2,1)}), bf16[64,5,32,128]{3,2,1,0:T(8,128)(2,1)S(1)}, u32[]{:S(2)}, u32[]{:S(2)}) async-start(bf16[64,5,32,128]{3,2,1,0:T(8,128)(2,1)} %bitcast.44), calls=%async_computation.3 | async-start | bytes 5242880 | tf_op jit(solution)/shard_map/all_to_all | solution.py:180
  180.1 0.6 copy-start.10
  273.0 2.8 copy-start.13
  273.0 4.7 %copy-start.2 = (bf16[1440,768]{1,0:T(8,128)(2,1)S(1)}, bf16[1440,768]{1,0:T(8,128)(2,1)}, u32[]{:S(2)}) copy-start(bf16[1440,768]{1,0:T(8,128)(2,1)} %copy-done.1) | copy-start | bytes 6635524
  275.8 2.4 copy-start.7
  275.8 2.4 copy-start.9
  275.8 2.4 copy-start.11
  275.8 2.4 copy-start.15
  275.8 2.4 copy-start.17
  305.5 19.5 %all-to-all-start.6 = ((bf16[64,12,128]{2,1,0:T(8,128)(2,1)}), bf16[64,12,128]{2,1,0:T(8,128)(2,1)S(1)}, u32[]{:S(2)}, u32[]{:S(2)}) async-start(bf16[64,12,128]{2,1,0:T(8,128)(2,1)} %broadcast_in_dim.14), calls=%async_computation.6 | async-start | bytes 524288 | tf_op jit(solution)/shard_map/all_to_all | solution.py:97

commit v2 on v0

v2 whole, which is shorter than its diff:
```python
import math

import jax
import jax.numpy as jnp
from jax import lax
from jax.experimental import pallas as pl
from jax.experimental.pallas import tpu as pltpu
from jax.sharding import PartitionSpec as P

F32 = jnp.float32
BF16 = jnp.bfloat16
SLOTS = 8
META_ROWS = 16
CODE, WHICH, VALID, HIGH, MID, LOW = 32, 33, 34, 35, 36, 37
WIDE = 256
GROUP = 16
PIECE = 16
VMEM = pl.BlockSpec(memory_space=pltpu.VMEM)
SMEM = pl.BlockSpec(memory_space=pltpu.SMEM)


def params():
    return pltpu.CompilerParams(vmem_limit_bytes=56 * 1024 * 1024)


def unit_rows(raw):
    length = jnp.sqrt(jnp.sum(raw * raw, axis=-1, keepdims=True) + 1e-06)
    return (raw / length, length)


def unit_back(grad, unit, length):
    return (grad - unit * jnp.sum(unit * grad, axis=-1, keepdims=True)) / length


def iota(shape, dim):
    return lax.broadcasted_iota(jnp.int32, shape, dim)


def request_kernel(reps, passes, query_ref, proj_ref, neg_ref, pos_ref, teacher_ref, send_ref, field_ref):
    owners, rows, _ = send_ref.shape
    queries, neg = neg_ref.shape
    query_len = pos_ref.shape[2]
    unit, _ = unit_rows(jnp.dot(query_ref[...], proj_ref[...], preferred_element_type=F32))
    emb = unit.astype(BF16)
    send_ref[:, : emb.shape[0], :] = jnp.broadcast_to(emb[None], (owners,) + emb.shape)
    target = jnp.exp(teacher_ref[...])
    target = target / jnp.sum(target, axis=-1, keepdims=True)
    high = target.astype(BF16).astype(F32)
    rest = target - high
    mid = rest.astype(BF16).astype(F32)
    low = (rest - mid).astype(BF16).astype(F32)
    ids = neg_ref[...]
    owner = lax.div(ids, jnp.int32(reps * passes))
    within = lax.rem(ids, jnp.int32(passes))
    before = (iota((neg, neg), 0) < iota((neg, neg), 1)).astype(F32).astype(BF16)
    total = jnp.zeros((owners, 1), F32)
    meta = jnp.zeros((owners * SLOTS, neg), F32)
    for q in range(queries):
        own = jnp.where(iota((owners, neg), 0) == owner[q : q + 1, :], 1.0, 0.0)
        rank = jnp.dot(own.astype(BF16), before, preferred_element_type=F32) + total
        total = total + jnp.sum(own, axis=1, keepdims=True)
        rank = jnp.sum(own * rank, axis=0, keepdims=True).astype(jnp.int32)
        slot = owner[q : q + 1, :] * SLOTS + rank
        table = jnp.where(iota((owners * SLOTS, neg), 0) == slot, 1.0, 0.0).astype(BF16)
        lines = {
            CODE: (within[q : q + 1, :] * queries + q).astype(F32),
            WHICH: jnp.full((1, neg), float(q), F32),
            VALID: jnp.ones((1, neg), F32),
            HIGH: high[q : q + 1, :],
            MID: mid[q : q + 1, :],
            LOW: low[q : q + 1, :],
        }
        line = iota((neg, neg), 0)
        fields = jnp.zeros((neg, neg), F32)
        for at, value in lines.items():
            fields = fields + jnp.where(line == at, value, 0.0)
        field_ref[...] = fields.T
        field_ref[:, :query_len] = pos_ref[q].astype(F32)
        meta = meta + jnp.dot(table, field_ref[...].astype(BF16), preferred_element_type=F32)
    meta = meta.reshape(owners, SLOTS, neg)
    meta = jnp.concatenate([meta, jnp.zeros((owners, META_ROWS - SLOTS, neg), F32)], axis=1)
    send_ref[:, emb.shape[0] :, :] = meta.astype(BF16)


def embed_kernel(hidden_ref, proj_ref, emb_ref, wide_ref):
    passes, pass_len, _ = hidden_ref.shape
    wide_ref[...] = jnp.zeros_like(wide_ref)
    for p in range(passes):
        unit, _ = unit_rows(jnp.dot(hidden_ref[p], proj_ref[...], preferred_element_type=F32))
        wide_ref[:pass_len, :] = unit
        emb_ref[p] = wide_ref[...].astype(BF16)


def picked_at(meta, group):
    own = meta[group * GROUP : (group + 1) * GROUP]
    return own.reshape(GROUP * SLOTS, own.shape[2]).T


def score_kernel(capacity, block, recv_ref, emb_ref, code_ref, exp_ref, part_ref, table_ref, acc_ref):
    owners = recv_ref.shape[0]
    passes = emb_ref.shape[0]
    queries, query_len = block
    rows = queries * query_len
    emb_dim = recv_ref.shape[2]
    meta = recv_ref[:, rows:, :].astype(F32)[:, :SLOTS, :]
    lane = iota((query_len, WIDE), 1).astype(F32)
    acc_ref[...] = jnp.zeros_like(acc_ref)
    for group in range(owners // GROUP):
        left = recv_ref[group * GROUP : (group + 1) * GROUP, :rows, :].reshape(GROUP * rows, emb_dim)
        for p in range(passes):
            table_ref[p] = lax.dot_general(
                left, emb_ref[p], (((1,), (1,)), ((), ())), preferred_element_type=F32
            )
        spots = picked_at(meta, group)[:query_len]
        for d in range(GROUP):
            for k in range(capacity):
                at = d * SLOTS + k
                code = code_ref[group * GROUP + d, k]
                p = lax.div(code, jnp.int32(queries))
                j = lax.rem(code, jnp.int32(queries))
                start = pl.multiple_of(d * rows + j * query_len, query_len)
                values = table_ref[p, pl.ds(start, query_len), :]
                chosen = jnp.where(spots[:, at : at + 1] == lane, values, 0.0)
                chosen = chosen[:, :emb_dim] + chosen[:, emb_dim:]
                acc_ref[group * GROUP + d, k : k + 1, :] = jnp.sum(chosen, axis=0, keepdims=True)
    scores = jnp.sum(acc_ref[...], axis=-1, keepdims=True)
    exps = jnp.exp(scores) * meta[:, :, VALID : VALID + 1]
    exp_ref[...] = jnp.broadcast_to(exps, exp_ref.shape)
    which = meta[:, :, WHICH : WHICH + 1]
    shape = (owners, 1, emb_dim)
    place = iota(shape, 2) - queries * iota(shape, 0)
    total = jnp.zeros(shape, F32)
    for q in range(queries):
        share = jnp.sum(jnp.where(which == float(q), exps, 0.0), axis=1, keepdims=True)
        total = total + jnp.where(place == q, share, 0.0)
    part_ref[...] = jnp.broadcast_to(jnp.sum(total, axis=0, keepdims=True), part_ref.shape)


def slot_weights(queries, neg, meta, exps, parts):
    owners = exps.shape[0]
    shape = (owners, 1, parts.shape[2])
    place = iota(shape, 2) - queries * iota(shape, 0)
    sums = jnp.sum(parts, axis=0, keepdims=True)
    which = meta[:, :, WHICH : WHICH + 1]
    share = jnp.zeros_like(exps)
    for q in range(queries):
        norm = jnp.sum(jnp.where(place == q, sums, 0.0), axis=-1, keepdims=True)
        share = share + jnp.where(which == float(q), exps / norm, 0.0)
    target = meta[:, :, HIGH : HIGH + 1] + meta[:, :, MID : MID + 1]
    target = target + meta[:, :, LOW : LOW + 1]
    return neg * (share - target) * meta[:, :, VALID : VALID + 1]


def fill_table(capacity, queries, query_len, group, spots, code_ref, weight_ref, table_ref):
    rows = queries * query_len
    lane = iota((query_len, WIDE), 1).astype(F32)
    table_ref[...] = jnp.zeros_like(table_ref)
    for d in range(GROUP):
        for k in range(capacity):
            at = d * SLOTS + k
            code = code_ref[group * GROUP + d, k]
            p = lax.div(code, jnp.int32(queries))
            j = lax.rem(code, jnp.int32(queries))
            start = pl.multiple_of(d * rows + j * query_len, query_len)
            weight = weight_ref[group * GROUP + d, k : k + 1, :]
            weight = jnp.concatenate([weight] * (WIDE // weight.shape[1]), axis=1)
            mask = spots[:, at : at + 1] == lane
            added = jnp.where(mask, weight, 0.0).astype(table_ref.dtype)
            table_ref[p, pl.ds(start, query_len), :] = (
                table_ref[p, pl.ds(start, query_len), :] + added
            )


def query_part_kernel(
    capacity, block, neg, recv_ref, emb_ref, code_ref, exp_ref, part_ref, out_ref, weight_ref, table_ref
):
    owners = recv_ref.shape[0]
    passes = emb_ref.shape[0]
    queries, query_len = block
    rows = queries * query_len
    meta = recv_ref[:, rows:, :].astype(F32)[:, :SLOTS, :]
    weight_ref[...] = slot_weights(queries, neg, meta, exp_ref[...], part_ref[...])
    for group in range(owners // GROUP):
        spots = picked_at(meta, group)[:query_len]
        fill_table(capacity, queries, query_len, group, spots, code_ref, weight_ref, table_ref)
        grad = jnp.zeros((GROUP * rows, emb_ref.shape[2]), F32)
        for p in range(passes):
            grad = grad + jnp.dot(table_ref[p], emb_ref[p], preferred_element_type=F32)
        grad = grad.astype(BF16).reshape(GROUP, rows, emb_ref.shape[2])
        out_ref[group * GROUP : (group + 1) * GROUP] = grad


def passage_kernel(
    capacity,
    block,
    neg,
    recv_ref,
    hidden_ref,
    proj_ref,
    code_ref,
    exp_ref,
    part_ref,
    grad_ref,
    term_ref,
    weight_ref,
    table_ref,
    total_ref,
):
    owners = recv_ref.shape[0]
    passes, pass_len, _ = hidden_ref.shape
    queries, query_len = block
    rows = queries * query_len
    emb_dim = recv_ref.shape[2]
    meta = recv_ref[:, rows:, :].astype(F32)[:, :SLOTS, :]
    weight_ref[...] = slot_weights(queries, neg, meta, exp_ref[...], part_ref[...])
    for group in range(owners // GROUP):
        spots = picked_at(meta, group)[:query_len]
        fill_table(capacity, queries, query_len, group, spots, code_ref, weight_ref, table_ref)
        left = recv_ref[group * GROUP : (group + 1) * GROUP, :rows, :].reshape(GROUP * rows, emb_dim)
        left = left.T
        for p in range(passes):
            grad = jnp.dot(left, table_ref[p], preferred_element_type=F32)
            if group == 0:
                total_ref[p] = grad
            else:
                total_ref[p] = total_ref[p] + grad
    term = jnp.zeros(term_ref.shape, F32)
    for p in range(passes):
        unit, length = unit_rows(jnp.dot(hidden_ref[p], proj_ref[...], preferred_element_type=F32))
        grad = total_ref[p].T[:pass_len]
        raw_grad = unit_back(grad, unit, length).astype(BF16)
        grad_ref[p] = raw_grad
        term = term + lax.dot_general(
            raw_grad, hidden_ref[p], (((0,), (0,)), ((), ())), preferred_element_type=F32
        )
    term_ref[...] = term


def query_kernel(parts_ref, query_ref, proj_ref, term_ref, out_ref):
    hidden = query_ref[...]
    unit, length = unit_rows(jnp.dot(hidden, proj_ref[...], preferred_element_type=F32))
    grad = jnp.sum(parts_ref[...].astype(F32), axis=0)
    raw_grad = unit_back(grad, unit, length).astype(BF16)
    term = term_ref[...] + lax.dot_general(
        raw_grad, hidden, (((0,), (0,)), ((), ())), preferred_element_type=F32
    )
    used = term.shape[1] // PIECE
    out_ref[:used] = term.T.astype(BF16).reshape(used, PIECE, term.shape[0])
    out_ref[used:] = jnp.zeros((out_ref.shape[0] - used,) + out_ref.shape[1:], BF16)


def swap(array, axis):
    return lax.all_to_all(array, axis, split_axis=0, concat_axis=0, tiled=True)


def per_device(query_hidden, passage_hidden, projection, negatives, positions, teacher):
    query_count, query_len, hidden_dim = query_hidden.shape
    pass_count, pass_len, _ = passage_hidden.shape
    emb_dim = projection.shape[1]
    neg_count = negatives.shape[1]
    owners = lax.axis_size("dp")
    reps = lax.axis_size("rep")
    pair_count = query_count * neg_count
    capacity = (pair_count + owners - 2) // (owners - 1)
    rows = query_count * query_len
    block = (query_count, query_len)
    query_flat = query_hidden.reshape(rows, hidden_dim)

    def call(kernel, outs, scratch, specs, *args):
        return pl.pallas_call(
            kernel,
            out_shape=outs,
            in_specs=specs,
            out_specs=jax.tree.map(lambda _: VMEM, outs),
            scratch_shapes=scratch,
            compiler_params=params(),
        )(*args)

    send = call(
        lambda *refs: request_kernel(reps, pass_count, *refs),
        jax.ShapeDtypeStruct((owners, rows + META_ROWS, emb_dim), BF16),
        [pltpu.VMEM((neg_count, neg_count), F32)],
        [VMEM] * 5,
        query_flat,
        projection,
        negatives,
        positions,
        teacher,
    )
    recv = swap(send, "dp")
    emb = call(
        embed_kernel,
        jax.ShapeDtypeStruct((pass_count, WIDE, emb_dim), BF16),
        [pltpu.VMEM((WIDE, emb_dim), F32)],
        [VMEM] * 2,
        passage_hidden,
        projection,
    )
    codes = recv[:, rows : rows + SLOTS, CODE].astype(jnp.int32)
    slot_shape = (owners, SLOTS, emb_dim)
    exps, parts = call(
        lambda *refs: score_kernel(capacity, block, *refs),
        (
            jax.ShapeDtypeStruct(slot_shape, F32),
            jax.ShapeDtypeStruct((owners, 1, emb_dim), F32),
        ),
        [pltpu.VMEM((pass_count, GROUP * rows, WIDE), F32), pltpu.VMEM(slot_shape, F32)],
        [VMEM, VMEM, SMEM],
        recv,
        emb,
        codes,
    )
    parts = swap(parts, "dp")
    table = pltpu.VMEM((pass_count, GROUP * rows, WIDE), BF16)
    query_parts = call(
        lambda *refs: query_part_kernel(capacity, block, neg_count, *refs),
        jax.ShapeDtypeStruct((owners, rows, emb_dim), BF16),
        [pltpu.VMEM(slot_shape, F32), table],
        [VMEM, VMEM, SMEM, VMEM, VMEM],
        recv,
        emb,
        codes,
        exps,
        parts,
    )
    query_parts = swap(query_parts, "dp")
    grad_passages, term = call(
        lambda *refs: passage_kernel(capacity, block, neg_count, *refs),
        (
            jax.ShapeDtypeStruct((pass_count, pass_len, emb_dim), BF16),
            jax.ShapeDtypeStruct((emb_dim, hidden_dim), F32),
        ),
        [pltpu.VMEM(slot_shape, F32), table, pltpu.VMEM((pass_count, emb_dim, WIDE), F32)],
        [VMEM, VMEM, VMEM, SMEM, VMEM, VMEM],
        recv,
        passage_hidden,
        projection,
        codes,
        exps,
        parts,
    )
    pieces = call(
        query_kernel,
        jax.ShapeDtypeStruct((owners, PIECE, emb_dim), BF16),
        [],
        [VMEM] * 4,
        query_parts,
        query_flat,
        projection,
        term,
    )
    pieces = swap(pieces, "dp")
    mine = jnp.sum(pieces.astype(F32), axis=0)
    copies = swap(jnp.broadcast_to(mine[None], (reps,) + mine.shape), "rep")
    scale = 1.0 / math.sqrt(owners * reps * (query_count * query_len + pass_count * pass_len))
    mine = (jnp.sum(copies, axis=0) * scale).astype(BF16)
    copies = swap(jnp.broadcast_to(mine[None], (owners,) + mine.shape), "dp")
    total = copies.reshape(owners * PIECE, emb_dim)[:hidden_dim].astype(F32)
    return (grad_passages, total)


def solution(mesh):
    in_specs = (
        P(("dp", "rep"), None, None),
        P(("dp", "rep"), None, None),
        P(),
        P(("dp", "rep"), None),
        P(("dp", "rep"), None, None),
        P(("dp", "rep"), None),
    )
    out_specs = (P(("dp", "rep"), None, None), P())
    return jax.shard_map(
        per_device, mesh=mesh, in_specs=in_specs, out_specs=out_specs, check_vma=False
    )
```

time: 541 us -> 175 us (0.32)
  waiting for transfers between devices: 372 us -> 54.9 us
  matrix products: 62.6 us -> 0 us
  Pallas kernels: 0 us -> 43 us
  blocking collectives: 0 us -> 41.9 us
  local copies, waits for them, and re-layouts: 44 us -> 6.38 us
  between operations: 14.5 us -> 0.71 us
  other arithmetic: 11.8 us -> 1.51 us
  starting transfers between devices: 34 us -> 25.4 us
    psum x1 -> x0, waiting for transfers between devices: 244 us -> none  [per_device(): total = lax.psum(local_sum, ('dp', 'rep'))]
    all_to_all x4 -> x3, waiting for transfers between devices: 128 us -> 54.9 us  [swap(): return lax.all_to_all(array, axis, split_axis=0, concat_axis=0, tiled=True)]
    dot_general x29 -> x0, matrix products: 62.6 us -> none  [the longest x5 17.7 us: pick_block(): jnp.dot(which, whole_rows, preferred_element_type=jnp.float32)]
    pallas_call x0 -> x6, Pallas kernels: none -> 43 us  [call(): pl.pallas_call(kernel, out_shape=outs, in_specs=specs, out_specs=jax.tree...]
    all_to_all x0 -> x3, blocking collectives: none -> 41.9 us  [swap(): return lax.all_to_all(array, axis, split_axis=0, concat_axis=0, tiled=True)]
    reshape x13 -> x0, local copies, waits for them, and re-layouts: 23.3 us -> none  [the longest x5 17 us: pick_block(): chosen = chosen.reshape(slot_block, pass_len, emb_dim)]
    all_to_all x4 -> x3, starting transfers between devices: 33.8 us -> 25.4 us  [swap(): return lax.all_to_all(array, axis, split_axis=0, concat_axis=0, tiled=True)]
    eq x20 -> x0, local copies, waits for them, and re-layouts: 7.29 us -> none  [the longest x5 3.8 us: add_block(): block_picks[:, :, None]]
  transfers between devices with their start and end apart: 5 -> 3, of which waited for: 4 -> 3; matrix products, arithmetic and copies ran while one was open for 3% -> 1% of each run, Pallas kernels for 0% -> 10%
where the time goes in v2:
time: 175 us; the launch traced here: 174 us
  waiting for transfers between devices  54.9 us (31%)
  Pallas kernels  43 us (25%)
  blocking collectives  41.9 us (24%)
  starting transfers between devices  25.4 us (15%)
  local copies, waits for them, and re-layouts  6.38 us (4%)
    all_to_all x3, waiting for transfers between devices, swap(): return lax.all_to_all(array, axis, split_axis=0, concat_axis=0, tiled=True)  54.9 us
    pallas_call x6, Pallas kernels, call(): pl.pallas_call(kernel, out_shape=outs, in_specs=specs, out_specs=jax.tree...  43 us
    all_to_all x3, blocking collectives, swap(): return lax.all_to_all(array, axis, split_axis=0, concat_axis=0, tiled=True)  41.9 us
    all_to_all x3, starting transfers between devices, swap(): return lax.all_to_all(array, axis, split_axis=0, concat_axis=0, tiled=True)  25.4 us
    unnamed x12, local copies, waits for them, and re-layouts  5.52 us
  transfers between devices with their start and end apart: 3, of which 3 were waited for; matrix products, arithmetic and copies ran while one was open for 1% of the time, Pallas kernels for 10%

profile of v2, /device:TPU:1, one launch (start us, length us, event | category | flops | bytes accessed | tf_op | source)
XLA Modules:
  0.0 173.8 jit_solution(17378780618303176342)
XLA Ops:
  0.6 1.5 copy.21.refs_3_
  2.1 2.8 %shard_map.77 = bf16[64,80,128]{2,1,0:T(8,128)(2,1)} custom-call(bf16[64,768]{1,0:T(8,128)(2,1)} %bitcast.7, bf16[768,128]{1,0:T(8,128)(2,1)} %proj_ref.3, s32[2,128]{1,0:T(2,128)} %refs_2_.2, s32[2,128,32]{2,1,0:T(8,128)} %copy.21.refs_3_, f32[2,128]{1,0:T(2,128)} %refs_4_.1), custom_call_target="tpu_custom_call" | custom-call | tf_op jit(solution)/shard_map/pallas_call | solution.py:270
  4.9 13.0 %all-to-all-start = ((bf16[64,80,128]{2,1,0:T(8,128)(2,1)}), bf16[64,80,128]{2,1,0:T(8,128)(2,1)S(1)}, u32[]{:S(2)}, u32[]{:S(2)}) async-start(bf16[64,80,128]{2,1,0:T(8,128)(2,1)} %shard_map.77), calls=%async_computation | async-start | bytes 2621440 | tf_op jit(solution)/shard_map/all_to_all | solution.py:253
  17.9 1.8 %copy.24.hidden_ref.refs_1_ = bf16[8,180,768]{2,1,0:T(8,128)(2,1)} copy(bf16[8,180,768]{2,0,1:T(8,128)(2,1)S(1)} %copy-done.2) | data formatting | bytes 4423680 | tf_op args[1]
  19.7 3.4 %shard_map.78.refs_1_ = bf16[8,256,128]{2,1,0:T(8,128)(2,1)} custom-call(bf16[8,180,768]{2,1,0:T(8,128)(2,1)} %copy.24.hidden_ref.refs_1_, bf16[768,128]{1,0:T(8,128)(2,1)} %proj_ref.3), custom_call_target="tpu_custom_call" | custom-call | tf_op jit(solution)/shard_map/pallas_call | solution.py:270
  23.1 28.9 %all-to-all-done.refs_0_ = bf16[64,80,128]{2,1,0:T(8,128)(2,1)S(1)} async-done(((bf16[64,80,128]{2,1,0:T(8,128)(2,1)}), bf16[64,80,128]{2,1,0:T(8,128)(2,1)S(1)}, u32[]{:S(2)}, u32[]{:S(2)}) %all-to-all-start) | async-done | bytes 1310752 | tf_op jit(solution)/shard_map/all_to_all | solution.py:253
  52.1 0.1 slice.9
  52.2 0.4 copy.26
  52.6 0.6 bitcast_convert_fusion.1.refs_2_.refs_3_
  53.3 9.1 %shard_map.79 = (f32[64,8,128]{2,1,0:T(8,128)}, f32[64,1,128]{2,1,0:T(1,128)}) custom-call(bf16[64,80,128]{2,1,0:T(8,128)(2,1)} %copy-done, bf16[8,256,128]{2,1,0:T(8,128)(2,1)} %shard_map.78.refs_1_, s32[64,8]{1,0:T(8,128)} %bitcast_convert_fusion.1.refs_2_.refs_3_), custom_call_target="tpu_custom_call" | custom-call | tf_op jit(solution)/shard_map/pallas_call | solution.py:270
  62.4 15.4 %all_to_all.30.refs_5_.refs_4_ = f32[64,1,128]{2,1,0:T(1,128)} all-to-all(f32[64,1,128]{2,1,0:T(1,128)} %get-tuple-element.7), channel_id=1, replica_groups=mesh['dp'=64,'rep'=4] {'dp'}, dimensions={0} | all-to-all | bytes 65536 | tf_op jit(solution)/shard_map/all_to_all | solution.py:253
  77.7 11.1 %shard_map.81 = bf16[64,64,128]{2,1,0:T(8,128)(2,1)} custom-call(bf16[64,80,128]{2,1,0:T(8,128)(2,1)} %copy-done, bf16[8,256,128]{2,1,0:T(8,128)(2,1)} %shard_map.78.refs_1_, s32[64,8]{1,0:T(8,128)} %bitcast_convert_fusion.1.refs_2_.refs_3_, f32[64,8,128]{2,1,0:T(8,128)} %get-tuple-element.6.refs_4_.refs_3_, f32[64,1,128]{2,1,0:T(1,128)} %all_to_all.30.refs_5_.refs_4_), custom_call_target="tpu_custom_call" | custom-call | tf_op jit(solution)/shard_map/pallas_call | solution.py:270
  88.8 4.9 %all-to-all-start.2 = ((bf16[64,64,128]{2,1,0:T(8,128)(2,1)}), bf16[64,64,128]{2,1,0:T(8,128)(2,1)S(1)}, u32[]{:S(2)}, u32[]{:S(2)}) async-start(bf16[64,64,128]{2,1,0:T(8,128)(2,1)} %shard_map.81), calls=%async_computation.2 | async-start | bytes 2097152 | tf_op jit(solution)/shard_map/all_to_all | solution.py:253
  93.8 13.8 %shard_map.80 = (bf16[8,180,128]{2,1,0:T(8,128)(2,1)}, f32[128,768]{1,0:T(8,128)}) custom-call(bf16[64,80,128]{2,1,0:T(8,128)(2,1)} %copy-done, bf16[8,180,768]{2,1,0:T(8,128)(2,1)} %copy.24.hidden_ref.refs_1_, bf16[768,128]{1,0:T(8,128)(2,1)} %proj_ref.3, s32[64,8]{1,0:T(8,128)} %bitcast_convert_fusion.1.refs_2_.refs_3_, ...), custom_call_target="tpu_custom_call" | custom-call | tf_op jit(solution)/shard_map/pallas_call | solution.py:270
  107.6 14.7 %all-to-all-done.2.parts_ref = bf16[64,64,128]{2,1,0:T(8,128)(2,1)S(1)} async-done(((bf16[64,64,128]{2,1,0:T(8,128)(2,1)}), bf16[64,64,128]{2,1,0:T(8,128)(2,1)S(1)}, u32[]{:S(2)}, u32[]{:S(2)}) %all-to-all-start.2) | async-done | bytes 1048608 | tf_op jit(solution)/shard_map/all_to_all | solution.py:253
  122.3 1.0 copy-done.1
  123.3 2.8 %shard_map.82 = bf16[64,16,128]{2,1,0:T(8,128)(2,1)} custom-call(bf16[64,64,128]{2,1,0:T(8,128)(2,1)} %copy-done.1, bf16[64,768]{1,0:T(8,128)(2,1)} %bitcast.8, bf16[768,128]{1,0:T(8,128)(2,1)} %proj_ref.3, f32[128,768]{1,0:T(8,128)} %get-tuple-element.9.term_ref), custom_call_target="tpu_custom_call" | custom-call | tf_op jit(solution)/shard_map/pallas_call | solution.py:270
  126.1 18.3 %all_to_all.31 = bf16[64,16,128]{2,1,0:T(8,128)(2,1)S(1)} all-to-all(bf16[64,16,128]{2,1,0:T(8,128)(2,1)} %shard_map.82), channel_id=1, replica_groups=mesh['dp'=64,'rep'=4] {'dp'}, dimensions={0} | all-to-all | bytes 524288 | tf_op jit(solution)/shard_map/all_to_all | solution.py:253
  144.5 8.3 %all_to_all.32 = f32[4,16,128]{2,1,0:T(8,128)S(1)} all-to-all(f32[4,16,128]{2,1,0:T(8,128)S(1)} %broadcast_in_dim.4), channel_id=1, replica_groups=mesh['dp'=64,'rep'=4] {'rep'}, dimensions={0} | all-to-all | bytes 65536 | tf_op jit(solution)/shard_map/all_to_all | solution.py:253
  152.8 0.7 broadcast_in_dim.5
  153.5 7.5 %all-to-all-start.5 = ((bf16[64,16,128]{2,1,0:T(8,128)(2,1)}), bf16[64,16,128]{2,1,0:T(8,128)(2,1)S(1)}, u32[]{:S(2)}, u32[]{:S(2)}) async-start(bf16[64,16,128]{2,1,0:T(8,128)(2,1)} %broadcast_in_dim.5), calls=%async_computation.5 | async-start | bytes 524288 | tf_op jit(solution)/shard_map/all_to_all | solution.py:253
  161.0 0.8 copy.25
  161.8 11.2 %all-to-all-done.5 = bf16[64,16,128]{2,1,0:T(8,128)(2,1)S(1)} async-done(((bf16[64,16,128]{2,1,0:T(8,128)(2,1)}), bf16[64,16,128]{2,1,0:T(8,128)(2,1)S(1)}, u32[]{:S(2)}, u32[]{:S(2)}) %all-to-all-start.5) | async-done | bytes 262176 | tf_op jit(solution)/shard_map/all_to_all | solution.py:253
  173.0 0.8 bitcast_convert_fusion
  (12 shorter events, 0.1 us)
Async XLA Ops:
  2.1 15.8 %copy-start.2 = (bf16[8,180,768]{2,0,1:T(8,128)(2,1)S(1)}, bf16[8,180,768]{2,0,1:T(8,128)(2,1)}, u32[]{:S(2)}) copy-start(bf16[8,180,768]{2,0,1:T(8,128)(2,1)} %param.7) | copy-start | bytes 6635524
  4.9 47.2 %all-to-all-start = ((bf16[64,80,128]{2,1,0:T(8,128)(2,1)}), bf16[64,80,128]{2,1,0:T(8,128)(2,1)S(1)}, u32[]{:S(2)}, u32[]{:S(2)}) async-start(bf16[64,80,128]{2,1,0:T(8,128)(2,1)} %shard_map.77), calls=%async_computation | async-start | bytes 2621440 | tf_op jit(solution)/shard_map/all_to_all | solution.py:253
  52.1 1.2 copy-start
  88.8 33.5 %all-to-all-start.2 = ((bf16[64,64,128]{2,1,0:T(8,128)(2,1)}), bf16[64,64,128]{2,1,0:T(8,128)(2,1)S(1)}, u32[]{:S(2)}, u32[]{:S(2)}) async-start(bf16[64,64,128]{2,1,0:T(8,128)(2,1)} %shard_map.81), calls=%async_computation.2 | async-start | bytes 2097152 | tf_op jit(solution)/shard_map/all_to_all | solution.py:253
  107.6 53.4 %copy-start.3 = (bf16[8,180,128]{2,1,0:T(8,128)(2,1)S(1)}, bf16[8,180,128]{2,1,0:T(8,128)(2,1)}, u32[]{:S(2)}) copy-start(bf16[8,180,128]{2,1,0:T(8,128)(2,1)} %get-tuple-element.14) | copy-start | bytes 1105924
  122.3 1.0 copy-start.1
  153.5 19.5 %all-to-all-start.5 = ((bf16[64,16,128]{2,1,0:T(8,128)(2,1)}), bf16[64,16,128]{2,1,0:T(8,128)(2,1)S(1)}, u32[]{:S(2)}, u32[]{:S(2)}) async-start(bf16[64,16,128]{2,1,0:T(8,128)(2,1)} %broadcast_in_dim.5), calls=%async_computation.5 | async-start | bytes 524288 | tf_op jit(solution)/shard_map/all_to_all | solution.py:253

commit v3 on v2

v3 whole, which is shorter than its diff:
```python
import math

import jax
import jax.numpy as jnp
from jax import lax
from jax.experimental import pallas as pl
from jax.experimental.pallas import tpu as pltpu
from jax.sharding import Mesh, PartitionSpec as P

F32 = jnp.float32
BF16 = jnp.bfloat16
CORES = 2
CHIPS_X = 4
SLOTS = 8
META_ROWS = CORES * SLOTS
CODE, WHICH, VALID, HIGH, MID, LOW = 32, 33, 34, 35, 36, 37
WIDE = 256
GROUP = 16
VMEM = pl.BlockSpec(memory_space=pltpu.VMEM)
SMEM = pl.BlockSpec(memory_space=pltpu.SMEM)


def params():
    return pltpu.CompilerParams(vmem_limit_bytes=56 * 1024 * 1024)


def unit_rows(raw):
    length = jnp.sqrt(jnp.sum(raw * raw, axis=-1, keepdims=True) + 1e-06)
    return (raw / length, length)


def unit_back(grad, unit, length):
    return (grad - unit * jnp.sum(unit * grad, axis=-1, keepdims=True)) / length


def iota(shape, dim):
    return lax.broadcasted_iota(jnp.int32, shape, dim)


def request_kernel(reps, passes, query_ref, proj_ref, neg_ref, pos_ref, teacher_ref, send_ref):
    chips, _, emb_dim = send_ref.shape
    owners = chips * CORES
    queries, neg = neg_ref.shape
    query_len = pos_ref.shape[1]
    unit, _ = unit_rows(jnp.dot(query_ref[...], proj_ref[...], preferred_element_type=F32))
    emb = unit.astype(BF16)
    send_ref[:, : emb.shape[0], :] = jnp.broadcast_to(emb[None], (chips,) + emb.shape)
    target = jnp.exp(teacher_ref[...])
    target = target / jnp.sum(target, axis=-1, keepdims=True)
    high = target.astype(BF16).astype(F32)
    rest = target - high
    mid = rest.astype(BF16).astype(F32)
    low = (rest - mid).astype(BF16).astype(F32)
    ids = neg_ref[...]
    owner = lax.div(ids, jnp.int32(reps * passes))
    within = lax.rem(ids, jnp.int32(passes))
    before = (iota((neg, neg), 0) < iota((neg, neg), 1)).astype(F32).astype(BF16)
    line = iota((emb_dim - query_len, neg), 0) + query_len
    total = jnp.zeros((owners, 1), F32)
    meta = jnp.zeros((owners * SLOTS, emb_dim), F32)
    for q in range(queries):
        own = jnp.where(iota((owners, neg), 0) == owner[q : q + 1, :], 1.0, 0.0)
        rank = jnp.dot(own.astype(BF16), before, preferred_element_type=F32) + total
        total = total + jnp.sum(own, axis=1, keepdims=True)
        rank = jnp.sum(own * rank, axis=0, keepdims=True).astype(jnp.int32)
        slot = owner[q : q + 1, :] * SLOTS + rank
        table = jnp.where(iota((owners * SLOTS, neg), 0) == slot, 1.0, 0.0).astype(BF16)
        values = {
            CODE: (within[q : q + 1, :] * queries + q).astype(F32),
            WHICH: float(q),
            VALID: 1.0,
            HIGH: high[q : q + 1, :],
            MID: mid[q : q + 1, :],
            LOW: low[q : q + 1, :],
        }
        fields = jnp.zeros(line.shape, F32)
        for at, value in values.items():
            fields = jnp.where(line == at, value, fields)
        fields = jnp.concatenate([pos_ref[q].astype(F32), fields], axis=0)
        meta = meta + jnp.dot(table, fields.T.astype(BF16), preferred_element_type=F32)
    send_ref[:, emb.shape[0] :, :] = meta.reshape(chips, META_ROWS, emb_dim).astype(BF16)


def embed_kernel(hidden_ref, proj_ref, emb_ref, wide_ref):
    passes, pass_len, _ = hidden_ref.shape
    wide_ref[...] = jnp.zeros_like(wide_ref)
    for p in range(passes):
        unit, _ = unit_rows(jnp.dot(hidden_ref[p], proj_ref[...], preferred_element_type=F32))
        wide_ref[:pass_len, :] = unit
        emb_ref[p] = wide_ref[...].astype(BF16)


def picked(meta_ref, group, query_len):
    own = meta_ref[pl.ds(group * GROUP, GROUP)]
    return own.reshape(GROUP * SLOTS, own.shape[2]).T[:query_len]


def slot_code(code_ref, core, d, k, queries):
    code = code_ref[d, core * SLOTS + k]
    return lax.div(code, jnp.int32(queries)), lax.rem(code, jnp.int32(queries))


def places(core, other, shape, queries):
    source = (1 - core) if other else core
    return iota(shape, 2) - queries * (source * shape[0] + iota(shape, 0))


def token_kernel(capacity, block, other, core_ref, code_ref, recv_ref, emb_ref, *refs):
    if other:
        so_far_ref, *refs = refs
    meta_ref, token_ref, exp_ref, part_ref, acc_ref = refs
    chips, _, emb_dim = recv_ref.shape
    queries, query_len = block
    rows = queries * query_len
    core = core_ref[0]
    both = recv_ref[:, rows:, :].astype(F32)
    meta_ref[...] = jnp.where(core == 0, both[:, :SLOTS, :], both[:, SLOTS:, :])
    acc_ref[...] = jnp.zeros_like(acc_ref)
    lane = iota((query_len, WIDE), 1).astype(F32)

    def one_group(group, carry):
        spots = picked(meta_ref, group, query_len)
        for step in range(GROUP):
            d = group * GROUP + step
            for k in range(capacity):
                p, j = slot_code(code_ref, core, d, k, queries)
                at = step * SLOTS + k
                mask = jnp.where(spots[:, at : at + 1] == lane, 1.0, 0.0).astype(BF16)
                token = jnp.dot(mask, emb_ref[p], preferred_element_type=F32)
                token_ref[d, k] = token.astype(BF16)
                start = pl.multiple_of(j * query_len, query_len)
                query = recv_ref[d, pl.ds(start, query_len), :].astype(F32)
                acc_ref[d, k : k + 1, :] = jnp.sum(token * query, axis=0, keepdims=True)
        return carry

    lax.fori_loop(0, chips // GROUP, one_group, 0)
    meta = meta_ref[...]
    exps = jnp.exp(jnp.sum(acc_ref[...], axis=-1, keepdims=True)) * meta[:, :, VALID : VALID + 1]
    exp_ref[...] = jnp.broadcast_to(exps, exp_ref.shape)
    which = meta[:, :, WHICH : WHICH + 1]
    place = places(core, other, (chips, 1, emb_dim), queries)
    total = jnp.zeros(place.shape, F32)
    for q in range(queries):
        share = jnp.sum(jnp.where(which == float(q), exps, 0.0), axis=1, keepdims=True)
        total = total + jnp.where(place == q, share, 0.0)
    total = jnp.sum(total, axis=0, keepdims=True)
    if other:
        total = total + so_far_ref[...]
    part_ref[...] = jnp.broadcast_to(total, part_ref.shape)


def weight_kernel(capacity, block, neg, other, core_ref, parts_ref, meta_ref, exp_ref, token_ref, out_ref, weight_ref):
    queries, query_len = block
    chips, _, emb_dim = exp_ref.shape
    meta = meta_ref[...]
    exps = exp_ref[...]
    place = places(core_ref[0], other, (chips, 1, emb_dim), queries)
    sums = jnp.sum(parts_ref[...], axis=0, keepdims=True)
    which = meta[:, :, WHICH : WHICH + 1]
    share = jnp.zeros_like(exps)
    for q in range(queries):
        norm = jnp.sum(jnp.where(place == q, sums, 0.0), axis=-1, keepdims=True)
        share = share + jnp.where(which == float(q), exps / norm, 0.0)
    target = meta[:, :, HIGH : HIGH + 1] + meta[:, :, MID : MID + 1]
    target = target + meta[:, :, LOW : LOW + 1]
    weight_ref[...] = neg * (share - target) * meta[:, :, VALID : VALID + 1]

    def one_device(d, carry):
        chosen = meta_ref[d][:, WHICH : WHICH + 1]
        weights = weight_ref[d]
        for q in range(queries):
            scale = jnp.where(chosen == float(q), weights, 0.0)
            grad = jnp.zeros((query_len, emb_dim), F32)
            for k in range(capacity):
                grad = grad + scale[k : k + 1, :] * token_ref[d, k].astype(F32)
            out_ref[d, q * query_len : (q + 1) * query_len, :] = grad.astype(BF16)
        return carry

    lax.fori_loop(0, chips, one_device, 0, unroll=4)


def passage_kernel(capacity, block, core_ref, hidden_ref, proj_ref, *refs):
    halves = [refs[4 * h : 4 * h + 4] for h in range(CORES)]
    grad_ref, term_ref, table_ref, total_ref = refs[4 * CORES :]
    passes, pass_len, _ = hidden_ref.shape
    queries, query_len = block
    rows = queries * query_len
    core = core_ref[0]
    lane = iota((query_len, WIDE), 1).astype(F32)
    total_ref[...] = jnp.zeros_like(total_ref)
    for code_ref, recv_ref, meta_ref, weight_ref in halves:
        chips, _, emb_dim = recv_ref.shape

        def one_group(group, carry):
            spots = picked(meta_ref, group, query_len)
            table_ref[...] = jnp.zeros_like(table_ref)
            for step in range(GROUP):
                d = group * GROUP + step
                for k in range(capacity):
                    p, j = slot_code(code_ref, core, d, k, queries)
                    at = step * SLOTS + k
                    start = pl.multiple_of(step * rows + j * query_len, query_len)
                    weight = weight_ref[d, k : k + 1, :]
                    weight = jnp.concatenate([weight] * (WIDE // emb_dim), axis=1)
                    added = jnp.where(spots[:, at : at + 1] == lane, weight, 0.0).astype(BF16)
                    table_ref[p, pl.ds(start, query_len), :] = (
                        table_ref[p, pl.ds(start, query_len), :] + added
                    )
            left = recv_ref[pl.ds(group * GROUP, GROUP), :rows, :].reshape(GROUP * rows, emb_dim)
            left = left.T
            for p in range(passes):
                total_ref[p] = total_ref[p] + jnp.dot(
                    left, table_ref[p], preferred_element_type=F32
                )
            return carry

        lax.fori_loop(0, chips // GROUP, one_group, 0)
    term = jnp.zeros(term_ref.shape, F32)
    for p in range(passes):
        unit, length = unit_rows(jnp.dot(hidden_ref[p], proj_ref[...], preferred_element_type=F32))
        grad = total_ref[p].T[:pass_len]
        raw_grad = unit_back(grad, unit, length).astype(BF16)
        grad_ref[p] = raw_grad
        term = term + lax.dot_general(
            raw_grad, hidden_ref[p], (((0,), (0,)), ((), ())), preferred_element_type=F32
        )
    term_ref[...] = term


def query_kernel(parts_ref, query_ref, proj_ref, term_ref, out_ref):
    hidden = query_ref[...]
    unit, length = unit_rows(jnp.dot(hidden, proj_ref[...], preferred_element_type=F32))
    grad = jnp.sum(parts_ref[...].astype(F32), axis=0)
    raw_grad = unit_back(grad, unit, length).astype(BF16)
    term = term_ref[...] + lax.dot_general(
        raw_grad, hidden, (((0,), (0,)), ((), ())), preferred_element_type=F32
    )
    out_ref[...] = term.T.reshape(out_ref.shape).astype(BF16)


def swap(array, axes):
    return lax.all_to_all(array, axes, split_axis=0, concat_axis=0, tiled=True)


def to_other_core(array):
    return lax.ppermute(array, "core", [(c, CORES - 1 - c) for c in range(CORES)])


def per_device(query_hidden, passage_hidden, projection, negatives, positions, teacher):
    query_count, query_len, hidden_dim = query_hidden.shape
    pass_count, pass_len, _ = passage_hidden.shape
    emb_dim = projection.shape[1]
    neg_count = negatives.shape[1]
    chips = lax.axis_size("x") * lax.axis_size("z")
    owners = chips * CORES
    reps = lax.axis_size("rep")
    pair_count = query_count * neg_count
    capacity = (pair_count + owners - 2) // (owners - 1)
    rows = query_count * query_len
    block = (query_count, query_len)
    query_flat = query_hidden.reshape(rows, hidden_dim)
    core = lax.axis_index("core").reshape(1)

    def call(kernel, outs, scratch, scalars, *args):
        return pl.pallas_call(
            kernel,
            out_shape=outs,
            in_specs=[SMEM if n in scalars else VMEM for n in range(len(args))],
            out_specs=jax.tree.map(lambda _: VMEM, outs),
            scratch_shapes=scratch,
            compiler_params=params(),
        )(*args)

    shape = jax.ShapeDtypeStruct
    send = call(
        lambda *refs: request_kernel(reps, pass_count, *refs),
        shape((chips, rows + META_ROWS, emb_dim), BF16),
        [],
        (),
        query_flat,
        projection,
        negatives,
        jnp.swapaxes(positions, 1, 2),
        teacher,
    )
    near = swap(send, ("x", "z"))
    far = to_other_core(near)
    emb = call(
        embed_kernel,
        shape((pass_count, WIDE, emb_dim), BF16),
        [pltpu.VMEM((WIDE, emb_dim), F32)],
        (),
        passage_hidden,
        projection,
    )
    slot_shape = (chips, SLOTS, emb_dim)
    halves = []
    so_far = []
    for other, recv in ((False, near), (True, far)):
        codes = recv[:, rows:, CODE].astype(jnp.int32)
        meta, tokens, exps, part = call(
            lambda *refs: token_kernel(capacity, block, other, *refs),
            (
                shape(slot_shape, F32),
                shape((chips, capacity, query_len, emb_dim), BF16),
                shape(slot_shape, F32),
                shape((owners if other else 1, 1, emb_dim), F32),
            ),
            [pltpu.VMEM(slot_shape, F32)],
            (0, 1),
            core,
            codes,
            recv,
            emb,
            *so_far,
        )
        so_far = [part]
        halves.append((codes, recv, meta, exps, tokens))
    parts = swap(part, ("x", "z", "core"))

    def weigh(other):
        codes, recv, meta, exps, tokens = halves[other]
        return call(
            lambda *refs: weight_kernel(capacity, block, neg_count, other, *refs),
            (shape((chips, rows, emb_dim), BF16), shape(slot_shape, F32)),
            [],
            (0,),
            core,
            parts,
            meta,
            exps,
            tokens,
        )

    far_part, far_weight = weigh(True)
    far_part = to_other_core(far_part)
    near_part, near_weight = weigh(False)
    query_parts = (near_part.astype(F32) + far_part.astype(F32)).astype(BF16)
    query_parts, near_weight = lax.optimization_barrier((query_parts, near_weight))
    query_parts = swap(query_parts, ("x", "z"))
    passage_args = []
    for (codes, recv, meta, _, _), weight in zip(halves, (near_weight, far_weight)):
        passage_args += [codes, recv, meta, weight]
    grad_passages, term = call(
        lambda *refs: passage_kernel(capacity, block, *refs),
        (
            shape((pass_count, pass_len, emb_dim), BF16),
            shape((emb_dim, hidden_dim), F32),
        ),
        [
            pltpu.VMEM((pass_count, GROUP * rows, WIDE), BF16),
            pltpu.VMEM((pass_count, emb_dim, WIDE), F32),
        ],
        (0, 3, 7),
        core,
        passage_hidden,
        projection,
        *passage_args,
    )
    groups = lax.axis_size(("x", "core", "rep"))
    pieces = call(
        query_kernel,
        shape((groups, hidden_dim // groups, emb_dim), BF16),
        [],
        (),
        query_parts,
        query_flat,
        projection,
        term,
    )
    pieces = swap(pieces, ("x", "core", "rep"))
    mine = jnp.sum(pieces.astype(F32), axis=0).astype(BF16)
    copies = swap(jnp.broadcast_to(mine[None], (lax.axis_size("z"),) + mine.shape), "z")
    scale = 1.0 / math.sqrt(owners * reps * (query_count * query_len + pass_count * pass_len))
    mine = (jnp.sum(copies.astype(F32), axis=0) * scale).astype(BF16)
    copies = swap(jnp.broadcast_to(mine[None], (groups,) + mine.shape), ("x", "core", "rep"))
    return (grad_passages, copies.reshape(hidden_dim, emb_dim).astype(F32))


def solution(mesh):
    devices = mesh.devices.reshape(CHIPS_X, -1, CORES, mesh.shape["rep"])
    mesh = Mesh(devices, ("x", "z", "core", "rep"))
    whole = ("x", "z", "core", "rep")
    in_specs = (
        P(whole, None, None),
        P(whole, None, None),
        P(),
        P(whole, None),
        P(whole, None, None),
        P(whole, None),
    )
    out_specs = (P(whole, None, None), P())
    return jax.shard_map(
        per_device, mesh=mesh, in_specs=in_specs, out_specs=out_specs, check_vma=False
    )
```

time: 175 us -> 143 us (0.82)
  waiting for transfers between devices: 54.9 us -> 10.6 us
  blocking collectives: 41.9 us -> 68.6 us
  starting transfers between devices: 25.4 us -> 15.4 us
  Pallas kernels: 43 us -> 37.9 us
    all_to_all x3 -> x2, waiting for transfers between devices: 54.9 us -> 10.6 us  [swap(): return lax.all_to_all(array, axes, split_axis=0, concat_axis=0, tiled=True)]
    all_to_all x3 -> x4, blocking collectives: 41.9 us -> 68.6 us  [swap(): return lax.all_to_all(array, axes, split_axis=0, concat_axis=0, tiled=True)]
    all_to_all x3 -> x2, starting transfers between devices: 25.4 us -> 9.57 us  [swap(): return lax.all_to_all(array, axes, split_axis=0, concat_axis=0, tiled=True)]
    ppermute x0 -> x2, starting transfers between devices: none -> 5.83 us  [to_other_core(): lax.ppermute(array, 'core', [(c, CORES - 1 - c) for c in range(CORES)])]
    pallas_call x6 -> x8, Pallas kernels: 43 us -> 37.9 us  [call(): pl.pallas_call(kernel, out_shape=outs, in_specs=[SMEM if n in scalars els...]
    unnamed x12, local copies, waits for them, and re-layouts: 5.52 us -> 3.4 us
  transfers between devices with their start and end apart: 3 -> 4, of which waited for: 3 -> 2; matrix products, arithmetic and copies ran while one was open for 1% -> 3% of each run, Pallas kernels for 10% -> 17%
where the time goes in v3:
time: 143 us; the launch traced here: 142 us
  blocking collectives  68.6 us (48%)
  Pallas kernels  37.9 us (27%)
  starting transfers between devices  15.4 us (11%)
  waiting for transfers between devices  10.6 us (7%)
  local copies, waits for them, and re-layouts  5.83 us (4%)
  other arithmetic  3.09 us (2%)
    all_to_all x4, blocking collectives, swap(): return lax.all_to_all(array, axes, split_axis=0, concat_axis=0, tiled=True)  68.6 us
    pallas_call x8, Pallas kernels, call(): pl.pallas_call(kernel, out_shape=outs, in_specs=[SMEM if n in scalars els...  37.9 us
    all_to_all x2, waiting for transfers between devices, swap(): return lax.all_to_all(array, axes, split_axis=0, concat_axis=0, tiled=True)  10.6 us
    all_to_all x2, starting transfers between devices, swap(): return lax.all_to_all(array, axes, split_axis=0, concat_axis=0, tiled=True)  9.57 us
    ppermute x2, starting transfers between devices, to_other_core(): lax.ppermute(array, 'core', [(c, CORES - 1 - c) for c in range(CORES)])  5.83 us
    unnamed x12, local copies, waits for them, and re-layouts  3.4 us
  transfers between devices with their start and end apart: 4, of which 2 were waited for; matrix products, arithmetic and copies ran while one was open for 3% of the time, Pallas kernels for 17%

profile of v3, /device:TPU:1, one launch (start us, length us, event | category | flops | bytes accessed | tf_op | source)
XLA Modules:
  0.0 142.2 jit_solution(2250722060113357826)
XLA Ops:
  0.6 2.5 %shard_map.77 = bf16[32,80,128]{2,1,0:T(8,128)(2,1)} custom-call(bf16[64,768]{1,0:T(8,128)(2,1)} %bitcast.10, bf16[768,128]{1,0:T(8,128)(2,1)} %proj_ref.3, s32[2,128]{1,0:T(2,128)} %refs_2_.2, s32[2,32,128]{2,1,0:T(8,128)} %bitcast.16, f32[2,128]{1,0:T(2,128)} %refs_4_.1), custom_call_target="tpu_custom_call" | custom-call | tf_op jit(solution)/shard_map/pallas_call | solution.py:265
  3.1 28.2 %all_to_all.30.refs_2_.refs_4_ = bf16[32,80,128]{2,1,0:T(8,128)(2,1)S(1)} all-to-all(bf16[32,80,128]{2,1,0:T(8,128)(2,1)} %shard_map.77), channel_id=1, replica_groups=mesh['x'=4,'z'=8,'core'=2,'rep'=4] {'x','z'}, dimensions={0} | all-to-all | bytes 1310720 | tf_op jit(solution)/shard_map/all_to_all | solution.py:242
  31.3 5.0 %collective-permute-start = (bf16[32,80,128]{2,1,0:T(8,128)(2,1)S(1)}, bf16[32,80,128]{2,1,0:T(8,128)(2,1)S(1)}, u32[]{:S(2)}, u32[]{:S(2)}) collective-permute-start(bf16[32,80,128]{2,1,0:T(8,128)(2,1)S(1)} %all_to_all.30.refs_2_.refs_4_), channel_id=1, source_target_pairs={{0,4},{4,0},{1,5},{5,1},{2,6},{6,2},{3,7},{7,3},{8,12},{12,8},{9,1... | collective-permute-start | bytes 1966088 | tf_op jit(solution)/shard_map/ppermute | solution.py:246
  36.4 1.8 %copy.34.hidden_ref.refs_1_ = bf16[8,180,768]{2,1,0:T(8,128)(2,1)} copy(bf16[8,180,768]{2,0,1:T(8,128)(2,1)S(1)} %copy-done.2) | data formatting | bytes 4423680 | tf_op args[1]
  38.2 3.4 %shard_map.78.refs_3_ = bf16[8,256,128]{2,1,0:T(8,128)(2,1)} custom-call(bf16[8,180,768]{2,1,0:T(8,128)(2,1)} %copy.34.hidden_ref.refs_1_, bf16[768,128]{1,0:T(8,128)(2,1)} %proj_ref.3), custom_call_target="tpu_custom_call" | custom-call | tf_op jit(solution)/shard_map/pallas_call | solution.py:265
  41.7 0.9 copy.38
  42.6 4.3 %shard_map.79 = (f32[32,8,128]{2,1,0:T(8,128)}, bf16[32,5,32,128]{3,2,1,0:T(8,128)(2,1)}, f32[32,8,128]{2,1,0:T(8,128)}, f32[1,1,128]{2,1,0:T(1,128)}) custom-call(s32[1]{0:T(128)} %bitcast.refs_0_, s32[32,16]{1,0:T(8,128)} %bitcast.12, bf16[32,80,128]{2,1,0:T(8,128)(2,1)} %copy-done, bf16[8,256,128]{2,1,0:T(8,128)(2,1)} %shard_map.78.refs_3_), custom_call_target="tpu_custom_call" | custom-call | tf_op jit(solution)/shard_map/pallas_call | solution.py:265
  47.0 0.9 copy.39
  47.8 4.3 %shard_map.80 = (f32[32,8,128]{2,1,0:T(8,128)}, bf16[32,5,32,128]{3,2,1,0:T(8,128)(2,1)}, f32[32,8,128]{2,1,0:T(8,128)}, f32[64,1,128]{2,1,0:T(1,128)}) custom-call(s32[1]{0:T(128)} %bitcast.refs_0_, s32[32,16]{1,0:T(8,128)} %bitcast.14, bf16[32,80,128]{2,1,0:T(8,128)(2,1)} %copy-done.1, bf16[8,256,128]{2,1,0:T(8,128)(2,1)} %shard_map.78.refs_3_, ...), custom_call_target="tpu_custom_call" | custom-call | tf_op jit(solution)/shard_map/pallas_call | solution.py:265
  52.2 14.4 %all_to_all.31.refs_1_ = f32[64,1,128]{2,1,0:T(1,128)} all-to-all(f32[64,1,128]{2,1,0:T(1,128)} %get-tuple-element.20), channel_id=1, replica_groups=mesh['x'=4,'z'=8,'core'=2,'rep'=4] {'x','z','core'}, dimensions={0} | all-to-all | bytes 65536 | tf_op jit(solution)/shard_map/all_to_all | solution.py:242
  66.6 3.9 %shard_map.82 = (bf16[32,64,128]{2,1,0:T(8,128)(2,1)}, f32[32,8,128]{2,1,0:T(8,128)}) custom-call(s32[1]{0:T(128)} %bitcast.refs_0_, f32[64,1,128]{2,1,0:T(1,128)} %all_to_all.31.refs_1_, f32[32,8,128]{2,1,0:T(8,128)} %get-tuple-element.24.refs_2_.refs_9_, f32[32,8,128]{2,1,0:T(8,128)} %get-tuple-element.25.refs_3_, ...), custom_call_target="tpu_custom_call" | custom-call | tf_op jit(solution)/shard_map/pallas_call | solution.py:265
  70.4 0.8 collective-permute-start.1
  71.2 3.8 %shard_map.81 = (bf16[32,64,128]{2,1,0:T(8,128)(2,1)}, f32[32,8,128]{2,1,0:T(8,128)}) custom-call(s32[1]{0:T(128)} %bitcast.refs_0_, f32[64,1,128]{2,1,0:T(1,128)} %all_to_all.31.refs_1_, f32[32,8,128]{2,1,0:T(8,128)} %get-tuple-element.18.refs_2_.refs_5_, f32[32,8,128]{2,1,0:T(8,128)} %get-tuple-element.21.refs_3_, ...), custom_call_target="tpu_custom_call" | custom-call | tf_op jit(solution)/shard_map/pallas_call | solution.py:265
  75.1 2.0 %add_convert_fusion = bf16[32,64,128]{2,1,0:T(8,128)(2,1)} fusion(bf16[32,64,128]{2,1,0:T(8,128)(2,1)S(1)} %collective-permute-done.1, bf16[32,64,128]{2,1,0:T(8,128)(2,1)} %get-tuple-element.23), kind=kLoop, calls=%fused_computation | loop fusion | flops 1048576 | bytes 1572864 | tf_op jit(solution)/shard_map/convert_element_type | solution.py:338
  77.1 4.1 %all-to-all-start.2 = ((bf16[32,64,128]{2,1,0:T(8,128)(2,1)}), bf16[32,64,128]{2,1,0:T(8,128)(2,1)S(1)}, u32[]{:S(2)}, u32[]{:S(2)}) async-start(bf16[32,64,128]{2,1,0:T(8,128)(2,1)} %add_convert_fusion), calls=%async_computation.2 | async-start | bytes 1048576 | tf_op jit(solution)/shard_map/all_to_all | solution.py:242
  81.2 13.1 %shard_map.83 = (bf16[8,180,128]{2,1,0:T(8,128)(2,1)}, f32[128,768]{1,0:T(8,128)}) custom-call(s32[1]{0:T(128)} %bitcast.refs_0_, bf16[8,180,768]{2,1,0:T(8,128)(2,1)} %copy.34.hidden_ref.refs_1_, bf16[768,128]{1,0:T(8,128)(2,1)} %proj_ref.3, s32[32,16]{1,0:T(8,128)} %bitcast.13, bf16[32,80,128]{2,1,0:T(8,128)(2,1)} %copy-done, ...), custom_call_target="tpu_custom_call" | custom-call | tf_op jit(solution)/shard_map/pallas_call | solution.py:265
  94.3 3.2 %all-to-all-done.2.parts_ref = bf16[32,64,128]{2,1,0:T(8,128)(2,1)S(1)} async-done(((bf16[32,64,128]{2,1,0:T(8,128)(2,1)}), bf16[32,64,128]{2,1,0:T(8,128)(2,1)S(1)}, u32[]{:S(2)}, u32[]{:S(2)}) %all-to-all-start.2) | async-done | bytes 524320 | tf_op jit(solution)/shard_map/all_to_all | solution.py:242
  97.4 0.8 copy-done.3
  98.2 2.6 %shard_map.84 = bf16[32,24,128]{2,1,0:T(8,128)(2,1)} custom-call(bf16[32,64,128]{2,1,0:T(8,128)(2,1)} %copy-done.3, bf16[64,768]{1,0:T(8,128)(2,1)} %bitcast.11, bf16[768,128]{1,0:T(8,128)(2,1)} %proj_ref.3, f32[128,768]{1,0:T(8,128)} %get-tuple-element.33.term_ref), custom_call_target="tpu_custom_call" | custom-call | tf_op jit(solution)/shard_map/pallas_call | solution.py:265
  100.8 15.1 %all_to_all.32 = bf16[32,24,128]{2,1,0:T(8,128)(2,1)S(1)} all-to-all(bf16[32,24,128]{2,1,0:T(8,128)(2,1)} %shard_map.84), channel_id=1, replica_groups=mesh['x'=4,'z'=8,'core'=2,'rep'=4] {'x','core','rep'}, dimensions={0} | all-to-all | bytes 393216 | tf_op jit(solution)/shard_map/all_to_all | solution.py:242
  116.0 10.9 %all_to_all.33 = bf16[8,24,128]{2,1,0:T(8,128)(2,1)S(1)} all-to-all(bf16[8,24,128]{2,1,0:T(8,128)(2,1)S(1)} %broadcast_in_dim.4), channel_id=1, replica_groups=mesh['x'=4,'z'=8,'core'=2,'rep'=4] {'z'}, dimensions={0} | all-to-all | bytes 98304 | tf_op jit(solution)/shard_map/all_to_all | solution.py:242
  127.6 5.5 %all-to-all-start.5 = ((bf16[32,24,128]{2,1,0:T(8,128)(2,1)}), bf16[32,24,128]{2,1,0:T(8,128)(2,1)S(1)}, u32[]{:S(2)}, u32[]{:S(2)}) async-start(bf16[32,24,128]{2,1,0:T(8,128)(2,1)} %broadcast_in_dim.5), calls=%async_computation.5 | async-start | bytes 393216 | tf_op jit(solution)/shard_map/all_to_all | solution.py:242
  133.1 0.8 copy.37
  133.9 7.5 %all-to-all-done.5 = bf16[32,24,128]{2,1,0:T(8,128)(2,1)S(1)} async-done(((bf16[32,24,128]{2,1,0:T(8,128)(2,1)}), bf16[32,24,128]{2,1,0:T(8,128)(2,1)S(1)}, u32[]{:S(2)}, u32[]{:S(2)}) %all-to-all-start.5) | async-done | bytes 196640 | tf_op jit(solution)/shard_map/all_to_all | solution.py:242
  (19 shorter events, 1.8 us)
Async XLA Ops:
  0.6 35.7 %copy-start.2 = (bf16[8,180,768]{2,0,1:T(8,128)(2,1)S(1)}, bf16[8,180,768]{2,0,1:T(8,128)(2,1)}, u32[]{:S(2)}) copy-start(bf16[8,180,768]{2,0,1:T(8,128)(2,1)} %param.7) | copy-start | bytes 6635524
  31.3 10.3 %copy-start = (bf16[32,80,128]{2,1,0:T(8,128)(2,1)}, bf16[32,80,128]{2,1,0:T(8,128)(2,1)S(1)}, u32[]{:S(2)}) copy-start(bf16[32,80,128]{2,1,0:T(8,128)(2,1)S(1)} %all_to_all.30.refs_2_.refs_4_) | copy-start | bytes 1966084
  31.3 15.5 %collective-permute-start = (bf16[32,80,128]{2,1,0:T(8,128)(2,1)S(1)}, bf16[32,80,128]{2,1,0:T(8,128)(2,1)S(1)}, u32[]{:S(2)}, u32[]{:S(2)}) collective-permute-start(bf16[32,80,128]{2,1,0:T(8,128)(2,1)S(1)} %all_to_all.30.refs_2_.refs_4_), channel_id=1, source_target_pairs={{0,4},{4,0},{1,5},{5,1},{2,6},{6,2},{3,7},{7,3},{8,12},{12,8},{9,1... | collective-permute-start | bytes 1966088 | tf_op jit(solution)/shard_map/ppermute | solution.py:246
  46.9 1.0 copy-start.1
  70.4 4.7 %collective-permute-start.1 = (bf16[32,64,128]{2,1,0:T(8,128)(2,1)}, bf16[32,64,128]{2,1,0:T(8,128)(2,1)S(1)}, u32[]{:S(2)}, u32[]{:S(2)}) collective-permute-start(bf16[32,64,128]{2,1,0:T(8,128)(2,1)} %get-tuple-element.27), channel_id=1, source_target_pairs={{0,4},{4,0},{1,5},{5,1},{2,6},{6,2},{3,7},{7,3},{8,12},{12,8},{9,1... | collective-permute-start | bytes 1572872 | tf_op jit(solution)/shard_map/ppermute | solution.py:246
  77.1 20.3 %all-to-all-start.2 = ((bf16[32,64,128]{2,1,0:T(8,128)(2,1)}), bf16[32,64,128]{2,1,0:T(8,128)(2,1)S(1)}, u32[]{:S(2)}, u32[]{:S(2)}) async-start(bf16[32,64,128]{2,1,0:T(8,128)(2,1)} %add_convert_fusion), calls=%async_computation.2 | async-start | bytes 1048576 | tf_op jit(solution)/shard_map/all_to_all | solution.py:242
  94.3 38.9 %copy-start.4 = (bf16[8,180,128]{2,1,0:T(8,128)(2,1)S(1)}, bf16[8,180,128]{2,1,0:T(8,128)(2,1)}, u32[]{:S(2)}) copy-start(bf16[8,180,128]{2,1,0:T(8,128)(2,1)} %get-tuple-element.40) | copy-start | bytes 1105924
  97.4 0.8 copy-start.3
  127.6 13.8 %all-to-all-start.5 = ((bf16[32,24,128]{2,1,0:T(8,128)(2,1)}), bf16[32,24,128]{2,1,0:T(8,128)(2,1)S(1)}, u32[]{:S(2)}, u32[]{:S(2)}) async-start(bf16[32,24,128]{2,1,0:T(8,128)(2,1)} %broadcast_in_dim.5), calls=%async_computation.5 | async-start | bytes 393216 | tf_op jit(solution)/shard_map/all_to_all | solution.py:242

commit v4 on v3

--- a/solution.py
+++ b/solution.py
@@ -12,8 +12,9 @@
 CORES = 2
 CHIPS_X = 4
 SLOTS = 8
-META_ROWS = CORES * SLOTS
-CODE, WHICH, VALID, HIGH, MID, LOW = 32, 33, 34, 35, 36, 37
+META_ROWS = 8
+PER_CORE = 2
+CODE, WHICH, VALID, HIGH, MID, LOW = range(6)
 WIDE = 256
 GROUP = 16
 VMEM = pl.BlockSpec(memory_space=pltpu.VMEM)
@@ -37,11 +38,12 @@
     return lax.broadcasted_iota(jnp.int32, shape, dim)
 
 
-def request_kernel(reps, passes, query_ref, proj_ref, neg_ref, pos_ref, teacher_ref, send_ref):
+def request_kernel(reps, passes, query_ref, proj_ref, neg_ref, pos_ref, teacher_ref, send_ref, meta_ref):
     chips, _, emb_dim = send_ref.shape
     owners = chips * CORES
     queries, neg = neg_ref.shape
     query_len = pos_ref.shape[1]
+    per_row = emb_dim // query_len
     unit, _ = unit_rows(jnp.dot(query_ref[...], proj_ref[...], preferred_element_type=F32))
     emb = unit.astype(BF16)
     send_ref[:, : emb.shape[0], :] = jnp.broadcast_to(emb[None], (chips,) + emb.shape)
@@ -55,30 +57,38 @@
     owner = lax.div(ids, jnp.int32(reps * passes))
     within = lax.rem(ids, jnp.int32(passes))
     before = (iota((neg, neg), 0) < iota((neg, neg), 1)).astype(F32).astype(BF16)
-    line = iota((emb_dim - query_len, neg), 0) + query_len
     total = jnp.zeros((owners, 1), F32)
-    meta = jnp.zeros((owners * SLOTS, emb_dim), F32)
+    meta = [jnp.zeros((chips, PER_CORE * emb_dim), F32) for _ in range(CORES)]
     for q in range(queries):
-        own = jnp.where(iota((owners, neg), 0) == owner[q : q + 1, :], 1.0, 0.0)
+        mine = owner[q : q + 1, :]
+        own = jnp.where(iota((owners, neg), 0) == mine, 1.0, 0.0)
         rank = jnp.dot(own.astype(BF16), before, preferred_element_type=F32) + total
         total = total + jnp.sum(own, axis=1, keepdims=True)
         rank = jnp.sum(own * rank, axis=0, keepdims=True).astype(jnp.int32)
-        slot = owner[q : q + 1, :] * SLOTS + rank
-        table = jnp.where(iota((owners * SLOTS, neg), 0) == slot, 1.0, 0.0).astype(BF16)
+        spots = pos_ref[q].astype(F32)
+        lines = [jnp.where(rank == k, spots, 0.0) for k in range(per_row + 1)]
         values = {
             CODE: (within[q : q + 1, :] * queries + q).astype(F32),
-            WHICH: float(q),
-            VALID: 1.0,
+            WHICH: jnp.full((1, neg), float(q), F32),
+            VALID: jnp.ones((1, neg), F32),
             HIGH: high[q : q + 1, :],
             MID: mid[q : q + 1, :],
             LOW: low[q : q + 1, :],
         }
-        fields = jnp.zeros(line.shape, F32)
-        for at, value in values.items():
-            fields = jnp.where(line == at, value, fields)
-        fields = jnp.concatenate([pos_ref[q].astype(F32), fields], axis=0)
-        meta = meta + jnp.dot(table, fields.T.astype(BF16), preferred_element_type=F32)
-    send_ref[:, emb.shape[0] :, :] = meta.reshape(chips, META_ROWS, emb_dim).astype(BF16)
+        line = iota((SLOTS, neg), 0)
+        lines += [jnp.where(line == rank, values[at], 0.0) for at in sorted(values)]
+        lines = jnp.concatenate(lines, axis=0)
+        extra = PER_CORE * emb_dim - lines.shape[0]
+        lines = jnp.concatenate([lines, jnp.zeros((extra, neg), F32)], axis=0)
+        fields = jnp.concatenate([lines[:emb_dim].T, lines[emb_dim:].T], axis=1).astype(BF16)
+        for c in range(CORES):
+            to = jnp.where(iota((chips, neg), 0) * CORES + c == mine, 1.0, 0.0).astype(BF16)
+            meta[c] = meta[c] + jnp.dot(to, fields, preferred_element_type=F32)
+    meta_ref[...] = jnp.zeros_like(meta_ref)
+    for c in range(CORES):
+        for r in range(PER_CORE):
+            meta_ref[:, c * PER_CORE + r, :] = meta[c][:, r * emb_dim : (r + 1) * emb_dim]
+    send_ref[:, emb.shape[0] :, :] = meta_ref[...].astype(BF16)
 
 
 def embed_kernel(hidden_ref, proj_ref, emb_ref, wide_ref):
@@ -90,119 +100,142 @@
         emb_ref[p] = wide_ref[...].astype(BF16)
 
 
-def picked(meta_ref, group, query_len):
-    own = meta_ref[pl.ds(group * GROUP, GROUP)]
-    return own.reshape(GROUP * SLOTS, own.shape[2]).T[:query_len]
-
-
-def slot_code(code_ref, core, d, k, queries):
-    code = code_ref[d, core * SLOTS + k]
+def field(extra, query_len, name):
+    lanes = extra.shape[1]
+    return pltpu.roll(extra, lanes - query_len - name * SLOTS, 1)
+
+
+def picked(spots_ref, extra_ref, group, query_len, capacity):
+    spots = spots_ref[pl.ds(pl.multiple_of(group * GROUP, GROUP), GROUP), :].T
+    extra = extra_ref[pl.ds(pl.multiple_of(group * GROUP, GROUP), GROUP), :].T
+    both = jnp.concatenate([spots, extra[:query_len]], axis=0)
+    return [both[k * query_len : (k + 1) * query_len] for k in range(capacity)]
+
+
+def slot_code(code_ref, d, k, query_len, queries):
+    code = code_ref[d, query_len + k]
     return lax.div(code, jnp.int32(queries)), lax.rem(code, jnp.int32(queries))
 
 
 def places(core, other, shape, queries):
     source = (1 - core) if other else core
-    return iota(shape, 2) - queries * (source * shape[0] + iota(shape, 0))
-
-
-def token_kernel(capacity, block, other, core_ref, code_ref, recv_ref, emb_ref, *refs):
+    return iota(shape, 1) - queries * (source * shape[0] + iota(shape, 0))
+
+
+def token_kernel(capacity, block, other, core_ref, recv_ref, emb_ref, *refs):
     if other:
         so_far_ref, *refs = refs
-    meta_ref, token_ref, exp_ref, part_ref, acc_ref = refs
+    spots_ref, extra_ref, code_ref, token_ref, exp_ref, part_ref, both_ref, acc_ref, scalar_ref, sem = refs
     chips, _, emb_dim = recv_ref.shape
     queries, query_len = block
     rows = queries * query_len
     core = core_ref[0]
-    both = recv_ref[:, rows:, :].astype(F32)
-    meta_ref[...] = jnp.where(core == 0, both[:, :SLOTS, :], both[:, SLOTS:, :])
+    both_ref[...] = recv_ref[:, rows:, :].astype(F32)
+    spots_ref[...] = jnp.where(core == 0, both_ref[:, 0, :], both_ref[:, PER_CORE, :])
+    extra = jnp.where(core == 0, both_ref[:, 1, :], both_ref[:, PER_CORE + 1, :])
+    extra_ref[...] = extra
+    code_ref[...] = extra.astype(jnp.int32)
+    copy = pltpu.make_async_copy(code_ref, scalar_ref, sem)
+    copy.start()
     acc_ref[...] = jnp.zeros_like(acc_ref)
+    copy.wait()
     lane = iota((query_len, WIDE), 1).astype(F32)
 
     def one_group(group, carry):
-        spots = picked(meta_ref, group, query_len)
+        spots = picked(spots_ref, extra_ref, group, query_len, capacity)
         for step in range(GROUP):
             d = group * GROUP + step
             for k in range(capacity):
-                p, j = slot_code(code_ref, core, d, k, queries)
-                at = step * SLOTS + k
-                mask = jnp.where(spots[:, at : at + 1] == lane, 1.0, 0.0).astype(BF16)
+                p, j = slot_code(scalar_ref, d, k, query_len, queries)
+                mask = jnp.where(spots[k][:, step : step + 1] == lane, 1.0, 0.0).astype(BF16)
                 token = jnp.dot(mask, emb_ref[p], preferred_element_type=F32)
                 token_ref[d, k] = token.astype(BF16)
                 start = pl.multiple_of(j * query_len, query_len)
                 query = recv_ref[d, pl.ds(start, query_len), :].astype(F32)
-                acc_ref[d, k : k + 1, :] = jnp.sum(token * query, axis=0, keepdims=True)
+                acc_ref[k, pl.ds(d, 1), :] = jnp.sum(token * query, axis=0, keepdims=True)
         return carry
 
     lax.fori_loop(0, chips // GROUP, one_group, 0)
-    meta = meta_ref[...]
-    exps = jnp.exp(jnp.sum(acc_ref[...], axis=-1, keepdims=True)) * meta[:, :, VALID : VALID + 1]
-    exp_ref[...] = jnp.broadcast_to(exps, exp_ref.shape)
-    which = meta[:, :, WHICH : WHICH + 1]
-    place = places(core, other, (chips, 1, emb_dim), queries)
-    total = jnp.zeros(place.shape, F32)
+    shape = (chips, emb_dim)
+    at = iota(shape, 1)
+    scores = jnp.zeros(shape, F32)
+    for k in range(capacity):
+        scores = jnp.where(at == k, jnp.sum(acc_ref[k], axis=-1, keepdims=True), scores)
+    exps = jnp.where(at < capacity, jnp.exp(scores) * field(extra, query_len, VALID), 0.0)
+    exp_ref[...] = exps
+    which = field(extra, query_len, WHICH)
+    place = places(core, other, shape, queries)
+    total = jnp.zeros(shape, F32)
     for q in range(queries):
         share = jnp.sum(jnp.where(which == float(q), exps, 0.0), axis=1, keepdims=True)
-        total = total + jnp.where(place == q, share, 0.0)
+        total = jnp.where(place == q, share, total)
     total = jnp.sum(total, axis=0, keepdims=True)
     if other:
-        total = total + so_far_ref[...]
-    part_ref[...] = jnp.broadcast_to(total, part_ref.shape)
-
-
-def weight_kernel(capacity, block, neg, other, core_ref, parts_ref, meta_ref, exp_ref, token_ref, out_ref, weight_ref):
+        total = total + so_far_ref[0]
+    part_ref[...] = jnp.broadcast_to(total[None], part_ref.shape)
+
+
+def weight_kernel(capacity, block, neg, other, core_ref, parts_ref, extra_ref, exp_ref, token_ref, out_ref, weight_ref, scale_ref):
     queries, query_len = block
-    chips, _, emb_dim = exp_ref.shape
-    meta = meta_ref[...]
+    chips, emb_dim = exp_ref.shape
     exps = exp_ref[...]
-    place = places(core_ref[0], other, (chips, 1, emb_dim), queries)
-    sums = jnp.sum(parts_ref[...], axis=0, keepdims=True)
-    which = meta[:, :, WHICH : WHICH + 1]
+    extra = extra_ref[...]
+    place = places(core_ref[0], other, exps.shape, queries)
+    sums = jnp.sum(parts_ref[...], axis=0)
+    which = field(extra, query_len, WHICH)
     share = jnp.zeros_like(exps)
     for q in range(queries):
         norm = jnp.sum(jnp.where(place == q, sums, 0.0), axis=-1, keepdims=True)
-        share = share + jnp.where(which == float(q), exps / norm, 0.0)
-    target = meta[:, :, HIGH : HIGH + 1] + meta[:, :, MID : MID + 1]
-    target = target + meta[:, :, LOW : LOW + 1]
-    weight_ref[...] = neg * (share - target) * meta[:, :, VALID : VALID + 1]
+        share = jnp.where(which == float(q), exps / norm, share)
+    target = field(extra, query_len, HIGH) + field(extra, query_len, MID)
+    target = target + field(extra, query_len, LOW)
+    weights = neg * (share - target) * field(extra, query_len, VALID)
+    weights = jnp.where(iota(exps.shape, 1) < capacity, weights, 0.0)
+    for k in range(capacity):
+        weight_ref[k] = jnp.broadcast_to(weights[:, k : k + 1], exps.shape)
+    for q in range(queries):
+        scale = jnp.where(which == float(q), weights, 0.0)
+        for k in range(capacity):
+            scale_ref[q * capacity + k] = jnp.broadcast_to(scale[:, k : k + 1], exps.shape)
 
     def one_device(d, carry):
-        chosen = meta_ref[d][:, WHICH : WHICH + 1]
-        weights = weight_ref[d]
+        tokens = [token_ref[d, k].astype(F32) for k in range(capacity)]
         for q in range(queries):
-            scale = jnp.where(chosen == float(q), weights, 0.0)
-            grad = jnp.zeros((query_len, emb_dim), F32)
-            for k in range(capacity):
-                grad = grad + scale[k : k + 1, :] * token_ref[d, k].astype(F32)
+            grad = scale_ref[q * capacity, pl.ds(d, 1), :] * tokens[0]
+            for k in range(1, capacity):
+                grad = grad + scale_ref[q * capacity + k, pl.ds(d, 1), :] * tokens[k]
             out_ref[d, q * query_len : (q + 1) * query_len, :] = grad.astype(BF16)
         return carry
 
-    lax.fori_loop(0, chips, one_device, 0, unroll=4)
+    lax.fori_loop(0, chips, one_device, 0, unroll=8)
+
+
+def add_kernel(left_ref, right_ref, out_ref):
+    out_ref[...] = (left_ref[...].astype(F32) + right_ref[...].astype(F32)).astype(BF16)
 
 
 def passage_kernel(capacity, block, core_ref, hidden_ref, proj_ref, *refs):
-    halves = [refs[4 * h : 4 * h + 4] for h in range(CORES)]
-    grad_ref, term_ref, table_ref, total_ref = refs[4 * CORES :]
+    halves = [refs[5 * h : 5 * h + 5] for h in range(CORES)]
+    grad_ref, term_ref, table_ref, total_ref = refs[5 * CORES :]
     passes, pass_len, _ = hidden_ref.shape
     queries, query_len = block
     rows = queries * query_len
-    core = core_ref[0]
     lane = iota((query_len, WIDE), 1).astype(F32)
     total_ref[...] = jnp.zeros_like(total_ref)
-    for code_ref, recv_ref, meta_ref, weight_ref in halves:
+    for code_ref, recv_ref, spots_ref, extra_ref, weight_ref in halves:
         chips, _, emb_dim = recv_ref.shape
 
         def one_group(group, carry):
-            spots = picked(meta_ref, group, query_len)
+            spots = picked(spots_ref, extra_ref, group, query_len, capacity)
             table_ref[...] = jnp.zeros_like(table_ref)
             for step in range(GROUP):
                 d = group * GROUP + step
                 for k in range(capacity):
-                    p, j = slot_code(code_ref, core, d, k, queries)
-                    at = step * SLOTS + k
+                    p, j = slot_code(code_ref, d, k, query_len, queries)
                     start = pl.multiple_of(step * rows + j * query_len, query_len)
-                    weight = weight_ref[d, k : k + 1, :]
+                    weight = weight_ref[k, pl.ds(d, 1), :]
                     weight = jnp.concatenate([weight] * (WIDE // emb_dim), axis=1)
-                    added = jnp.where(spots[:, at : at + 1] == lane, weight, 0.0).astype(BF16)
+                    added = jnp.where(spots[k][:, step : step + 1] == lane, weight, 0.0).astype(BF16)
                     table_ref[p, pl.ds(start, query_len), :] = (
                         table_ref[p, pl.ds(start, query_len), :] + added
                     )
@@ -275,7 +308,7 @@
     send = call(
         lambda *refs: request_kernel(reps, pass_count, *refs),
         shape((chips, rows + META_ROWS, emb_dim), BF16),
-        [],
+        [pltpu.VMEM((chips, META_ROWS, emb_dim), F32)],
         (),
         query_flat,
         projection,
@@ -284,7 +317,6 @@
         teacher,
     )
     near = swap(send, ("x", "z"))
-    far = to_other_core(near)
     emb = call(
         embed_kernel,
         shape((pass_count, WIDE, emb_dim), BF16),
@@ -293,41 +325,48 @@
         passage_hidden,
         projection,
     )
-    slot_shape = (chips, SLOTS, emb_dim)
+    near, emb = lax.optimization_barrier((near, emb))
+    far = to_other_core(near)
+    slot_shape = (chips, emb_dim)
     halves = []
     so_far = []
     for other, recv in ((False, near), (True, far)):
-        codes = recv[:, rows:, CODE].astype(jnp.int32)
-        meta, tokens, exps, part = call(
+        spots, extra, codes, tokens, exps, part = call(
             lambda *refs: token_kernel(capacity, block, other, *refs),
             (
                 shape(slot_shape, F32),
+                shape(slot_shape, F32),
+                shape(slot_shape, jnp.int32),
                 shape((chips, capacity, query_len, emb_dim), BF16),
                 shape(slot_shape, F32),
                 shape((owners if other else 1, 1, emb_dim), F32),
             ),
-            [pltpu.VMEM(slot_shape, F32)],
-            (0, 1),
+            [
+                pltpu.VMEM((chips, META_ROWS, emb_dim), F32),
+                pltpu.VMEM((capacity,) + slot_shape, F32),
+                pltpu.SMEM(slot_shape, jnp.int32),
+                pltpu.SemaphoreType.DMA,
+            ],
+            (0,),
             core,
-            codes,
             recv,
             emb,
             *so_far,
         )
         so_far = [part]
-        halves.append((codes, recv, meta, exps, tokens))
+        halves.append((codes, recv, spots, extra, exps, tokens))
     parts = swap(part, ("x", "z", "core"))
 
     def weigh(other):
-        codes, recv, meta, exps, tokens = halves[other]
+        _, _, _, extra, exps, tokens = halves[other]
         return call(
             lambda *refs: weight_kernel(capacity, block, neg_count, other, *refs),
-            (shape((chips, rows, emb_dim), BF16), shape(slot_shape, F32)),
-            [],
+            (shape((chips, rows, emb_dim), BF16), shape((capacity,) + slot_shape, F32)),
+            [pltpu.VMEM((query_count * capacity,) + slot_shape, F32)],
             (0,),
             core,
             parts,
-            meta,
+            extra,
             exps,
             tokens,
         )
@@ -335,12 +374,12 @@
     far_part, far_weight = weigh(True)
     far_part = to_other_core(far_part)
     near_part, near_weight = weigh(False)
-    query_parts = (near_part.astype(F32) + far_part.astype(F32)).astype(BF16)
+    query_parts = call(add_kernel, shape(near_part.shape, BF16), [], (), near_part, far_part)
     query_parts, near_weight = lax.optimization_barrier((query_parts, near_weight))
     query_parts = swap(query_parts, ("x", "z"))
     passage_args = []
-    for (codes, recv, meta, _, _), weight in zip(halves, (near_weight, far_weight)):
-        passage_args += [codes, recv, meta, weight]
+    for (codes, recv, spots, extra, _, _), weight in zip(halves, (near_weight, far_weight)):
+        passage_args += [codes, recv, spots, extra, weight]
     grad_passages, term = call(
         lambda *refs: passage_kernel(capacity, block, *refs),
         (
@@ -351,7 +390,7 @@
             pltpu.VMEM((pass_count, GROUP * rows, WIDE), BF16),
             pltpu.VMEM((pass_count, emb_dim, WIDE), F32),
         ],
-        (0, 3, 7),
+        (0, 3, 8),
         core,
         passage_hidden,
         projection,

time: 143 us -> 137 us (0.958)
  blocking collectives: 68.6 us -> 41.6 us
  starting transfers between devices: 15.4 us -> 26.4 us
  waiting for transfers between devices: 10.6 us -> 19.2 us
  other arithmetic: 3.09 us -> 0.84 us
  Pallas kernels: 37.9 us -> 39.9 us
  local copies, waits for them, and re-layouts: 5.83 us -> 7.35 us
    all_to_all x4 -> x3, blocking collectives: 68.6 us -> 41.6 us  [swap(): return lax.all_to_all(array, axes, split_axis=0, concat_axis=0, tiled=True)]
    all_to_all x2 -> x3, starting transfers between devices: 9.57 us -> 21.4 us  [swap(): return lax.all_to_all(array, axes, split_axis=0, concat_axis=0, tiled=True)]
    all_to_all x2 -> x3, waiting for transfers between devices: 10.6 us -> 19.1 us  [swap(): return lax.all_to_all(array, axes, split_axis=0, concat_axis=0, tiled=True)]
    unnamed x12, local copies, waits for them, and re-layouts: 3.4 us -> 6.64 us
    convert_element_type x3 -> x0, other arithmetic: 2.25 us -> none  [the longest x1 2.03 us: per_device(): query_parts = (near_part.astype(F32) + far_part.astype(F32)).astype(BF16)]
    pallas_call x8 -> x9, Pallas kernels: 37.9 us -> 39.9 us  [call(): pl.pallas_call(kernel, out_shape=outs, in_specs=[SMEM if n in scalars els...]
    convert_element_type x2 -> x0, local copies, waits for them, and re-layouts: 1.71 us -> none  [per_device(): codes = recv[:, rows:, CODE].astype(jnp.int32)]
  transfers between devices with their start and end apart: 4 -> 5, of which waited for: 2 -> 3; matrix products, arithmetic and copies ran while one was open for 3% -> 3% of each run, Pallas kernels for 17% -> 18%
where the time goes in v4:
time: 137 us; the launch traced here: 136 us
  blocking collectives  41.6 us (30%)
  Pallas kernels  39.9 us (29%)
  starting transfers between devices  26.4 us (19%)
  waiting for transfers between devices  19.2 us (14%)
  local copies, waits for them, and re-layouts  7.35 us (5%)
    all_to_all x3, blocking collectives, swap(): return lax.all_to_all(array, axes, split_axis=0, concat_axis=0, tiled=True)  41.6 us
    pallas_call x9, Pallas kernels, call(): pl.pallas_call(kernel, out_shape=outs, in_specs=[SMEM if n in scalars els...  39.9 us
    all_to_all x3, starting transfers between devices, swap(): return lax.all_to_all(array, axes, split_axis=0, concat_axis=0, tiled=True)  21.4 us
    all_to_all x3, waiting for transfers between devices, swap(): return lax.all_to_all(array, axes, split_axis=0, concat_axis=0, tiled=True)  19.1 us
    unnamed x12, local copies, waits for them, and re-layouts  6.64 us
    ppermute x2, starting transfers between devices, to_other_core(): lax.ppermute(array, 'core', [(c, CORES - 1 - c) for c in range(CORES)])  4.94 us
  transfers between devices with their start and end apart: 5, of which 3 were waited for; matrix products, arithmetic and copies ran while one was open for 3% of the time, Pallas kernels for 18%

profile of v4, /device:TPU:1, one launch (start us, length us, event | category | flops | bytes accessed | tf_op | source)
XLA Modules:
  0.0 135.9 jit_solution(14015448082380315568)
XLA Ops:
  0.6 2.3 %shard_map.77 = bf16[32,72,128]{2,1,0:T(8,128)(2,1)} custom-call(bf16[64,768]{1,0:T(8,128)(2,1)} %bitcast.6, bf16[768,128]{1,0:T(8,128)(2,1)} %proj_ref.3, s32[2,128]{1,0:T(2,128)} %refs_2_.2, s32[2,32,128]{2,1,0:T(8,128)} %bitcast.8, f32[2,128]{1,0:T(2,128)} %refs_4_.1), custom_call_target="tpu_custom_call" | custom-call | tf_op jit(solution)/shard_map/pallas_call | solution.py:298
  3.0 11.9 %all-to-all-start = ((bf16[32,72,128]{2,1,0:T(8,128)(2,1)}), bf16[32,72,128]{2,1,0:T(8,128)(2,1)S(1)}, u32[]{:S(2)}, u32[]{:S(2)}) async-start(bf16[32,72,128]{2,1,0:T(8,128)(2,1)} %shard_map.77), calls=%async_computation | async-start | bytes 1179648 | tf_op jit(solution)/shard_map/all_to_all | solution.py:275
  14.8 3.4 %copy.12.hidden_ref.refs_1_ = bf16[8,180,768]{2,1,0:T(8,128)(2,1)} copy(bf16[8,180,768]{2,0,1:T(8,128)(2,1)} %param.7) | data formatting | bytes 4423680 | tf_op args[1]
  18.3 3.4 %shard_map.78.refs_2_ = bf16[8,256,128]{2,1,0:T(8,128)(2,1)} custom-call(bf16[8,180,768]{2,1,0:T(8,128)(2,1)} %copy.12.hidden_ref.refs_1_, bf16[768,128]{1,0:T(8,128)(2,1)} %proj_ref.3), custom_call_target="tpu_custom_call" | custom-call | tf_op jit(solution)/shard_map/pallas_call | solution.py:298
  21.7 8.4 %all-to-all-done.refs_1_.refs_4_ = bf16[32,72,128]{2,1,0:T(8,128)(2,1)S(1)} async-done(((bf16[32,72,128]{2,1,0:T(8,128)(2,1)}), bf16[32,72,128]{2,1,0:T(8,128)(2,1)S(1)}, u32[]{:S(2)}, u32[]{:S(2)}) %all-to-all-start) | async-done | bytes 589856 | tf_op jit(solution)/shard_map/all_to_all | solution.py:275
  30.1 4.1 %collective-permute-start = (bf16[32,72,128]{2,1,0:T(8,128)(2,1)S(1)}, bf16[32,72,128]{2,1,0:T(8,128)(2,1)S(1)}, u32[]{:S(2)}, u32[]{:S(2)}) collective-permute-start(bf16[32,72,128]{2,1,0:T(8,128)(2,1)S(1)} %all-to-all-done.refs_1_.refs_4_), channel_id=1, source_target_pairs={{0,4},{4,0},{1,5},{5,1},{2,6},{6,2},{3,7},{7,3},{8,12},{12,8},{9,1... | collective-permute-start | bytes 1769480 | tf_op jit(solution)/shard_map/ppermute | solution.py:279
  34.3 5.3 %shard_map.79 = (f32[32,128]{1,0:T(8,128)}, f32[32,128]{1,0:T(8,128)}, s32[32,128]{1,0:T(8,128)}, bf16[32,5,32,128]{3,2,1,0:T(8,128)(2,1)}, f32[32,128]{1,0:T(8,128)}, /*index=5*/f32[1,1,128]{2,1,0:T(1,128)}) custom-call(s32[1]{0:T(128)} %bitcast.refs_0_, bf16[32,72,128]{2,1,0:T(8,128)(2,1)} %copy-done, bf16[8,256,128]{2,1,0:T(8,128)(2,1)} %shard_map.78.refs_2_), custom_call_target="tpu_custom_call" | custom-call | tf_op jit(solution)/shard_map/pallas_call | solution.py:298
  39.6 0.8 copy-done.1
  40.4 5.3 %shard_map.80 = (f32[32,128]{1,0:T(8,128)}, f32[32,128]{1,0:T(8,128)}, s32[32,128]{1,0:T(8,128)}, bf16[32,5,32,128]{3,2,1,0:T(8,128)(2,1)}, f32[32,128]{1,0:T(8,128)}, /*index=5*/f32[64,1,128]{2,1,0:T(1,128)}) custom-call(s32[1]{0:T(128)} %bitcast.refs_0_, bf16[32,72,128]{2,1,0:T(8,128)(2,1)} %copy-done.1, bf16[8,256,128]{2,1,0:T(8,128)(2,1)} %shard_map.78.refs_2_, ...), custom_call_target="tpu_custom_call" | custom-call | tf_op jit(solution)/shard_map/pallas_call | solution.py:298
  45.7 15.6 %all_to_all.30.refs_1_ = f32[64,1,128]{2,1,0:T(1,128)} all-to-all(f32[64,1,128]{2,1,0:T(1,128)} %get-tuple-element.30), channel_id=1, replica_groups=mesh['x'=4,'z'=8,'core'=2,'rep'=4] {'x','z','core'}, dimensions={0} | all-to-all | bytes 65536 | tf_op jit(solution)/shard_map/all_to_all | solution.py:275
  61.3 2.9 %shard_map.82 = (bf16[32,64,128]{2,1,0:T(8,128)(2,1)}, f32[5,32,128]{2,1,0:T(8,128)}) custom-call(s32[1]{0:T(128)} %bitcast.refs_0_, f32[64,1,128]{2,1,0:T(1,128)} %all_to_all.30.refs_1_, f32[32,128]{1,0:T(8,128)} %get-tuple-element.34.refs_2_.refs_11_, f32[32,128]{1,0:T(8,128)} %get-tuple-element.35.refs_3_, bf16[32,5,32,128]{3,2,1,0:T(8,128)(2,1)} %get-tuple-element.36.refs_4_), custom_call_target="tpu_custom_call" | custom-call | tf_op jit(solution)/shard_map/pallas_call | solution.py:298
  64.2 0.8 collective-permute-start.1
  65.0 2.9 %shard_map.81 = (bf16[32,64,128]{2,1,0:T(8,128)(2,1)}, f32[5,32,128]{2,1,0:T(8,128)}) custom-call(s32[1]{0:T(128)} %bitcast.refs_0_, f32[64,1,128]{2,1,0:T(1,128)} %all_to_all.30.refs_1_, f32[32,128]{1,0:T(8,128)} %get-tuple-element.28.refs_2_.refs_6_, f32[32,128]{1,0:T(8,128)} %get-tuple-element.31.refs_3_, bf16[32,5,32,128]{3,2,1,0:T(8,128)(2,1)} %get-tuple-element.32.refs_4_), custom_call_target="tpu_custom_call" | custom-call | tf_op jit(solution)/shard_map/pallas_call | solution.py:298
  67.9 0.8 copy-done.3
  68.7 2.1 %shard_map.83 = bf16[32,64,128]{2,1,0:T(8,128)(2,1)} custom-call(bf16[32,64,128]{2,1,0:T(8,128)(2,1)} %get-tuple-element.33.left_ref, bf16[32,64,128]{2,1,0:T(8,128)(2,1)} %copy-done.3), custom_call_target="tpu_custom_call" | custom-call | tf_op jit(solution)/shard_map/pallas_call | solution.py:298
  70.8 4.1 %all-to-all-start.2 = ((bf16[32,64,128]{2,1,0:T(8,128)(2,1)}), bf16[32,64,128]{2,1,0:T(8,128)(2,1)S(1)}, u32[]{:S(2)}, u32[]{:S(2)}) async-start(bf16[32,64,128]{2,1,0:T(8,128)(2,1)} %shard_map.83), calls=%async_computation.2 | async-start | bytes 1048576 | tf_op jit(solution)/shard_map/all_to_all | solution.py:275
  74.9 13.0 %shard_map.84 = (bf16[8,180,128]{2,1,0:T(8,128)(2,1)}, f32[128,768]{1,0:T(8,128)}) custom-call(s32[1]{0:T(128)} %bitcast.refs_0_, bf16[8,180,768]{2,1,0:T(8,128)(2,1)} %copy.12.hidden_ref.refs_1_, bf16[768,128]{1,0:T(8,128)(2,1)} %proj_ref.3, s32[32,128]{1,0:T(8,128)} %get-tuple-element.26.refs_3_, bf16[32,72,128]{2,1,0:T(8,128)(2,1)} %copy-done, ...), custom_call_target="tpu_custom_call" | custom-call | tf_op jit(solution)/shard_map/pallas_call | solution.py:298
  87.9 3.2 %all-to-all-done.2.parts_ref = bf16[32,64,128]{2,1,0:T(8,128)(2,1)S(1)} async-done(((bf16[32,64,128]{2,1,0:T(8,128)(2,1)}), bf16[32,64,128]{2,1,0:T(8,128)(2,1)S(1)}, u32[]{:S(2)}, u32[]{:S(2)}) %all-to-all-start.2) | async-done | bytes 524320 | tf_op jit(solution)/shard_map/all_to_all | solution.py:275
  91.2 0.8 copy-done.2
  92.0 2.6 %shard_map.85 = bf16[32,24,128]{2,1,0:T(8,128)(2,1)} custom-call(bf16[32,64,128]{2,1,0:T(8,128)(2,1)} %copy-done.2, bf16[64,768]{1,0:T(8,128)(2,1)} %bitcast.7, bf16[768,128]{1,0:T(8,128)(2,1)} %proj_ref.3, f32[128,768]{1,0:T(8,128)} %get-tuple-element.45.term_ref), custom_call_target="tpu_custom_call" | custom-call | tf_op jit(solution)/shard_map/pallas_call | solution.py:298
  94.6 15.1 %all_to_all.31 = bf16[32,24,128]{2,1,0:T(8,128)(2,1)S(1)} all-to-all(bf16[32,24,128]{2,1,0:T(8,128)(2,1)} %shard_map.85), channel_id=1, replica_groups=mesh['x'=4,'z'=8,'core'=2,'rep'=4] {'x','core','rep'}, dimensions={0} | all-to-all | bytes 393216 | tf_op jit(solution)/shard_map/all_to_all | solution.py:275
  109.7 10.9 %all_to_all.32 = bf16[8,24,128]{2,1,0:T(8,128)(2,1)S(1)} all-to-all(bf16[8,24,128]{2,1,0:T(8,128)(2,1)S(1)} %broadcast_in_dim.4), channel_id=1, replica_groups=mesh['x'=4,'z'=8,'core'=2,'rep'=4] {'z'}, dimensions={0} | all-to-all | bytes 98304 | tf_op jit(solution)/shard_map/all_to_all | solution.py:275
  121.4 5.5 %all-to-all-start.5 = ((bf16[32,24,128]{2,1,0:T(8,128)(2,1)}), bf16[32,24,128]{2,1,0:T(8,128)(2,1)S(1)}, u32[]{:S(2)}, u32[]{:S(2)}) async-start(bf16[32,24,128]{2,1,0:T(8,128)(2,1)} %broadcast_in_dim.5), calls=%async_computation.5 | async-start | bytes 393216 | tf_op jit(solution)/shard_map/all_to_all | solution.py:275
  127.7 7.5 %all-to-all-done.5 = bf16[32,24,128]{2,1,0:T(8,128)(2,1)S(1)} async-done(((bf16[32,24,128]{2,1,0:T(8,128)(2,1)}), bf16[32,24,128]{2,1,0:T(8,128)(2,1)S(1)}, u32[]{:S(2)}, u32[]{:S(2)}) %all-to-all-start.5) | async-done | bytes 196640 | tf_op jit(solution)/shard_map/all_to_all | solution.py:275
  (16 shorter events, 2.4 us)
Async XLA Ops:
  3.0 27.2 %all-to-all-start = ((bf16[32,72,128]{2,1,0:T(8,128)(2,1)}), bf16[32,72,128]{2,1,0:T(8,128)(2,1)S(1)}, u32[]{:S(2)}, u32[]{:S(2)}) async-start(bf16[32,72,128]{2,1,0:T(8,128)(2,1)} %shard_map.77), calls=%async_computation | async-start | bytes 1179648 | tf_op jit(solution)/shard_map/all_to_all | solution.py:275
  30.1 4.1 %copy-start = (bf16[32,72,128]{2,1,0:T(8,128)(2,1)}, bf16[32,72,128]{2,1,0:T(8,128)(2,1)S(1)}, u32[]{:S(2)}) copy-start(bf16[32,72,128]{2,1,0:T(8,128)(2,1)S(1)} %all-to-all-done.refs_1_.refs_4_) | copy-start | bytes 1769476
  30.1 9.4 %collective-permute-start = (bf16[32,72,128]{2,1,0:T(8,128)(2,1)S(1)}, bf16[32,72,128]{2,1,0:T(8,128)(2,1)S(1)}, u32[]{:S(2)}, u32[]{:S(2)}) collective-permute-start(bf16[32,72,128]{2,1,0:T(8,128)(2,1)S(1)} %all-to-all-done.refs_1_.refs_4_), channel_id=1, source_target_pairs={{0,4},{4,0},{1,5},{5,1},{2,6},{6,2},{3,7},{7,3},{8,12},{12,8},{9,1... | collective-permute-start | bytes 1769480 | tf_op jit(solution)/shard_map/ppermute | solution.py:279
  39.5 0.8 copy-start.1
  64.2 3.7 %collective-permute-start.1 = (bf16[32,64,128]{2,1,0:T(8,128)(2,1)}, bf16[32,64,128]{2,1,0:T(8,128)(2,1)S(1)}, u32[]{:S(2)}, u32[]{:S(2)}) collective-permute-start(bf16[32,64,128]{2,1,0:T(8,128)(2,1)} %get-tuple-element.37), channel_id=1, source_target_pairs={{0,4},{4,0},{1,5},{5,1},{2,6},{6,2},{3,7},{7,3},{8,12},{12,8},{9,1... | collective-permute-start | bytes 1572872 | tf_op jit(solution)/shard_map/ppermute | solution.py:279
  67.9 0.8 copy-start.3
  70.8 20.3 %all-to-all-start.2 = ((bf16[32,64,128]{2,1,0:T(8,128)(2,1)}), bf16[32,64,128]{2,1,0:T(8,128)(2,1)S(1)}, u32[]{:S(2)}, u32[]{:S(2)}) async-start(bf16[32,64,128]{2,1,0:T(8,128)(2,1)} %shard_map.83), calls=%async_computation.2 | async-start | bytes 1048576 | tf_op jit(solution)/shard_map/all_to_all | solution.py:275
  87.9 38.9 %copy-start.4 = (bf16[8,180,128]{2,1,0:T(8,128)(2,1)S(1)}, bf16[8,180,128]{2,1,0:T(8,128)(2,1)}, u32[]{:S(2)}) copy-start(bf16[8,180,128]{2,1,0:T(8,128)(2,1)} %get-tuple-element.48) | copy-start | bytes 1105924
  91.2 0.8 copy-start.2
  121.4 13.8 %all-to-all-start.5 = ((bf16[32,24,128]{2,1,0:T(8,128)(2,1)}), bf16[32,24,128]{2,1,0:T(8,128)(2,1)S(1)}, u32[]{:S(2)}, u32[]{:S(2)}) async-start(bf16[32,24,128]{2,1,0:T(8,128)(2,1)} %broadcast_in_dim.5), calls=%async_computation.5 | async-start | bytes 393216 | tf_op jit(solution)/shard_map/all_to_all | solution.py:275

commit v5 on v4

--- a/solution.py
+++ b/solution.py
@@ -21,8 +21,8 @@
 SMEM = pl.BlockSpec(memory_space=pltpu.SMEM)
 
 
-def params():
-    return pltpu.CompilerParams(vmem_limit_bytes=56 * 1024 * 1024)
+def params(mb):
+    return pltpu.CompilerParams(vmem_limit_bytes=mb * 1024 * 1024)
 
 
 def unit_rows(raw):
@@ -91,13 +91,14 @@
     send_ref[:, emb.shape[0] :, :] = meta_ref[...].astype(BF16)
 
 
-def embed_kernel(hidden_ref, proj_ref, emb_ref, wide_ref):
+def embed_kernel(hidden_ref, proj_ref, emb_ref, unit_ref, inverse_ref):
     passes, pass_len, _ = hidden_ref.shape
-    wide_ref[...] = jnp.zeros_like(wide_ref)
+    unit_ref[...] = jnp.zeros_like(unit_ref)
     for p in range(passes):
-        unit, _ = unit_rows(jnp.dot(hidden_ref[p], proj_ref[...], preferred_element_type=F32))
-        wide_ref[:pass_len, :] = unit
-        emb_ref[p] = wide_ref[...].astype(BF16)
+        unit, length = unit_rows(jnp.dot(hidden_ref[p], proj_ref[...], preferred_element_type=F32))
+        unit_ref[p, :pass_len, :] = unit
+        inverse_ref[p, :pass_len, :] = jnp.broadcast_to(1.0 / length, unit.shape)
+        emb_ref[p] = unit_ref[p].astype(BF16)
 
 
 def field(extra, query_len, name):
@@ -112,30 +113,35 @@
     return [both[k * query_len : (k + 1) * query_len] for k in range(capacity)]
 
 
-def slot_code(code_ref, d, k, query_len, queries):
-    code = code_ref[d, query_len + k]
-    return lax.div(code, jnp.int32(queries)), lax.rem(code, jnp.int32(queries))
-
-
-def places(core, other, shape, queries):
-    source = (1 - core) if other else core
-    return iota(shape, 1) - queries * (source * shape[0] + iota(shape, 0))
-
-
-def token_kernel(capacity, block, other, core_ref, recv_ref, emb_ref, *refs):
-    if other:
-        so_far_ref, *refs = refs
-    spots_ref, extra_ref, code_ref, token_ref, exp_ref, part_ref, both_ref, acc_ref, scalar_ref, sem = refs
-    chips, _, emb_dim = recv_ref.shape
-    queries, query_len = block
-    rows = queries * query_len
-    core = core_ref[0]
+def unpack(core, recv_ref, rows, both_ref, spots_ref, extra_ref, code_ref, scalar_ref, sem):
     both_ref[...] = recv_ref[:, rows:, :].astype(F32)
     spots_ref[...] = jnp.where(core == 0, both_ref[:, 0, :], both_ref[:, PER_CORE, :])
     extra = jnp.where(core == 0, both_ref[:, 1, :], both_ref[:, PER_CORE + 1, :])
     extra_ref[...] = extra
     code_ref[...] = extra.astype(jnp.int32)
-    copy = pltpu.make_async_copy(code_ref, scalar_ref, sem)
+    return pltpu.make_async_copy(code_ref, scalar_ref, sem)
+
+
+def slot_code(code_ref, d, k, query_len, queries):
+    code = code_ref[d, query_len + k]
+    return lax.div(code, jnp.int32(queries)), lax.rem(code, jnp.int32(queries))
+
+
+def places(core, other, shape, queries):
+    source = (1 - core) if other else core
+    return iota(shape, 1) - queries * (source * shape[0] + iota(shape, 0))
+
+
+def token_kernel(capacity, block, other, core_ref, recv_ref, emb_ref, *refs):
+    if other:
+        so_far_ref, *refs = refs
+    extra_ref, token_ref, exp_ref, part_ref, *refs = refs
+    both_ref, spots_ref, code_ref, acc_ref, scalar_ref, sem = refs
+    chips, _, emb_dim = recv_ref.shape
+    queries, query_len = block
+    rows = queries * query_len
+    core = core_ref[0]
+    copy = unpack(core, recv_ref, rows, both_ref, spots_ref, extra_ref, code_ref, scalar_ref, sem)
     copy.start()
     acc_ref[...] = jnp.zeros_like(acc_ref)
     copy.wait()
@@ -158,6 +164,7 @@
     lax.fori_loop(0, chips // GROUP, one_group, 0)
     shape = (chips, emb_dim)
     at = iota(shape, 1)
+    extra = extra_ref[...]
     scores = jnp.zeros(shape, F32)
     for k in range(capacity):
         scores = jnp.where(at == k, jnp.sum(acc_ref[k], axis=-1, keepdims=True), scores)
@@ -175,13 +182,8 @@
     part_ref[...] = jnp.broadcast_to(total[None], part_ref.shape)
 
 
-def weight_kernel(capacity, block, neg, other, core_ref, parts_ref, extra_ref, exp_ref, token_ref, out_ref, weight_ref, scale_ref):
-    queries, query_len = block
-    chips, emb_dim = exp_ref.shape
-    exps = exp_ref[...]
-    extra = extra_ref[...]
-    place = places(core_ref[0], other, exps.shape, queries)
-    sums = jnp.sum(parts_ref[...], axis=0)
+def slot_weights(capacity, queries, query_len, neg, core, other, sums, extra, exps):
+    place = places(core, other, exps.shape, queries)
     which = field(extra, query_len, WHICH)
     share = jnp.zeros_like(exps)
     for q in range(queries):
@@ -190,13 +192,22 @@
     target = field(extra, query_len, HIGH) + field(extra, query_len, MID)
     target = target + field(extra, query_len, LOW)
     weights = neg * (share - target) * field(extra, query_len, VALID)
-    weights = jnp.where(iota(exps.shape, 1) < capacity, weights, 0.0)
-    for k in range(capacity):
-        weight_ref[k] = jnp.broadcast_to(weights[:, k : k + 1], exps.shape)
+    return jnp.where(iota(exps.shape, 1) < capacity, weights, 0.0)
+
+
+def weight_kernel(capacity, block, neg, other, core_ref, parts_ref, extra_ref, exp_ref, token_ref, out_ref, scale_ref):
+    queries, query_len = block
+    chips, emb_dim = exp_ref.shape
+    extra = extra_ref[...]
+    sums = jnp.sum(parts_ref[...], axis=0)
+    weights = slot_weights(
+        capacity, queries, query_len, neg, core_ref[0], other, sums, extra, exp_ref[...]
+    )
+    which = field(extra, query_len, WHICH)
     for q in range(queries):
         scale = jnp.where(which == float(q), weights, 0.0)
         for k in range(capacity):
-            scale_ref[q * capacity + k] = jnp.broadcast_to(scale[:, k : k + 1], exps.shape)
+            scale_ref[q * capacity + k] = jnp.broadcast_to(scale[:, k : k + 1], scale.shape)
 
     def one_device(d, carry):
         tokens = [token_ref[d, k].astype(F32) for k in range(capacity)]
@@ -214,26 +225,61 @@
     out_ref[...] = (left_ref[...].astype(F32) + right_ref[...].astype(F32)).astype(BF16)
 
 
-def passage_kernel(capacity, block, core_ref, hidden_ref, proj_ref, *refs):
-    halves = [refs[5 * h : 5 * h + 5] for h in range(CORES)]
-    grad_ref, term_ref, table_ref, total_ref = refs[5 * CORES :]
+def passage_kernel(capacity, block, neg, core_ref, hidden_ref, unit_ref, inverse_ref, parts_ref, *refs):
+    halves = [refs[2 * h : 2 * h + 2] for h in range(CORES)]
+    grad_ref, term_ref, table_ref, total_ref, weight_ref, *refs = refs[2 * CORES :]
+    own_ref, unit_own_ref, inverse_own_ref, own_sem, *refs = refs
+    loads = []
+    for n, (source, target) in enumerate(
+        ((hidden_ref, own_ref), (unit_ref, unit_own_ref), (inverse_ref, inverse_own_ref))
+    ):
+        loads.append(pltpu.make_async_copy(source, target, own_sem.at[n]))
+        loads[n].start()
     passes, pass_len, _ = hidden_ref.shape
+    emb_dim = unit_ref.shape[2]
     queries, query_len = block
     rows = queries * query_len
     lane = iota((query_len, WIDE), 1).astype(F32)
+    copies = []
+    for half, (recv_ref, _) in enumerate(halves):
+        copy = unpack(core_ref[0], recv_ref, rows, *[ref.at[half] for ref in refs])
+        copy.start()
+        copies.append(copy)
+    _, spots_ref, extra_ref, _, scalar_ref, _ = refs
     total_ref[...] = jnp.zeros_like(total_ref)
-    for code_ref, recv_ref, spots_ref, extra_ref, weight_ref in halves:
-        chips, _, emb_dim = recv_ref.shape
+    table_ref[...] = jnp.zeros_like(table_ref)
+    sums = jnp.sum(parts_ref[...], axis=0)
+    for half, (recv_ref, exp_ref) in enumerate(halves):
+        weights = slot_weights(
+            capacity,
+            queries,
+            query_len,
+            neg,
+            core_ref[0],
+            half == 1,
+            sums,
+            extra_ref[half],
+            exp_ref[...],
+        )
+        for k in range(capacity):
+            weight_ref[half, k] = jnp.broadcast_to(weights[:, k : k + 1], weights.shape)
+    for half, (recv_ref, _) in enumerate(halves):
+        chips = recv_ref.shape[0]
+        copies[half].wait()
 
         def one_group(group, carry):
-            spots = picked(spots_ref, extra_ref, group, query_len, capacity)
+            spots = picked(spots_ref.at[half], extra_ref.at[half], group, query_len, capacity)
+
+            def place(step, k):
+                d = group * GROUP + step
+                p, j = slot_code(scalar_ref.at[half], d, k, query_len, queries)
+                return d, p, pl.multiple_of(step * rows + j * query_len, query_len)
+
             table_ref[...] = jnp.zeros_like(table_ref)
             for step in range(GROUP):
-                d = group * GROUP + step
                 for k in range(capacity):
-                    p, j = slot_code(code_ref, d, k, query_len, queries)
-                    start = pl.multiple_of(step * rows + j * query_len, query_len)
-                    weight = weight_ref[k, pl.ds(d, 1), :]
+                    d, p, start = place(step, k)
+                    weight = weight_ref[half, k, pl.ds(d, 1), :]
                     weight = jnp.concatenate([weight] * (WIDE // emb_dim), axis=1)
                     added = jnp.where(spots[k][:, step : step + 1] == lane, weight, 0.0).astype(BF16)
                     table_ref[p, pl.ds(start, query_len), :] = (
@@ -248,14 +294,17 @@
             return carry
 
         lax.fori_loop(0, chips // GROUP, one_group, 0)
+    for load in loads:
+        load.wait()
     term = jnp.zeros(term_ref.shape, F32)
     for p in range(passes):
-        unit, length = unit_rows(jnp.dot(hidden_ref[p], proj_ref[...], preferred_element_type=F32))
+        unit = unit_own_ref[p][:pass_len]
         grad = total_ref[p].T[:pass_len]
-        raw_grad = unit_back(grad, unit, length).astype(BF16)
+        grad = grad - unit * jnp.sum(unit * grad, axis=-1, keepdims=True)
+        raw_grad = (grad * inverse_own_ref[p][:pass_len]).astype(BF16)
         grad_ref[p] = raw_grad
         term = term + lax.dot_general(
-            raw_grad, hidden_ref[p], (((0,), (0,)), ((), ())), preferred_element_type=F32
+            raw_grad, own_ref[p], (((0,), (0,)), ((), ())), preferred_element_type=F32
         )
     term_ref[...] = term
 
@@ -265,9 +314,10 @@
     unit, length = unit_rows(jnp.dot(hidden, proj_ref[...], preferred_element_type=F32))
     grad = jnp.sum(parts_ref[...].astype(F32), axis=0)
     raw_grad = unit_back(grad, unit, length).astype(BF16)
-    term = term_ref[...] + lax.dot_general(
+    term = lax.dot_general(
         raw_grad, hidden, (((0,), (0,)), ((), ())), preferred_element_type=F32
     )
+    term = term + term_ref[...]
     out_ref[...] = term.T.reshape(out_ref.shape).astype(BF16)
 
 
@@ -294,118 +344,142 @@
     query_flat = query_hidden.reshape(rows, hidden_dim)
     core = lax.axis_index("core").reshape(1)
 
-    def call(kernel, outs, scratch, scalars, *args):
-        return pl.pallas_call(
+    def call(kernel, outs, scratch, *args, scalars=(), streamed=(), mb=16):
+        results = pl.pallas_call(
             kernel,
             out_shape=outs,
-            in_specs=[SMEM if n in scalars else VMEM for n in range(len(args))],
-            out_specs=jax.tree.map(lambda _: VMEM, outs),
+            in_specs=[
+                SMEM if n in scalars else pl.BlockSpec(memory_space=pl.ANY) if n in streamed else VMEM
+                for n in range(len(args))
+            ],
+            out_specs=[VMEM] * len(outs),
             scratch_shapes=scratch,
-            compiler_params=params(),
+            compiler_params=params(mb),
         )(*args)
+        return results[0] if len(outs) == 1 else results
 
     shape = jax.ShapeDtypeStruct
+    slot_shape = (chips, emb_dim)
+    meta_shape = (chips, META_ROWS, emb_dim)
+    recv_shape = (chips, rows + META_ROWS, emb_dim)
     send = call(
         lambda *refs: request_kernel(reps, pass_count, *refs),
-        shape((chips, rows + META_ROWS, emb_dim), BF16),
-        [pltpu.VMEM((chips, META_ROWS, emb_dim), F32)],
-        (),
+        [shape(recv_shape, BF16)],
+        [pltpu.VMEM(meta_shape, F32)],
         query_flat,
         projection,
         negatives,
         jnp.swapaxes(positions, 1, 2),
         teacher,
+        mb=56,
     )
     near = swap(send, ("x", "z"))
-    emb = call(
+    wide_shape = (pass_count, WIDE, emb_dim)
+    emb, unit, inverse = call(
         embed_kernel,
-        shape((pass_count, WIDE, emb_dim), BF16),
-        [pltpu.VMEM((WIDE, emb_dim), F32)],
-        (),
+        [shape(wide_shape, BF16), shape(wide_shape, F32), shape(wide_shape, F32)],
+        [],
         passage_hidden,
         projection,
     )
     near, emb = lax.optimization_barrier((near, emb))
     far = to_other_core(near)
-    slot_shape = (chips, emb_dim)
     halves = []
     so_far = []
     for other, recv in ((False, near), (True, far)):
-        spots, extra, codes, tokens, exps, part = call(
+        extra, tokens, exps, part = call(
             lambda *refs: token_kernel(capacity, block, other, *refs),
-            (
+            [
                 shape(slot_shape, F32),
-                shape(slot_shape, F32),
-                shape(slot_shape, jnp.int32),
                 shape((chips, capacity, query_len, emb_dim), BF16),
                 shape(slot_shape, F32),
                 shape((owners if other else 1, 1, emb_dim), F32),
-            ),
+            ],
             [
-                pltpu.VMEM((chips, META_ROWS, emb_dim), F32),
+                pltpu.VMEM(meta_shape, F32),
+                pltpu.VMEM(slot_shape, F32),
+                pltpu.VMEM(slot_shape, jnp.int32),
                 pltpu.VMEM((capacity,) + slot_shape, F32),
                 pltpu.SMEM(slot_shape, jnp.int32),
                 pltpu.SemaphoreType.DMA,
             ],
-            (0,),
             core,
             recv,
             emb,
             *so_far,
+            scalars=(0,),
         )
         so_far = [part]
-        halves.append((codes, recv, spots, extra, exps, tokens))
+        halves.append((recv, extra, exps, tokens))
     parts = swap(part, ("x", "z", "core"))
 
     def weigh(other):
-        _, _, _, extra, exps, tokens = halves[other]
+        _, extra, exps, tokens = halves[other]
         return call(
             lambda *refs: weight_kernel(capacity, block, neg_count, other, *refs),
-            (shape((chips, rows, emb_dim), BF16), shape((capacity,) + slot_shape, F32)),
-            [pltpu.VMEM((query_count * capacity,) + slot_shape, F32)],
-            (0,),
+            [shape((chips, rows, emb_dim), BF16)],
+            [
+                pltpu.VMEM((query_count * capacity,) + slot_shape, F32),
+            ],
             core,
             parts,
             extra,
             exps,
             tokens,
+            scalars=(0,),
         )
 
-    far_part, far_weight = weigh(True)
-    far_part = to_other_core(far_part)
-    near_part, near_weight = weigh(False)
-    query_parts = call(add_kernel, shape(near_part.shape, BF16), [], (), near_part, far_part)
-    query_parts, near_weight = lax.optimization_barrier((query_parts, near_weight))
+    far_part = to_other_core(weigh(True))
+    near_part = weigh(False)
+    query_parts = call(add_kernel, [shape(near_part.shape, BF16)], [], near_part, far_part)
+    query_parts, sums = lax.optimization_barrier((query_parts, parts))
     query_parts = swap(query_parts, ("x", "z"))
-    passage_args = []
-    for (codes, recv, spots, extra, _, _), weight in zip(halves, (near_weight, far_weight)):
-        passage_args += [codes, recv, spots, extra, weight]
     grad_passages, term = call(
-        lambda *refs: passage_kernel(capacity, block, *refs),
-        (
+        lambda *refs: passage_kernel(capacity, block, neg_count, *refs),
+        [
             shape((pass_count, pass_len, emb_dim), BF16),
             shape((emb_dim, hidden_dim), F32),
-        ),
+        ],
         [
             pltpu.VMEM((pass_count, GROUP * rows, WIDE), BF16),
             pltpu.VMEM((pass_count, emb_dim, WIDE), F32),
+        ]
+        + [
+            pltpu.VMEM((CORES, capacity) + slot_shape, F32),
+            pltpu.VMEM(passage_hidden.shape, BF16),
+            pltpu.VMEM(wide_shape, F32),
+            pltpu.VMEM(wide_shape, F32),
+            pltpu.SemaphoreType.DMA((3,)),
+            pltpu.VMEM((CORES,) + meta_shape, F32),
+            pltpu.VMEM((CORES,) + slot_shape, F32),
+            pltpu.VMEM((CORES,) + slot_shape, F32),
+            pltpu.VMEM((CORES,) + slot_shape, jnp.int32),
+            pltpu.SMEM((CORES,) + slot_shape, jnp.int32),
+            pltpu.SemaphoreType.DMA((CORES,)),
         ],
-        (0, 3, 8),
         core,
         passage_hidden,
-        projection,
-        *passage_args,
+        unit,
+        inverse,
+        sums,
+        halves[0][0],
+        halves[0][2],
+        halves[1][0],
+        halves[1][2],
+        scalars=(0,),
+        streamed=(1, 2, 3),
+        mb=56,
     )
     groups = lax.axis_size(("x", "core", "rep"))
     pieces = call(
         query_kernel,
-        shape((groups, hidden_dim // groups, emb_dim), BF16),
+        [shape((groups, hidden_dim // groups, emb_dim), BF16)],
         [],
-        (),
         query_parts,
         query_flat,
         projection,
         term,
+        mb=16,
     )
     pieces = swap(pieces, ("x", "core", "rep"))
     mine = jnp.sum(pieces.astype(F32), axis=0).astype(BF16)

time: 137 us -> 124 us (0.905)
  Pallas kernels: 39.9 us -> 23.3 us
  waiting for transfers between devices: 19.2 us -> 21.8 us
    pallas_call x9, Pallas kernels: 39.9 us -> 23.3 us  [call(): pl.pallas_call(kernel, out_shape=outs, in_specs=[SMEM if n in scalars els...]
    all_to_all x3, waiting for transfers between devices: 19.1 us -> 21 us  [swap(): return lax.all_to_all(array, axes, split_axis=0, concat_axis=0, tiled=True)]
    unnamed x12 -> x32, local copies, waits for them, and re-layouts: 6.64 us -> 7.73 us
  transfers between devices with their start and end apart: 5 -> 5, of which waited for: 3 -> 4; matrix products, arithmetic and copies ran while one was open for 3% -> 2% of each run, Pallas kernels for 18% -> 12%
where the time goes in v5:
time: 124 us
  blocking collectives  42.2 us (34%)
  starting transfers between devices  26.3 us (21%)
  Pallas kernels  23.3 us (19%)
  waiting for transfers between devices  21.8 us (18%)
  local copies, waits for them, and re-layouts  8.44 us (7%)
    all_to_all x3, blocking collectives, swap(): return lax.all_to_all(array, axes, split_axis=0, concat_axis=0, tiled=True)  42.2 us
    pallas_call x9, Pallas kernels, call(): pl.pallas_call(kernel, out_shape=outs, in_specs=[SMEM if n in scalars els...  23.3 us
    all_to_all x3, starting transfers between devices, swap(): return lax.all_to_all(array, axes, split_axis=0, concat_axis=0, tiled=True)  21.4 us
    all_to_all x3, waiting for transfers between devices, swap(): return lax.all_to_all(array, axes, split_axis=0, concat_axis=0, tiled=True)  21 us
    unnamed x32, local copies, waits for them, and re-layouts  7.73 us
    ppermute x2, starting transfers between devices, to_other_core(): lax.ppermute(array, 'core', [(c, CORES - 1 - c) for c in range(CORES)])  4.88 us
  transfers between devices with their start and end apart: 5, of which 4 were waited for; matrix products, arithmetic and copies ran while one was open for 2% of the time, Pallas kernels for 12%

profile of v5, /device:TPU:1, one launch (start us, length us, event | category | flops | bytes accessed | tf_op | source)
XLA Modules:
  0.0 123.7 jit_solution(6661899599790490615)
XLA Ops:
  0.6 2.4 %shard_map.78 = bf16[32,72,128]{2,1,0:T(8,128)(2,1)} custom-call(bf16[64,768]{1,0:T(8,128)(2,1)} %bitcast.6, bf16[768,128]{1,0:T(8,128)(2,1)} %proj_ref.3, s32[2,128]{1,0:T(2,128)} %refs_2_.1, s32[2,32,128]{2,1,0:T(8,128)} %bitcast.8, f32[2,128]{1,0:T(2,128)} %refs_4_.1), custom_call_target="tpu_custom_call" | custom-call | tf_op jit(solution)/shard_map/pallas_call | solution.py:348
  3.0 11.9 %all-to-all-start = ((bf16[32,72,128]{2,1,0:T(8,128)(2,1)}), bf16[32,72,128]{2,1,0:T(8,128)(2,1)S(1)}, u32[]{:S(2)}, u32[]{:S(2)}) async-start(bf16[32,72,128]{2,1,0:T(8,128)(2,1)} %shard_map.78), calls=%async_computation | async-start | bytes 1179648 | tf_op jit(solution)/shard_map/all_to_all | solution.py:325
  14.9 2.1 %copy.12.hidden_ref.refs_1_ = bf16[8,180,768]{2,1,0:T(8,128)(2,1)S(1)} copy(bf16[8,180,768]{2,0,1:T(8,128)(2,1)} %param.7) | data formatting | bytes 4423680 | tf_op args[1]
  17.0 0.9 shard_map.77
  17.9 0.8 copy-done.3
  18.7 1.0 copy-done.7
  19.7 1.0 copy-done.8
  20.6 9.5 %all-to-all-done.refs_1_.refs_5_ = bf16[32,72,128]{2,1,0:T(8,128)(2,1)S(1)} async-done(((bf16[32,72,128]{2,1,0:T(8,128)(2,1)}), bf16[32,72,128]{2,1,0:T(8,128)(2,1)S(1)}, u32[]{:S(2)}, u32[]{:S(2)}) %all-to-all-start) | async-done | bytes 589856 | tf_op jit(solution)/shard_map/all_to_all | solution.py:325
  30.1 4.1 %collective-permute-start = (bf16[32,72,128]{2,1,0:T(8,128)(2,1)S(1)}, bf16[32,72,128]{2,1,0:T(8,128)(2,1)S(1)}, u32[]{:S(2)}, u32[]{:S(2)}) collective-permute-start(bf16[32,72,128]{2,1,0:T(8,128)(2,1)S(1)} %all-to-all-done.refs_1_.refs_5_), channel_id=1, source_target_pairs={{0,4},{4,0},{1,5},{5,1},{2,6},{6,2},{3,7},{7,3},{8,12},{12,8},{9,1... | collective-permute-start | bytes 1769480 | tf_op jit(solution)/shard_map/ppermute | solution.py:329
  34.3 1.0 copy-done.4
  35.3 3.2 %shard_map.79 = (f32[32,128]{1,0:T(8,128)S(1)}, bf16[32,5,32,128]{3,2,1,0:T(8,128)(2,1)S(1)}, f32[32,128]{1,0:T(8,128)S(1)}, f32[1,1,128]{2,1,0:T(1,128)S(1)}) custom-call(s32[1]{0:T(128)} %bitcast.refs_0_, bf16[32,72,128]{2,1,0:T(8,128)(2,1)S(1)} %all-to-all-done.refs_1_.refs_5_, bf16[8,256,128]{2,1,0:T(8,128)(2,1)S(1)} %copy-done.4), custom_call_target="tpu_custom_call" | custom-call | tf_op jit(solution)/shard_map/pallas_call | solution.py:348
  38.5 3.2 %shard_map.80 = (f32[32,128]{1,0:T(8,128)S(1)}, bf16[32,5,32,128]{3,2,1,0:T(8,128)(2,1)S(1)}, f32[32,128]{1,0:T(8,128)S(1)}, f32[64,1,128]{2,1,0:T(1,128)S(1)}) custom-call(s32[1]{0:T(128)} %bitcast.refs_0_, bf16[32,72,128]{2,1,0:T(8,128)(2,1)S(1)} %collective-permute-done.refs_1_.refs_7_, bf16[8,256,128]{2,1,0:T(8,128)(2,1)S(1)} %copy-done.4, ...), custom_call_target="tpu_custom_call" | custom-call | tf_op jit(solution)/shard_map/pallas_call | solution.py:348
  41.7 14.9 %all_to_all.30.refs_1_.refs_4_ = f32[64,1,128]{2,1,0:T(1,128)S(1)} all-to-all(f32[64,1,128]{2,1,0:T(1,128)S(1)} %get-tuple-element.25), channel_id=1, replica_groups=mesh['x'=4,'z'=8,'core'=2,'rep'=4] {'x','z','core'}, dimensions={0} | all-to-all | bytes 65536 | tf_op jit(solution)/shard_map/all_to_all | solution.py:325
  59.6 0.9 shard_map.83
  60.5 4.1 %all-to-all-start.2 = ((bf16[32,64,128]{2,1,0:T(8,128)(2,1)}), bf16[32,64,128]{2,1,0:T(8,128)(2,1)S(1)}, u32[]{:S(2)}, u32[]{:S(2)}) async-start(bf16[32,64,128]{2,1,0:T(8,128)(2,1)} %shard_map.83), calls=%async_computation.2 | async-start | bytes 1048576 | tf_op jit(solution)/shard_map/all_to_all | solution.py:325
  64.6 10.7 %shard_map.84 = (bf16[8,180,128]{2,1,0:T(8,128)(2,1)}, f32[128,768]{1,0:T(8,128)}) custom-call(s32[1]{0:T(128)} %bitcast.refs_0_, bf16[8,180,768]{2,1,0:T(8,128)(2,1)} %copy-done, f32[8,256,128]{2,1,0:T(8,128)} %copy-done.7, f32[8,256,128]{2,1,0:T(8,128)} %copy-done.8, f32[64,1,128]{2,1,0:T(1,128)} %copy-done.9, bf16[32,72,128]{2,1,0:T(8,128)(2,1)} %copy-done.1, ...), custom_call_target="tpu_custom_call" | custom-call | tf_op jit(solution)/shard_map/pallas_call | solution.py:348
  75.4 4.0 %all-to-all-done.2.parts_ref = bf16[32,64,128]{2,1,0:T(8,128)(2,1)S(1)} async-done(((bf16[32,64,128]{2,1,0:T(8,128)(2,1)}), bf16[32,64,128]{2,1,0:T(8,128)(2,1)S(1)}, u32[]{:S(2)}, u32[]{:S(2)}) %all-to-all-start.2) | async-done | bytes 524320 | tf_op jit(solution)/shard_map/all_to_all | solution.py:325
  79.4 1.0 copy-done.10
  81.0 16.3 %all_to_all.31 = bf16[32,24,128]{2,1,0:T(8,128)(2,1)S(1)} all-to-all(bf16[32,24,128]{2,1,0:T(8,128)(2,1)S(1)} %shard_map.85), channel_id=1, replica_groups=mesh['x'=4,'z'=8,'core'=2,'rep'=4] {'x','core','rep'}, dimensions={0} | all-to-all | bytes 393216 | tf_op jit(solution)/shard_map/all_to_all | solution.py:325
  97.4 11.0 %all_to_all.32 = bf16[8,24,128]{2,1,0:T(8,128)(2,1)S(1)} all-to-all(bf16[8,24,128]{2,1,0:T(8,128)(2,1)S(1)} %broadcast_in_dim.4), channel_id=1, replica_groups=mesh['x'=4,'z'=8,'core'=2,'rep'=4] {'z'}, dimensions={0} | all-to-all | bytes 98304 | tf_op jit(solution)/shard_map/all_to_all | solution.py:325
  109.1 5.5 %all-to-all-start.5 = ((bf16[32,24,128]{2,1,0:T(8,128)(2,1)}), bf16[32,24,128]{2,1,0:T(8,128)(2,1)S(1)}, u32[]{:S(2)}, u32[]{:S(2)}) async-start(bf16[32,24,128]{2,1,0:T(8,128)(2,1)} %broadcast_in_dim.5), calls=%async_computation.5 | async-start | bytes 393216 | tf_op jit(solution)/shard_map/all_to_all | solution.py:325
  114.6 0.8 copy.13
  115.4 7.5 %all-to-all-done.5 = bf16[32,24,128]{2,1,0:T(8,128)(2,1)S(1)} async-done(((bf16[32,24,128]{2,1,0:T(8,128)(2,1)}), bf16[32,24,128]{2,1,0:T(8,128)(2,1)S(1)}, u32[]{:S(2)}, u32[]{:S(2)}) %all-to-all-start.5) | async-done | bytes 196640 | tf_op jit(solution)/shard_map/all_to_all | solution.py:325
  122.9 0.8 bitcast_convert_fusion
  (36 shorter events, 4.4 us)
Async XLA Ops:
  3.0 27.2 %all-to-all-start = ((bf16[32,72,128]{2,1,0:T(8,128)(2,1)}), bf16[32,72,128]{2,1,0:T(8,128)(2,1)S(1)}, u32[]{:S(2)}, u32[]{:S(2)}) async-start(bf16[32,72,128]{2,1,0:T(8,128)(2,1)} %shard_map.78), calls=%async_computation | async-start | bytes 1179648 | tf_op jit(solution)/shard_map/all_to_all | solution.py:325
  14.9 2.1 %copy-start.5 = (bf16[768,128]{1,0:T(8,128)(2,1)S(1)}, bf16[768,128]{1,0:T(8,128)(2,1)}, u32[]{:S(2)}) copy-start(bf16[768,128]{1,0:T(8,128)(2,1)} %proj_ref.3) | copy-start | bytes 589828
  17.0 24.7 %copy-start = (bf16[8,180,768]{2,1,0:T(8,128)(2,1)}, bf16[8,180,768]{2,1,0:T(8,128)(2,1)S(1)}, u32[]{:S(2)}) copy-start(bf16[8,180,768]{2,1,0:T(8,128)(2,1)S(1)} %copy.12.hidden_ref.refs_1_) | copy-start | bytes 6635524
  17.9 0.8 copy-start.3
  18.7 1.0 copy-start.7
  19.7 1.0 copy-start.8
  30.1 28.7 %copy-start.1 = (bf16[32,72,128]{2,1,0:T(8,128)(2,1)}, bf16[32,72,128]{2,1,0:T(8,128)(2,1)S(1)}, u32[]{:S(2)}) copy-start(bf16[32,72,128]{2,1,0:T(8,128)(2,1)S(1)} %all-to-all-done.refs_1_.refs_5_) | copy-start | bytes 1769476
  30.1 8.3 %collective-permute-start = (bf16[32,72,128]{2,1,0:T(8,128)(2,1)S(1)}, bf16[32,72,128]{2,1,0:T(8,128)(2,1)S(1)}, u32[]{:S(2)}, u32[]{:S(2)}) collective-permute-start(bf16[32,72,128]{2,1,0:T(8,128)(2,1)S(1)} %all-to-all-done.refs_1_.refs_5_), channel_id=1, source_target_pairs={{0,4},{4,0},{1,5},{5,1},{2,6},{6,2},{3,7},{7,3},{8,12},{12,8},{9,1... | collective-permute-start | bytes 1769480 | tf_op jit(solution)/shard_map/ppermute | solution.py:329
  34.3 1.0 copy-start.4
  38.5 20.3 %copy-start.12 = (f32[32,128]{1,0:T(8,128)}, f32[32,128]{1,0:T(8,128)S(1)}, u32[]{:S(2)}) copy-start(f32[32,128]{1,0:T(8,128)S(1)} %get-tuple-element.27.refs_3_.refs_6_) | copy-start | bytes 49156
  38.5 20.3 %copy-start.2 = (bf16[32,72,128]{2,1,0:T(8,128)(2,1)}, bf16[32,72,128]{2,1,0:T(8,128)(2,1)S(1)}, u32[]{:S(2)}) copy-start(bf16[32,72,128]{2,1,0:T(8,128)(2,1)S(1)} %collective-permute-done.refs_1_.refs_7_) | copy-start | bytes 1769476
  41.7 18.8 %copy-start.13 = (f32[32,128]{1,0:T(8,128)}, f32[32,128]{1,0:T(8,128)S(1)}, u32[]{:S(2)}) copy-start(f32[32,128]{1,0:T(8,128)S(1)} %get-tuple-element.30.refs_3_.refs_8_) | copy-start | bytes 49156
  56.6 3.9 %copy-start.9 = (f32[64,1,128]{2,1,0:T(1,128)}, f32[64,1,128]{2,1,0:T(1,128)S(1)}, u32[]{:S(2)}) copy-start(f32[64,1,128]{2,1,0:T(1,128)S(1)} %all_to_all.30.refs_1_.refs_4_) | copy-start | bytes 98308
  57.3 2.3 %collective-permute-start.1 = (bf16[32,64,128]{2,1,0:T(8,128)(2,1)S(1)}, bf16[32,64,128]{2,1,0:T(8,128)(2,1)S(1)}, u32[]{:S(2)}, u32[]{:S(2)}) collective-permute-start(bf16[32,64,128]{2,1,0:T(8,128)(2,1)S(1)} %shard_map.82), channel_id=1, source_target_pairs={{0,4},{4,0},{1,5},{5,1},{2,6},{6,2},{3,7},{7,3},{8,12},{12,8},{9,1... | collective-permute-start | bytes 1572872 | tf_op jit(solution)/shard_map/ppermute | solution.py:329
  60.5 18.8 %all-to-all-start.2 = ((bf16[32,64,128]{2,1,0:T(8,128)(2,1)}), bf16[32,64,128]{2,1,0:T(8,128)(2,1)S(1)}, u32[]{:S(2)}, u32[]{:S(2)}) async-start(bf16[32,64,128]{2,1,0:T(8,128)(2,1)} %shard_map.83), calls=%async_computation.2 | async-start | bytes 1048576 | tf_op jit(solution)/shard_map/all_to_all | solution.py:325
  64.6 14.7 %copy-start.6 = (bf16[768,128]{1,0:T(8,128)(2,1)S(1)}, bf16[768,128]{1,0:T(8,128)(2,1)}, u32[]{:S(2)}) copy-start(bf16[768,128]{1,0:T(8,128)(2,1)} %proj_ref.3) | copy-start | bytes 589828
  64.6 14.7 %copy-start.11 = (bf16[2,32,768]{2,1,0:T(8,128)(2,1)S(1)}, bf16[2,32,768]{2,1,0:T(8,128)(2,1)}, u32[]{:S(2)}) copy-start(bf16[2,32,768]{2,1,0:T(8,128)(2,1)} %param.6) | copy-start | bytes 294916
  79.4 1.0 copy-start.10
  80.4 34.3 %copy-start.14 = (bf16[8,180,128]{2,1,0:T(8,128)(2,1)S(1)}, bf16[8,180,128]{2,1,0:T(8,128)(2,1)}, u32[]{:S(2)}) copy-start(bf16[8,180,128]{2,1,0:T(8,128)(2,1)} %get-tuple-element.38) | copy-start | bytes 1105924
  109.1 13.8 %all-to-all-start.5 = ((bf16[32,24,128]{2,1,0:T(8,128)(2,1)}), bf16[32,24,128]{2,1,0:T(8,128)(2,1)S(1)}, u32[]{:S(2)}, u32[]{:S(2)}) async-start(bf16[32,24,128]{2,1,0:T(8,128)(2,1)} %broadcast_in_dim.5), calls=%async_computation.5 | async-start | bytes 393216 | tf_op jit(solution)/shard_map/all_to_all | solution.py:325

commit v6 on v5

--- a/solution.py
+++ b/solution.py
@@ -134,8 +134,14 @@
 
 def token_kernel(capacity, block, other, core_ref, recv_ref, emb_ref, *refs):
     if other:
-        so_far_ref, *refs = refs
+        so_far_ref, near_ref, *refs = refs
     extra_ref, token_ref, exp_ref, part_ref, *refs = refs
+    if other:
+        kept_ref, *refs, keep_sem = refs
+        keeps = []
+        for n, source in enumerate((near_ref, recv_ref)):
+            keeps.append(pltpu.make_async_copy(source, kept_ref.at[n], keep_sem.at[n]))
+            keeps[n].start()
     both_ref, spots_ref, code_ref, acc_ref, scalar_ref, sem = refs
     chips, _, emb_dim = recv_ref.shape
     queries, query_len = block
@@ -180,6 +186,9 @@
     if other:
         total = total + so_far_ref[0]
     part_ref[...] = jnp.broadcast_to(total[None], part_ref.shape)
+    if other:
+        for keep in keeps:
+            keep.wait()
 
 
 def slot_weights(capacity, queries, query_len, neg, core, other, sums, extra, exps):
@@ -226,9 +235,10 @@
 
 
 def passage_kernel(capacity, block, neg, core_ref, hidden_ref, unit_ref, inverse_ref, parts_ref, *refs):
-    halves = [refs[2 * h : 2 * h + 2] for h in range(CORES)]
-    grad_ref, term_ref, table_ref, total_ref, weight_ref, *refs = refs[2 * CORES :]
-    own_ref, unit_own_ref, inverse_own_ref, own_sem, *refs = refs
+    kept_ref, *refs = refs
+    halves = [(kept_ref.at[h], refs[h]) for h in range(CORES)]
+    grad_ref, term_ref, table_ref, total_ref, weight_ref, *refs = refs[CORES:]
+    order_ref, own_ref, unit_own_ref, inverse_own_ref, own_sem, *refs = refs
     loads = []
     for n, (source, target) in enumerate(
         ((hidden_ref, own_ref), (unit_ref, unit_own_ref), (inverse_ref, inverse_own_ref))
@@ -302,11 +312,16 @@
         grad = total_ref[p].T[:pass_len]
         grad = grad - unit * jnp.sum(unit * grad, axis=-1, keepdims=True)
         raw_grad = (grad * inverse_own_ref[p][:pass_len]).astype(BF16)
-        grad_ref[p] = raw_grad
+        order_ref[:, p, :] = raw_grad.astype(F32)
         term = term + lax.dot_general(
             raw_grad, own_ref[p], (((0,), (0,)), ((), ())), preferred_element_type=F32
         )
     term_ref[...] = term
+    grad_ref[...] = order_ref[...].astype(BF16)
+
+
+def copy_kernel(from_ref, to_ref):
+    to_ref[...] = from_ref[...]
 
 
 def query_kernel(parts_ref, query_ref, proj_ref, term_ref, out_ref):
@@ -387,14 +402,15 @@
     halves = []
     so_far = []
     for other, recv in ((False, near), (True, far)):
-        extra, tokens, exps, part = call(
+        extra, tokens, exps, part, *kept = call(
             lambda *refs: token_kernel(capacity, block, other, *refs),
             [
                 shape(slot_shape, F32),
                 shape((chips, capacity, query_len, emb_dim), BF16),
                 shape(slot_shape, F32),
                 shape((owners if other else 1, 1, emb_dim), F32),
-            ],
+            ]
+            + [shape((CORES,) + recv_shape, BF16)] * other,
             [
                 pltpu.VMEM(meta_shape, F32),
                 pltpu.VMEM(slot_shape, F32),
@@ -402,19 +418,20 @@
                 pltpu.VMEM((capacity,) + slot_shape, F32),
                 pltpu.SMEM(slot_shape, jnp.int32),
                 pltpu.SemaphoreType.DMA,
-            ],
+            ]
+            + [pltpu.SemaphoreType.DMA((CORES,))] * other,
             core,
             recv,
             emb,
             *so_far,
             scalars=(0,),
         )
-        so_far = [part]
-        halves.append((recv, extra, exps, tokens))
+        so_far = [part, near]
+        halves.append((extra, exps, tokens))
     parts = swap(part, ("x", "z", "core"))
 
     def weigh(other):
-        _, extra, exps, tokens = halves[other]
+        extra, exps, tokens = halves[other]
         return call(
             lambda *refs: weight_kernel(capacity, block, neg_count, other, *refs),
             [shape((chips, rows, emb_dim), BF16)],
@@ -437,7 +454,7 @@
     grad_passages, term = call(
         lambda *refs: passage_kernel(capacity, block, neg_count, *refs),
         [
-            shape((pass_count, pass_len, emb_dim), BF16),
+            shape((pass_len, pass_count, emb_dim), BF16),
             shape((emb_dim, hidden_dim), F32),
         ],
         [
@@ -446,6 +463,7 @@
         ]
         + [
             pltpu.VMEM((CORES, capacity) + slot_shape, F32),
+            pltpu.VMEM((pass_len, pass_count, emb_dim), F32),
             pltpu.VMEM(passage_hidden.shape, BF16),
             pltpu.VMEM(wide_shape, F32),
             pltpu.VMEM(wide_shape, F32),
@@ -462,14 +480,14 @@
         unit,
         inverse,
         sums,
-        halves[0][0],
-        halves[0][2],
-        halves[1][0],
-        halves[1][2],
+        kept[0],
+        halves[0][1],
+        halves[1][1],
         scalars=(0,),
         streamed=(1, 2, 3),
         mb=56,
     )
+    term = call(copy_kernel, [shape(term.shape, F32)], [], term, mb=8)
     groups = lax.axis_size(("x", "core", "rep"))
     pieces = call(
         query_kernel,
@@ -487,6 +505,7 @@
     scale = 1.0 / math.sqrt(owners * reps * (query_count * query_len + pass_count * pass_len))
     mine = (jnp.sum(copies.astype(F32), axis=0) * scale).astype(BF16)
     copies = swap(jnp.broadcast_to(mine[None], (groups,) + mine.shape), ("x", "core", "rep"))
+    grad_passages = jnp.swapaxes(grad_passages, 0, 1)
     return (grad_passages, copies.reshape(hidden_dim, emb_dim).astype(F32))
 
 

time: 124 us -> 122 us (0.984)
  blocking collectives: 42.2 us -> 55.6 us
  waiting for transfers between devices: 21.8 us -> 13.8 us
  starting transfers between devices: 26.3 us -> 20.8 us
  local copies, waits for them, and re-layouts: 8.44 us -> 5.15 us
  Pallas kernels: 23.3 us -> 24.9 us
    all_to_all x3 -> x4, blocking collectives: 42.2 us -> 55.6 us  [swap(): return lax.all_to_all(array, axes, split_axis=0, concat_axis=0, tiled=True)]
    all_to_all x3 -> x2, waiting for transfers between devices: 21 us -> 13 us  [swap(): return lax.all_to_all(array, axes, split_axis=0, concat_axis=0, tiled=True)]
    all_to_all x3 -> x2, starting transfers between devices: 21.4 us -> 15.9 us  [swap(): return lax.all_to_all(array, axes, split_axis=0, concat_axis=0, tiled=True)]
    unnamed x32 -> x23, local copies, waits for them, and re-layouts: 7.73 us -> 5.11 us
    pallas_call x9 -> x10, Pallas kernels: 23.3 us -> 24.9 us  [call(): pl.pallas_call(kernel, out_shape=outs, in_specs=[SMEM if n in scalars els...]
  transfers between devices with their start and end apart: 5 -> 4, of which waited for: 4 -> 3; matrix products, arithmetic and copies ran while one was open for 2% -> 2% of each run, Pallas kernels for 12% -> 13%
where the time goes in v6:
time: 122 us
  blocking collectives  55.6 us (46%)
  Pallas kernels  24.9 us (20%)
  starting transfers between devices  20.8 us (17%)
  waiting for transfers between devices  13.8 us (11%)
  local copies, waits for them, and re-layouts  5.15 us (4%)
    all_to_all x4, blocking collectives, swap(): return lax.all_to_all(array, axes, split_axis=0, concat_axis=0, tiled=True)  55.6 us
    pallas_call x10, Pallas kernels, call(): pl.pallas_call(kernel, out_shape=outs, in_specs=[SMEM if n in scalars els...  24.9 us
    all_to_all x2, starting transfers between devices, swap(): return lax.all_to_all(array, axes, split_axis=0, concat_axis=0, tiled=True)  15.9 us
    all_to_all x2, waiting for transfers between devices, swap(): return lax.all_to_all(array, axes, split_axis=0, concat_axis=0, tiled=True)  13 us
    unnamed x23, local copies, waits for them, and re-layouts  5.11 us
    ppermute x2, starting transfers between devices, to_other_core(): lax.ppermute(array, 'core', [(c, CORES - 1 - c) for c in range(CORES)])  4.88 us
  transfers between devices with their start and end apart: 4, of which 3 were waited for; matrix products, arithmetic and copies ran while one was open for 2% of the time, Pallas kernels for 13%

profile of v6, /device:TPU:1, one launch (start us, length us, event | category | flops | bytes accessed | tf_op | source)
XLA Modules:
  0.0 121.9 jit_solution(74569701359027463)
XLA Ops:
  0.6 2.3 %shard_map.78 = bf16[32,72,128]{2,1,0:T(8,128)(2,1)} custom-call(bf16[64,768]{1,0:T(8,128)(2,1)} %bitcast.7, bf16[768,128]{1,0:T(8,128)(2,1)} %proj_ref.3, s32[2,128]{1,0:T(2,128)} %refs_2_.1, s32[2,32,128]{2,1,0:T(8,128)} %bitcast.9, f32[2,128]{1,0:T(2,128)} %refs_4_.1), custom_call_target="tpu_custom_call" | custom-call | tf_op jit(solution)/shard_map/pallas_call | solution.py:363
  3.0 11.9 %all-to-all-start = ((bf16[32,72,128]{2,1,0:T(8,128)(2,1)}), bf16[32,72,128]{2,1,0:T(8,128)(2,1)S(1)}, u32[]{:S(2)}, u32[]{:S(2)}) async-start(bf16[32,72,128]{2,1,0:T(8,128)(2,1)} %shard_map.78), calls=%async_computation | async-start | bytes 1179648 | tf_op jit(solution)/shard_map/all_to_all | solution.py:340
  14.9 2.1 %copy.11.hidden_ref.refs_1_ = bf16[8,180,768]{2,1,0:T(8,128)(2,1)S(1)} copy(bf16[8,180,768]{2,0,1:T(8,128)(2,1)} %param.7) | data formatting | bytes 4423680 | tf_op args[1]
  17.0 0.9 shard_map.77
  17.9 1.0 copy-done.4
  18.8 1.0 copy-done.5
  19.9 10.3 %all-to-all-done.refs_1_.refs_4_ = bf16[32,72,128]{2,1,0:T(8,128)(2,1)S(1)} async-done(((bf16[32,72,128]{2,1,0:T(8,128)(2,1)}), bf16[32,72,128]{2,1,0:T(8,128)(2,1)S(1)}, u32[]{:S(2)}, u32[]{:S(2)}) %all-to-all-start) | async-done | bytes 589856 | tf_op jit(solution)/shard_map/all_to_all | solution.py:340
  30.1 4.1 %collective-permute-start = (bf16[32,72,128]{2,1,0:T(8,128)(2,1)S(1)}, bf16[32,72,128]{2,1,0:T(8,128)(2,1)}, u32[]{:S(2)}, u32[]{:S(2)}) collective-permute-start(bf16[32,72,128]{2,1,0:T(8,128)(2,1)S(1)} %all-to-all-done.refs_1_.refs_4_), channel_id=1, source_target_pairs={{0,4},{4,0},{1,5},{5,1},{2,6},{6,2},{3,7},{7,3},{8,12},{12,8},{9,1... | collective-permute-start | bytes 1769480 | tf_op jit(solution)/shard_map/ppermute | solution.py:344
  34.3 3.2 %shard_map.79 = (f32[32,128]{1,0:T(8,128)S(1)}, bf16[32,5,32,128]{3,2,1,0:T(8,128)(2,1)S(1)}, f32[32,128]{1,0:T(8,128)S(1)}, f32[1,1,128]{2,1,0:T(1,128)S(1)}) custom-call(s32[1]{0:T(128)} %bitcast.refs_0_, bf16[32,72,128]{2,1,0:T(8,128)(2,1)S(1)} %all-to-all-done.refs_1_.refs_4_, bf16[8,256,128]{2,1,0:T(8,128)(2,1)S(1)} %get-tuple-element.24.refs_2_), custom_call_target="tpu_custom_call" | custom-call | tf_op jit(solution)/shard_map/pallas_call | solution.py:363
  37.5 4.5 %shard_map.80 = (f32[32,128]{1,0:T(8,128)S(1)}, bf16[32,5,32,128]{3,2,1,0:T(8,128)(2,1)S(1)}, f32[32,128]{1,0:T(8,128)S(1)}, f32[64,1,128]{2,1,0:T(1,128)S(1)}, bf16[2,32,72,128]{3,2,1,0:T(8,128)(2,1)S(1)}) custom-call(s32[1]{0:T(128)} %bitcast.refs_0_, bf16[32,72,128]{2,1,0:T(8,128)(2,1)} %collective-permute-done.refs_1_, ...), custom_call_target="tpu_custom_call" | custom-call | tf_op jit(solution)/shard_map/pallas_call | solution.py:363
  42.0 14.8 %all_to_all.30.refs_1_.refs_4_ = f32[64,1,128]{2,1,0:T(1,128)S(1)} all-to-all(f32[64,1,128]{2,1,0:T(1,128)S(1)} %get-tuple-element.26), channel_id=1, replica_groups=mesh['x'=4,'z'=8,'core'=2,'rep'=4] {'x','z','core'}, dimensions={0} | all-to-all | bytes 65536 | tf_op jit(solution)/shard_map/all_to_all | solution.py:340
  56.8 0.7 shard_map.82
  57.5 0.8 collective-permute-start.1
  58.3 0.7 shard_map.81.left_ref
  59.0 0.8 collective-permute-done.1.right_ref
  59.8 0.9 shard_map.83
  60.7 4.1 %all-to-all-start.2 = ((bf16[32,64,128]{2,1,0:T(8,128)(2,1)}), bf16[32,64,128]{2,1,0:T(8,128)(2,1)S(1)}, u32[]{:S(2)}, u32[]{:S(2)}) async-start(bf16[32,64,128]{2,1,0:T(8,128)(2,1)} %shard_map.83), calls=%async_computation.2 | async-start | bytes 1048576 | tf_op jit(solution)/shard_map/all_to_all | solution.py:340
  64.8 10.9 %shard_map.84 = (bf16[180,8,128]{2,1,0:T(8,128)(2,1)}, f32[128,768]{1,0:T(8,128)}) custom-call(s32[1]{0:T(128)} %bitcast.refs_0_, bf16[8,180,768]{2,1,0:T(8,128)(2,1)} %copy-done, f32[8,256,128]{2,1,0:T(8,128)} %copy-done.4, f32[8,256,128]{2,1,0:T(8,128)} %copy-done.5, f32[64,1,128]{2,1,0:T(1,128)} %copy-done.6, bf16[2,32,72,128]{3,2,1,0:T(8,128)(2,1)} %copy-done.3, ...), custom_call_target="tpu_custom_call" | custom-call | tf_op jit(solution)/shard_map/pallas_call | solution.py:363
  75.8 1.0 copy-done.7
  76.8 2.8 %all-to-all-done.2.parts_ref = bf16[32,64,128]{2,1,0:T(8,128)(2,1)S(1)} async-done(((bf16[32,64,128]{2,1,0:T(8,128)(2,1)}), bf16[32,64,128]{2,1,0:T(8,128)(2,1)S(1)}, u32[]{:S(2)}, u32[]{:S(2)}) %all-to-all-start.2) | async-done | bytes 524320 | tf_op jit(solution)/shard_map/all_to_all | solution.py:340
  80.2 16.3 %all_to_all.31 = bf16[32,24,128]{2,1,0:T(8,128)(2,1)S(1)} all-to-all(bf16[32,24,128]{2,1,0:T(8,128)(2,1)S(1)} %shard_map.86), channel_id=1, replica_groups=mesh['x'=4,'z'=8,'core'=2,'rep'=4] {'x','core','rep'}, dimensions={0} | all-to-all | bytes 393216 | tf_op jit(solution)/shard_map/all_to_all | solution.py:340
  96.5 11.0 %all_to_all.32 = bf16[8,24,128]{2,1,0:T(8,128)(2,1)S(1)} all-to-all(bf16[8,24,128]{2,1,0:T(8,128)(2,1)S(1)} %broadcast_in_dim.4), channel_id=1, replica_groups=mesh['x'=4,'z'=8,'core'=2,'rep'=4] {'z'}, dimensions={0} | all-to-all | bytes 98304 | tf_op jit(solution)/shard_map/all_to_all | solution.py:340
  107.6 13.5 %all_to_all.33 = bf16[32,24,128]{2,1,0:T(8,128)(2,1)S(1)} all-to-all(bf16[32,24,128]{2,1,0:T(8,128)(2,1)S(1)} %broadcast_in_dim.5), channel_id=1, replica_groups=mesh['x'=4,'z'=8,'core'=2,'rep'=4] {'x','core','rep'}, dimensions={0} | all-to-all | bytes 393216 | tf_op jit(solution)/shard_map/all_to_all | solution.py:340
  121.1 0.8 bitcast_convert_fusion
  (27 shorter events, 0.8 us)
Async XLA Ops:
  3.0 27.2 %all-to-all-start = ((bf16[32,72,128]{2,1,0:T(8,128)(2,1)}), bf16[32,72,128]{2,1,0:T(8,128)(2,1)S(1)}, u32[]{:S(2)}, u32[]{:S(2)}) async-start(bf16[32,72,128]{2,1,0:T(8,128)(2,1)} %shard_map.78), calls=%async_computation | async-start | bytes 1179648 | tf_op jit(solution)/shard_map/all_to_all | solution.py:340
  14.8 2.1 %copy-start.1 = (bf16[768,128]{1,0:T(8,128)(2,1)S(1)}, bf16[768,128]{1,0:T(8,128)(2,1)}, u32[]{:S(2)}) copy-start(bf16[768,128]{1,0:T(8,128)(2,1)} %proj_ref.3) | copy-start | bytes 589828
  17.0 20.5 %copy-start = (bf16[8,180,768]{2,1,0:T(8,128)(2,1)}, bf16[8,180,768]{2,1,0:T(8,128)(2,1)S(1)}, u32[]{:S(2)}) copy-start(bf16[8,180,768]{2,1,0:T(8,128)(2,1)S(1)} %copy.11.hidden_ref.refs_1_) | copy-start | bytes 6635524
  17.9 1.0 copy-start.4
  18.8 1.0 copy-start.5
  30.1 7.3 %collective-permute-start = (bf16[32,72,128]{2,1,0:T(8,128)(2,1)S(1)}, bf16[32,72,128]{2,1,0:T(8,128)(2,1)}, u32[]{:S(2)}, u32[]{:S(2)}) collective-permute-start(bf16[32,72,128]{2,1,0:T(8,128)(2,1)S(1)} %all-to-all-done.refs_1_.refs_4_), channel_id=1, source_target_pairs={{0,4},{4,0},{1,5},{5,1},{2,6},{6,2},{3,7},{7,3},{8,12},{12,8},{9,1... | collective-permute-start | bytes 1769480 | tf_op jit(solution)/shard_map/ppermute | solution.py:344
  37.4 20.8 %copy-start.9 = (f32[32,128]{1,0:T(8,128)}, f32[32,128]{1,0:T(8,128)S(1)}, u32[]{:S(2)}) copy-start(f32[32,128]{1,0:T(8,128)S(1)} %get-tuple-element.28.refs_3_.refs_6_) | copy-start | bytes 49156
  42.0 17.0 %copy-start.3 = (bf16[2,32,72,128]{3,2,1,0:T(8,128)(2,1)}, bf16[2,32,72,128]{3,2,1,0:T(8,128)(2,1)S(1)}, u32[]{:S(2)}) copy-start(bf16[2,32,72,128]{3,2,1,0:T(8,128)(2,1)S(1)} %get-tuple-element.34.refs_5_) | copy-start | bytes 3538948
  42.0 17.0 %copy-start.10 = (f32[32,128]{1,0:T(8,128)}, f32[32,128]{1,0:T(8,128)S(1)}, u32[]{:S(2)}) copy-start(f32[32,128]{1,0:T(8,128)S(1)} %get-tuple-element.31.refs_3_.refs_7_) | copy-start | bytes 49156
  56.8 2.2 %copy-start.6 = (f32[64,1,128]{2,1,0:T(1,128)}, f32[64,1,128]{2,1,0:T(1,128)S(1)}, u32[]{:S(2)}) copy-start(f32[64,1,128]{2,1,0:T(1,128)S(1)} %all_to_all.30.refs_1_.refs_4_) | copy-start | bytes 98308
  57.5 2.3 %collective-permute-start.1 = (bf16[32,64,128]{2,1,0:T(8,128)(2,1)S(1)}, bf16[32,64,128]{2,1,0:T(8,128)(2,1)S(1)}, u32[]{:S(2)}, u32[]{:S(2)}) collective-permute-start(bf16[32,64,128]{2,1,0:T(8,128)(2,1)S(1)} %shard_map.82), channel_id=1, source_target_pairs={{0,4},{4,0},{1,5},{5,1},{2,6},{6,2},{3,7},{7,3},{8,12},{12,8},{9,1... | collective-permute-start | bytes 1572872 | tf_op jit(solution)/shard_map/ppermute | solution.py:344
  60.7 18.8 %all-to-all-start.2 = ((bf16[32,64,128]{2,1,0:T(8,128)(2,1)}), bf16[32,64,128]{2,1,0:T(8,128)(2,1)S(1)}, u32[]{:S(2)}, u32[]{:S(2)}) async-start(bf16[32,64,128]{2,1,0:T(8,128)(2,1)} %shard_map.83), calls=%async_computation.2 | async-start | bytes 1048576 | tf_op jit(solution)/shard_map/all_to_all | solution.py:340
  64.8 14.7 %copy-start.2 = (bf16[768,128]{1,0:T(8,128)(2,1)S(1)}, bf16[768,128]{1,0:T(8,128)(2,1)}, u32[]{:S(2)}) copy-start(bf16[768,128]{1,0:T(8,128)(2,1)} %proj_ref.3) | copy-start | bytes 589828
  64.8 14.7 %copy-start.8 = (bf16[2,32,768]{2,1,0:T(8,128)(2,1)S(1)}, bf16[2,32,768]{2,1,0:T(8,128)(2,1)}, u32[]{:S(2)}) copy-start(bf16[2,32,768]{2,1,0:T(8,128)(2,1)} %param.6) | copy-start | bytes 294916
  75.8 1.0 copy-start.7

commit v7 on v6

--- a/solution.py
+++ b/solution.py
@@ -45,8 +45,6 @@
     query_len = pos_ref.shape[1]
     per_row = emb_dim // query_len
     unit, _ = unit_rows(jnp.dot(query_ref[...], proj_ref[...], preferred_element_type=F32))
-    emb = unit.astype(BF16)
-    send_ref[:, : emb.shape[0], :] = jnp.broadcast_to(emb[None], (chips,) + emb.shape)
     target = jnp.exp(teacher_ref[...])
     target = target / jnp.sum(target, axis=-1, keepdims=True)
     high = target.astype(BF16).astype(F32)
@@ -88,7 +86,8 @@
     for c in range(CORES):
         for r in range(PER_CORE):
             meta_ref[:, c * PER_CORE + r, :] = meta[c][:, r * emb_dim : (r + 1) * emb_dim]
-    send_ref[:, emb.shape[0] :, :] = meta_ref[...].astype(BF16)
+    wide = jnp.broadcast_to(unit[None], (chips,) + unit.shape)
+    send_ref[...] = jnp.concatenate([wide, meta_ref[...]], axis=1).astype(BF16)
 
 
 def embed_kernel(hidden_ref, proj_ref, emb_ref, unit_ref, inverse_ref):
@@ -106,15 +105,15 @@
     return pltpu.roll(extra, lanes - query_len - name * SLOTS, 1)
 
 
-def picked(spots_ref, extra_ref, group, query_len, capacity):
-    spots = spots_ref[pl.ds(pl.multiple_of(group * GROUP, GROUP), GROUP), :].T
-    extra = extra_ref[pl.ds(pl.multiple_of(group * GROUP, GROUP), GROUP), :].T
+def picked(spots_ref, extra_ref, group, query_len, capacity, size=GROUP):
+    spots = spots_ref[pl.ds(pl.multiple_of(group * size, size), size), :].T
+    extra = extra_ref[pl.ds(pl.multiple_of(group * size, size), size), :].T
     both = jnp.concatenate([spots, extra[:query_len]], axis=0)
     return [both[k * query_len : (k + 1) * query_len] for k in range(capacity)]
 
 
 def unpack(core, recv_ref, rows, both_ref, spots_ref, extra_ref, code_ref, scalar_ref, sem):
-    both_ref[...] = recv_ref[:, rows:, :].astype(F32)
+    both_ref[...] = recv_ref[...].astype(F32)[:, rows:, :]
     spots_ref[...] = jnp.where(core == 0, both_ref[:, 0, :], both_ref[:, PER_CORE, :])
     extra = jnp.where(core == 0, both_ref[:, 1, :], both_ref[:, PER_CORE + 1, :])
     extra_ref[...] = extra
@@ -137,11 +136,9 @@
         so_far_ref, near_ref, *refs = refs
     extra_ref, token_ref, exp_ref, part_ref, *refs = refs
     if other:
-        kept_ref, *refs, keep_sem = refs
-        keeps = []
-        for n, source in enumerate((near_ref, recv_ref)):
-            keeps.append(pltpu.make_async_copy(source, kept_ref.at[n], keep_sem.at[n]))
-            keeps[n].start()
+        kept_ref, *refs = refs
+        kept_ref[0] = near_ref[...]
+        kept_ref[1] = recv_ref[...]
     both_ref, spots_ref, code_ref, acc_ref, scalar_ref, sem = refs
     chips, _, emb_dim = recv_ref.shape
     queries, query_len = block
@@ -153,21 +150,16 @@
     copy.wait()
     lane = iota((query_len, WIDE), 1).astype(F32)
 
-    def one_group(group, carry):
-        spots = picked(spots_ref, extra_ref, group, query_len, capacity)
-        for step in range(GROUP):
-            d = group * GROUP + step
-            for k in range(capacity):
-                p, j = slot_code(scalar_ref, d, k, query_len, queries)
-                mask = jnp.where(spots[k][:, step : step + 1] == lane, 1.0, 0.0).astype(BF16)
-                token = jnp.dot(mask, emb_ref[p], preferred_element_type=F32)
-                token_ref[d, k] = token.astype(BF16)
-                start = pl.multiple_of(j * query_len, query_len)
-                query = recv_ref[d, pl.ds(start, query_len), :].astype(F32)
-                acc_ref[k, pl.ds(d, 1), :] = jnp.sum(token * query, axis=0, keepdims=True)
-        return carry
-
-    lax.fori_loop(0, chips // GROUP, one_group, 0)
+    spots = picked(spots_ref, extra_ref, 0, query_len, capacity, chips)
+    for d in range(chips):
+        for k in range(capacity):
+            p, j = slot_code(scalar_ref, d, k, query_len, queries)
+            mask = jnp.where(spots[k][:, d : d + 1] == lane, 1.0, 0.0).astype(BF16)
+            token = jnp.dot(mask, emb_ref[p], preferred_element_type=F32)
+            token_ref[d, k] = token.astype(BF16)
+            start = pl.multiple_of(j * query_len, query_len)
+            query = recv_ref[d, pl.ds(start, query_len), :].astype(F32)
+            acc_ref[k, d : d + 1, :] = jnp.sum(token * query, axis=0, keepdims=True)
     shape = (chips, emb_dim)
     at = iota(shape, 1)
     extra = extra_ref[...]
@@ -186,9 +178,6 @@
     if other:
         total = total + so_far_ref[0]
     part_ref[...] = jnp.broadcast_to(total[None], part_ref.shape)
-    if other:
-        for keep in keeps:
-            keep.wait()
 
 
 def slot_weights(capacity, queries, query_len, neg, core, other, sums, extra, exps):
@@ -238,10 +227,10 @@
     kept_ref, *refs = refs
     halves = [(kept_ref.at[h], refs[h]) for h in range(CORES)]
     grad_ref, term_ref, table_ref, total_ref, weight_ref, *refs = refs[CORES:]
-    order_ref, own_ref, unit_own_ref, inverse_own_ref, own_sem, *refs = refs
+    order_ref, unit_own_ref, inverse_own_ref, own_sem, *refs = refs
     loads = []
     for n, (source, target) in enumerate(
-        ((hidden_ref, own_ref), (unit_ref, unit_own_ref), (inverse_ref, inverse_own_ref))
+        ((unit_ref, unit_own_ref), (inverse_ref, inverse_own_ref))
     ):
         loads.append(pltpu.make_async_copy(source, target, own_sem.at[n]))
         loads[n].start()
@@ -314,7 +303,7 @@
         raw_grad = (grad * inverse_own_ref[p][:pass_len]).astype(BF16)
         order_ref[:, p, :] = raw_grad.astype(F32)
         term = term + lax.dot_general(
-            raw_grad, own_ref[p], (((0,), (0,)), ((), ())), preferred_element_type=F32
+            raw_grad, hidden_ref[p], (((0,), (0,)), ((), ())), preferred_element_type=F32
         )
     term_ref[...] = term
     grad_ref[...] = order_ref[...].astype(BF16)
@@ -418,8 +407,7 @@
                 pltpu.VMEM((capacity,) + slot_shape, F32),
                 pltpu.SMEM(slot_shape, jnp.int32),
                 pltpu.SemaphoreType.DMA,
-            ]
-            + [pltpu.SemaphoreType.DMA((CORES,))] * other,
+            ],
             core,
             recv,
             emb,
@@ -464,10 +452,9 @@
         + [
             pltpu.VMEM((CORES, capacity) + slot_shape, F32),
             pltpu.VMEM((pass_len, pass_count, emb_dim), F32),
-            pltpu.VMEM(passage_hidden.shape, BF16),
             pltpu.VMEM(wide_shape, F32),
             pltpu.VMEM(wide_shape, F32),
-            pltpu.SemaphoreType.DMA((3,)),
+            pltpu.SemaphoreType.DMA((2,)),
             pltpu.VMEM((CORES,) + meta_shape, F32),
             pltpu.VMEM((CORES,) + slot_shape, F32),
             pltpu.VMEM((CORES,) + slot_shape, F32),
@@ -484,7 +471,7 @@
         halves[0][1],
         halves[1][1],
         scalars=(0,),
-        streamed=(1, 2, 3),
+        streamed=(2, 3),
         mb=56,
     )
     term = call(copy_kernel, [shape(term.shape, F32)], [], term, mb=8)

time: 122 us -> 122 us (level)
  no operation moved by 1% of the time
where the time goes in v7:
time: 122 us; the launch traced here: 121 us
  blocking collectives  55.6 us (46%)
  Pallas kernels  24.8 us (20%)
  starting transfers between devices  20.8 us (17%)
  waiting for transfers between devices  13.1 us (11%)
  local copies, waits for them, and re-layouts  5.15 us (4%)
    all_to_all x4, blocking collectives, swap(): return lax.all_to_all(array, axes, split_axis=0, concat_axis=0, tiled=True)  55.6 us
    pallas_call x10, Pallas kernels, call(): pl.pallas_call(kernel, out_shape=outs, in_specs=[SMEM if n in scalars els...  24.8 us
    all_to_all x2, starting transfers between devices, swap(): return lax.all_to_all(array, axes, split_axis=0, concat_axis=0, tiled=True)  15.9 us
    all_to_all x2, waiting for transfers between devices, swap(): return lax.all_to_all(array, axes, split_axis=0, concat_axis=0, tiled=True)  12.3 us
    unnamed x23, local copies, waits for them, and re-layouts  5.11 us
    ppermute x2, starting transfers between devices, to_other_core(): lax.ppermute(array, 'core', [(c, CORES - 1 - c) for c in range(CORES)])  4.88 us
  transfers between devices with their start and end apart: 4, of which 3 were waited for; matrix products, arithmetic and copies ran while one was open for 2% of the time, Pallas kernels for 13%

profile of v7, /device:TPU:1, one launch (start us, length us, event | category | flops | bytes accessed | tf_op | source)
XLA Modules:
  0.0 121.1 jit_solution(1944517106519163779)
XLA Ops:
  0.6 2.3 %shard_map.78 = bf16[32,72,128]{2,1,0:T(8,128)(2,1)} custom-call(bf16[64,768]{1,0:T(8,128)(2,1)} %bitcast.7, bf16[768,128]{1,0:T(8,128)(2,1)} %proj_ref.3, s32[2,128]{1,0:T(2,128)} %refs_2_.1, s32[2,32,128]{2,1,0:T(8,128)} %bitcast.9, f32[2,128]{1,0:T(2,128)} %refs_4_.1), custom_call_target="tpu_custom_call" | custom-call | tf_op jit(solution)/shard_map/pallas_call | solution.py:352
  3.0 11.9 %all-to-all-start = ((bf16[32,72,128]{2,1,0:T(8,128)(2,1)}), bf16[32,72,128]{2,1,0:T(8,128)(2,1)S(1)}, u32[]{:S(2)}, u32[]{:S(2)}) async-start(bf16[32,72,128]{2,1,0:T(8,128)(2,1)} %shard_map.78), calls=%async_computation | async-start | bytes 1179648 | tf_op jit(solution)/shard_map/all_to_all | solution.py:329
  14.9 2.1 %copy.11.hidden_ref.refs_1_ = bf16[8,180,768]{2,1,0:T(8,128)(2,1)S(1)} copy(bf16[8,180,768]{2,0,1:T(8,128)(2,1)} %param.7) | data formatting | bytes 4423680 | tf_op args[1]
  17.0 0.9 shard_map.77
  17.9 1.0 copy-done.4
  18.8 1.0 copy-done.5
  19.9 10.3 %all-to-all-done.refs_1_.refs_4_ = bf16[32,72,128]{2,1,0:T(8,128)(2,1)S(1)} async-done(((bf16[32,72,128]{2,1,0:T(8,128)(2,1)}), bf16[32,72,128]{2,1,0:T(8,128)(2,1)S(1)}, u32[]{:S(2)}, u32[]{:S(2)}) %all-to-all-start) | async-done | bytes 589856 | tf_op jit(solution)/shard_map/all_to_all | solution.py:329
  30.1 4.1 %collective-permute-start = (bf16[32,72,128]{2,1,0:T(8,128)(2,1)S(1)}, bf16[32,72,128]{2,1,0:T(8,128)(2,1)}, u32[]{:S(2)}, u32[]{:S(2)}) collective-permute-start(bf16[32,72,128]{2,1,0:T(8,128)(2,1)S(1)} %all-to-all-done.refs_1_.refs_4_), channel_id=1, source_target_pairs={{0,4},{4,0},{1,5},{5,1},{2,6},{6,2},{3,7},{7,3},{8,12},{12,8},{9,1... | collective-permute-start | bytes 1769480 | tf_op jit(solution)/shard_map/ppermute | solution.py:333
  34.3 2.9 %shard_map.79 = (f32[32,128]{1,0:T(8,128)S(1)}, bf16[32,5,32,128]{3,2,1,0:T(8,128)(2,1)S(1)}, f32[32,128]{1,0:T(8,128)S(1)}, f32[1,1,128]{2,1,0:T(1,128)S(1)}) custom-call(s32[1]{0:T(128)} %bitcast.refs_0_, bf16[32,72,128]{2,1,0:T(8,128)(2,1)S(1)} %all-to-all-done.refs_1_.refs_4_, bf16[8,256,128]{2,1,0:T(8,128)(2,1)S(1)} %get-tuple-element.24.refs_2_), custom_call_target="tpu_custom_call" | custom-call | tf_op jit(solution)/shard_map/pallas_call | solution.py:352
  37.2 4.0 %shard_map.80 = (f32[32,128]{1,0:T(8,128)S(1)}, bf16[32,5,32,128]{3,2,1,0:T(8,128)(2,1)S(1)}, f32[32,128]{1,0:T(8,128)S(1)}, f32[64,1,128]{2,1,0:T(1,128)S(1)}, bf16[2,32,72,128]{3,2,1,0:T(8,128)(2,1)S(1)}) custom-call(s32[1]{0:T(128)} %bitcast.refs_0_, bf16[32,72,128]{2,1,0:T(8,128)(2,1)} %collective-permute-done.refs_1_, ...), custom_call_target="tpu_custom_call" | custom-call | tf_op jit(solution)/shard_map/pallas_call | solution.py:352
  41.2 14.8 %all_to_all.30.refs_1_.refs_4_ = f32[64,1,128]{2,1,0:T(1,128)S(1)} all-to-all(f32[64,1,128]{2,1,0:T(1,128)S(1)} %get-tuple-element.26), channel_id=1, replica_groups=mesh['x'=4,'z'=8,'core'=2,'rep'=4] {'x','z','core'}, dimensions={0} | all-to-all | bytes 65536 | tf_op jit(solution)/shard_map/all_to_all | solution.py:329
  56.0 0.7 shard_map.82
  56.7 0.8 collective-permute-start.1
  57.5 0.7 shard_map.81.left_ref
  58.2 0.8 collective-permute-done.1.right_ref
  59.0 0.9 shard_map.83
  60.0 4.1 %all-to-all-start.2 = ((bf16[32,64,128]{2,1,0:T(8,128)(2,1)}), bf16[32,64,128]{2,1,0:T(8,128)(2,1)S(1)}, u32[]{:S(2)}, u32[]{:S(2)}) async-start(bf16[32,64,128]{2,1,0:T(8,128)(2,1)} %shard_map.83), calls=%async_computation.2 | async-start | bytes 1048576 | tf_op jit(solution)/shard_map/all_to_all | solution.py:329
  64.1 11.6 %shard_map.84 = (bf16[180,8,128]{2,1,0:T(8,128)(2,1)}, f32[128,768]{1,0:T(8,128)}) custom-call(s32[1]{0:T(128)} %bitcast.refs_0_, bf16[8,180,768]{2,1,0:T(8,128)(2,1)} %copy-done, f32[8,256,128]{2,1,0:T(8,128)} %copy-done.4, f32[8,256,128]{2,1,0:T(8,128)} %copy-done.5, f32[64,1,128]{2,1,0:T(1,128)} %copy-done.6, bf16[2,32,72,128]{3,2,1,0:T(8,128)(2,1)} %copy-done.3, ...), custom_call_target="tpu_custom_call" | custom-call | tf_op jit(solution)/shard_map/pallas_call | solution.py:352
  75.7 1.0 copy-done.7
  76.7 2.1 %all-to-all-done.2.parts_ref = bf16[32,64,128]{2,1,0:T(8,128)(2,1)S(1)} async-done(((bf16[32,64,128]{2,1,0:T(8,128)(2,1)}), bf16[32,64,128]{2,1,0:T(8,128)(2,1)S(1)}, u32[]{:S(2)}, u32[]{:S(2)}) %all-to-all-start.2) | async-done | bytes 524320 | tf_op jit(solution)/shard_map/all_to_all | solution.py:329
  79.4 16.3 %all_to_all.31 = bf16[32,24,128]{2,1,0:T(8,128)(2,1)S(1)} all-to-all(bf16[32,24,128]{2,1,0:T(8,128)(2,1)S(1)} %shard_map.86), channel_id=1, replica_groups=mesh['x'=4,'z'=8,'core'=2,'rep'=4] {'x','core','rep'}, dimensions={0} | all-to-all | bytes 393216 | tf_op jit(solution)/shard_map/all_to_all | solution.py:329
  95.8 11.0 %all_to_all.32 = bf16[8,24,128]{2,1,0:T(8,128)(2,1)S(1)} all-to-all(bf16[8,24,128]{2,1,0:T(8,128)(2,1)S(1)} %broadcast_in_dim.4), channel_id=1, replica_groups=mesh['x'=4,'z'=8,'core'=2,'rep'=4] {'z'}, dimensions={0} | all-to-all | bytes 98304 | tf_op jit(solution)/shard_map/all_to_all | solution.py:329
  106.9 13.5 %all_to_all.33 = bf16[32,24,128]{2,1,0:T(8,128)(2,1)S(1)} all-to-all(bf16[32,24,128]{2,1,0:T(8,128)(2,1)S(1)} %broadcast_in_dim.5), channel_id=1, replica_groups=mesh['x'=4,'z'=8,'core'=2,'rep'=4] {'x','core','rep'}, dimensions={0} | all-to-all | bytes 393216 | tf_op jit(solution)/shard_map/all_to_all | solution.py:329
  120.3 0.8 bitcast_convert_fusion
  (27 shorter events, 0.8 us)
Async XLA Ops:
  3.0 27.2 %all-to-all-start = ((bf16[32,72,128]{2,1,0:T(8,128)(2,1)}), bf16[32,72,128]{2,1,0:T(8,128)(2,1)S(1)}, u32[]{:S(2)}, u32[]{:S(2)}) async-start(bf16[32,72,128]{2,1,0:T(8,128)(2,1)} %shard_map.78), calls=%async_computation | async-start | bytes 1179648 | tf_op jit(solution)/shard_map/all_to_all | solution.py:329
  14.8 2.1 %copy-start.1 = (bf16[768,128]{1,0:T(8,128)(2,1)S(1)}, bf16[768,128]{1,0:T(8,128)(2,1)}, u32[]{:S(2)}) copy-start(bf16[768,128]{1,0:T(8,128)(2,1)} %proj_ref.3) | copy-start | bytes 589828
  17.0 20.2 %copy-start = (bf16[8,180,768]{2,1,0:T(8,128)(2,1)}, bf16[8,180,768]{2,1,0:T(8,128)(2,1)S(1)}, u32[]{:S(2)}) copy-start(bf16[8,180,768]{2,1,0:T(8,128)(2,1)S(1)} %copy.11.hidden_ref.refs_1_) | copy-start | bytes 6635524
  17.9 1.0 copy-start.4
  18.8 1.0 copy-start.5
  30.1 7.0 %collective-permute-start = (bf16[32,72,128]{2,1,0:T(8,128)(2,1)S(1)}, bf16[32,72,128]{2,1,0:T(8,128)(2,1)}, u32[]{:S(2)}, u32[]{:S(2)}) collective-permute-start(bf16[32,72,128]{2,1,0:T(8,128)(2,1)S(1)} %all-to-all-done.refs_1_.refs_4_), channel_id=1, source_target_pairs={{0,4},{4,0},{1,5},{5,1},{2,6},{6,2},{3,7},{7,3},{8,12},{12,8},{9,1... | collective-permute-start | bytes 1769480 | tf_op jit(solution)/shard_map/ppermute | solution.py:333
  37.1 20.4 %copy-start.9 = (f32[32,128]{1,0:T(8,128)}, f32[32,128]{1,0:T(8,128)S(1)}, u32[]{:S(2)}) copy-start(f32[32,128]{1,0:T(8,128)S(1)} %get-tuple-element.28.refs_3_.refs_6_) | copy-start | bytes 49156
  41.2 17.0 %copy-start.3 = (bf16[2,32,72,128]{3,2,1,0:T(8,128)(2,1)}, bf16[2,32,72,128]{3,2,1,0:T(8,128)(2,1)S(1)}, u32[]{:S(2)}) copy-start(bf16[2,32,72,128]{3,2,1,0:T(8,128)(2,1)S(1)} %get-tuple-element.34.refs_5_) | copy-start | bytes 3538948
  41.2 17.0 %copy-start.10 = (f32[32,128]{1,0:T(8,128)}, f32[32,128]{1,0:T(8,128)S(1)}, u32[]{:S(2)}) copy-start(f32[32,128]{1,0:T(8,128)S(1)} %get-tuple-element.31.refs_3_.refs_7_) | copy-start | bytes 49156
  56.0 2.2 %copy-start.6 = (f32[64,1,128]{2,1,0:T(1,128)}, f32[64,1,128]{2,1,0:T(1,128)S(1)}, u32[]{:S(2)}) copy-start(f32[64,1,128]{2,1,0:T(1,128)S(1)} %all_to_all.30.refs_1_.refs_4_) | copy-start | bytes 98308
  56.7 2.3 %collective-permute-start.1 = (bf16[32,64,128]{2,1,0:T(8,128)(2,1)S(1)}, bf16[32,64,128]{2,1,0:T(8,128)(2,1)S(1)}, u32[]{:S(2)}, u32[]{:S(2)}) collective-permute-start(bf16[32,64,128]{2,1,0:T(8,128)(2,1)S(1)} %shard_map.82), channel_id=1, source_target_pairs={{0,4},{4,0},{1,5},{5,1},{2,6},{6,2},{3,7},{7,3},{8,12},{12,8},{9,1... | collective-permute-start | bytes 1572872 | tf_op jit(solution)/shard_map/ppermute | solution.py:333
  60.0 18.8 %all-to-all-start.2 = ((bf16[32,64,128]{2,1,0:T(8,128)(2,1)}), bf16[32,64,128]{2,1,0:T(8,128)(2,1)S(1)}, u32[]{:S(2)}, u32[]{:S(2)}) async-start(bf16[32,64,128]{2,1,0:T(8,128)(2,1)} %shard_map.83), calls=%async_computation.2 | async-start | bytes 1048576 | tf_op jit(solution)/shard_map/all_to_all | solution.py:329
  64.0 14.7 %copy-start.2 = (bf16[768,128]{1,0:T(8,128)(2,1)S(1)}, bf16[768,128]{1,0:T(8,128)(2,1)}, u32[]{:S(2)}) copy-start(bf16[768,128]{1,0:T(8,128)(2,1)} %proj_ref.3) | copy-start | bytes 589828
  64.0 14.7 %copy-start.8 = (bf16[2,32,768]{2,1,0:T(8,128)(2,1)S(1)}, bf16[2,32,768]{2,1,0:T(8,128)(2,1)}, u32[]{:S(2)}) copy-start(bf16[2,32,768]{2,1,0:T(8,128)(2,1)} %param.6) | copy-start | bytes 294916
  75.7 1.0 copy-start.7

commit v8 on v7

--- a/solution.py
+++ b/solution.py
@@ -292,7 +292,8 @@
                 )
             return carry
 
-        lax.fori_loop(0, chips // GROUP, one_group, 0)
+        for group in range(chips // GROUP):
+            one_group(group, 0)
     for load in loads:
         load.wait()
     term = jnp.zeros(term_ref.shape, F32)

time: 122 us -> 122 us (level)
  no operation moved by 1% of the time
where the time goes in v8:
time: 122 us; the launch traced here: 121 us
  blocking collectives  55.6 us (46%)
  Pallas kernels  24 us (20%)
  starting transfers between devices  20.8 us (17%)
  waiting for transfers between devices  13.9 us (11%)
  local copies, waits for them, and re-layouts  5.15 us (4%)
    all_to_all x4, blocking collectives, swap(): return lax.all_to_all(array, axes, split_axis=0, concat_axis=0, tiled=True)  55.6 us
    pallas_call x10, Pallas kernels, call(): pl.pallas_call(kernel, out_shape=outs, in_specs=[SMEM if n in scalars els...  24 us
    all_to_all x2, starting transfers between devices, swap(): return lax.all_to_all(array, axes, split_axis=0, concat_axis=0, tiled=True)  15.9 us
    all_to_all x2, waiting for transfers between devices, swap(): return lax.all_to_all(array, axes, split_axis=0, concat_axis=0, tiled=True)  13.1 us
    unnamed x23, local copies, waits for them, and re-layouts  5.11 us
    ppermute x2, starting transfers between devices, to_other_core(): lax.ppermute(array, 'core', [(c, CORES - 1 - c) for c in range(CORES)])  4.88 us
  transfers between devices with their start and end apart: 4, of which 3 were waited for; matrix products, arithmetic and copies ran while one was open for 2% of the time, Pallas kernels for 13%

profile of v8, /device:TPU:1, one launch (start us, length us, event | category | flops | bytes accessed | tf_op | source)
XLA Modules:
  0.0 121.1 jit_solution(14999185604682040855)
XLA Ops:
  0.6 2.3 %shard_map.78 = bf16[32,72,128]{2,1,0:T(8,128)(2,1)} custom-call(bf16[64,768]{1,0:T(8,128)(2,1)} %bitcast.7, bf16[768,128]{1,0:T(8,128)(2,1)} %proj_ref.3, s32[2,128]{1,0:T(2,128)} %refs_2_.1, s32[2,32,128]{2,1,0:T(8,128)} %bitcast.9, f32[2,128]{1,0:T(2,128)} %refs_4_.1), custom_call_target="tpu_custom_call" | custom-call | tf_op jit(solution)/shard_map/pallas_call | solution.py:353
  3.0 11.9 %all-to-all-start = ((bf16[32,72,128]{2,1,0:T(8,128)(2,1)}), bf16[32,72,128]{2,1,0:T(8,128)(2,1)S(1)}, u32[]{:S(2)}, u32[]{:S(2)}) async-start(bf16[32,72,128]{2,1,0:T(8,128)(2,1)} %shard_map.78), calls=%async_computation | async-start | bytes 1179648 | tf_op jit(solution)/shard_map/all_to_all | solution.py:330
  14.9 2.1 %copy.11.hidden_ref.refs_1_ = bf16[8,180,768]{2,1,0:T(8,128)(2,1)S(1)} copy(bf16[8,180,768]{2,0,1:T(8,128)(2,1)} %param.7) | data formatting | bytes 4423680 | tf_op args[1]
  17.0 0.9 shard_map.77
  17.9 1.0 copy-done.4
  18.8 1.0 copy-done.5
  19.9 10.3 %all-to-all-done.refs_1_.refs_4_ = bf16[32,72,128]{2,1,0:T(8,128)(2,1)S(1)} async-done(((bf16[32,72,128]{2,1,0:T(8,128)(2,1)}), bf16[32,72,128]{2,1,0:T(8,128)(2,1)S(1)}, u32[]{:S(2)}, u32[]{:S(2)}) %all-to-all-start) | async-done | bytes 589856 | tf_op jit(solution)/shard_map/all_to_all | solution.py:330
  30.1 4.1 %collective-permute-start = (bf16[32,72,128]{2,1,0:T(8,128)(2,1)S(1)}, bf16[32,72,128]{2,1,0:T(8,128)(2,1)}, u32[]{:S(2)}, u32[]{:S(2)}) collective-permute-start(bf16[32,72,128]{2,1,0:T(8,128)(2,1)S(1)} %all-to-all-done.refs_1_.refs_4_), channel_id=1, source_target_pairs={{0,4},{4,0},{1,5},{5,1},{2,6},{6,2},{3,7},{7,3},{8,12},{12,8},{9,1... | collective-permute-start | bytes 1769480 | tf_op jit(solution)/shard_map/ppermute | solution.py:334
  34.3 2.9 %shard_map.79 = (f32[32,128]{1,0:T(8,128)S(1)}, bf16[32,5,32,128]{3,2,1,0:T(8,128)(2,1)S(1)}, f32[32,128]{1,0:T(8,128)S(1)}, f32[1,1,128]{2,1,0:T(1,128)S(1)}) custom-call(s32[1]{0:T(128)} %bitcast.refs_0_, bf16[32,72,128]{2,1,0:T(8,128)(2,1)S(1)} %all-to-all-done.refs_1_.refs_4_, bf16[8,256,128]{2,1,0:T(8,128)(2,1)S(1)} %get-tuple-element.24.refs_2_), custom_call_target="tpu_custom_call" | custom-call | tf_op jit(solution)/shard_map/pallas_call | solution.py:353
  37.2 4.0 %shard_map.80 = (f32[32,128]{1,0:T(8,128)S(1)}, bf16[32,5,32,128]{3,2,1,0:T(8,128)(2,1)S(1)}, f32[32,128]{1,0:T(8,128)S(1)}, f32[64,1,128]{2,1,0:T(1,128)S(1)}, bf16[2,32,72,128]{3,2,1,0:T(8,128)(2,1)S(1)}) custom-call(s32[1]{0:T(128)} %bitcast.refs_0_, bf16[32,72,128]{2,1,0:T(8,128)(2,1)} %collective-permute-done.refs_1_, ...), custom_call_target="tpu_custom_call" | custom-call | tf_op jit(solution)/shard_map/pallas_call | solution.py:353
  41.2 14.8 %all_to_all.30.refs_1_.refs_4_ = f32[64,1,128]{2,1,0:T(1,128)S(1)} all-to-all(f32[64,1,128]{2,1,0:T(1,128)S(1)} %get-tuple-element.26), channel_id=1, replica_groups=mesh['x'=4,'z'=8,'core'=2,'rep'=4] {'x','z','core'}, dimensions={0} | all-to-all | bytes 65536 | tf_op jit(solution)/shard_map/all_to_all | solution.py:330
  56.0 0.7 shard_map.82
  56.7 0.8 collective-permute-start.1
  57.5 0.7 shard_map.81.left_ref
  58.2 0.8 collective-permute-done.1.right_ref
  59.0 0.9 shard_map.83
  60.0 4.1 %all-to-all-start.2 = ((bf16[32,64,128]{2,1,0:T(8,128)(2,1)}), bf16[32,64,128]{2,1,0:T(8,128)(2,1)S(1)}, u32[]{:S(2)}, u32[]{:S(2)}) async-start(bf16[32,64,128]{2,1,0:T(8,128)(2,1)} %shard_map.83), calls=%async_computation.2 | async-start | bytes 1048576 | tf_op jit(solution)/shard_map/all_to_all | solution.py:330
  64.1 10.8 %shard_map.84 = (bf16[180,8,128]{2,1,0:T(8,128)(2,1)}, f32[128,768]{1,0:T(8,128)}) custom-call(s32[1]{0:T(128)} %bitcast.refs_0_, bf16[8,180,768]{2,1,0:T(8,128)(2,1)} %copy-done, f32[8,256,128]{2,1,0:T(8,128)} %copy-done.4, f32[8,256,128]{2,1,0:T(8,128)} %copy-done.5, f32[64,1,128]{2,1,0:T(1,128)} %copy-done.6, bf16[2,32,72,128]{3,2,1,0:T(8,128)(2,1)} %copy-done.3, ...), custom_call_target="tpu_custom_call" | custom-call | tf_op jit(solution)/shard_map/pallas_call | solution.py:353
  74.9 1.0 copy-done.7
  75.9 2.9 %all-to-all-done.2.parts_ref = bf16[32,64,128]{2,1,0:T(8,128)(2,1)S(1)} async-done(((bf16[32,64,128]{2,1,0:T(8,128)(2,1)}), bf16[32,64,128]{2,1,0:T(8,128)(2,1)S(1)}, u32[]{:S(2)}, u32[]{:S(2)}) %all-to-all-start.2) | async-done | bytes 524320 | tf_op jit(solution)/shard_map/all_to_all | solution.py:330
  79.4 16.3 %all_to_all.31 = bf16[32,24,128]{2,1,0:T(8,128)(2,1)S(1)} all-to-all(bf16[32,24,128]{2,1,0:T(8,128)(2,1)S(1)} %shard_map.86), channel_id=1, replica_groups=mesh['x'=4,'z'=8,'core'=2,'rep'=4] {'x','core','rep'}, dimensions={0} | all-to-all | bytes 393216 | tf_op jit(solution)/shard_map/all_to_all | solution.py:330
  95.8 11.0 %all_to_all.32 = bf16[8,24,128]{2,1,0:T(8,128)(2,1)S(1)} all-to-all(bf16[8,24,128]{2,1,0:T(8,128)(2,1)S(1)} %broadcast_in_dim.4), channel_id=1, replica_groups=mesh['x'=4,'z'=8,'core'=2,'rep'=4] {'z'}, dimensions={0} | all-to-all | bytes 98304 | tf_op jit(solution)/shard_map/all_to_all | solution.py:330
  106.9 13.5 %all_to_all.33 = bf16[32,24,128]{2,1,0:T(8,128)(2,1)S(1)} all-to-all(bf16[32,24,128]{2,1,0:T(8,128)(2,1)S(1)} %broadcast_in_dim.5), channel_id=1, replica_groups=mesh['x'=4,'z'=8,'core'=2,'rep'=4] {'x','core','rep'}, dimensions={0} | all-to-all | bytes 393216 | tf_op jit(solution)/shard_map/all_to_all | solution.py:330
  120.3 0.8 bitcast_convert_fusion
  (27 shorter events, 0.8 us)
Async XLA Ops:
  3.0 27.2 %all-to-all-start = ((bf16[32,72,128]{2,1,0:T(8,128)(2,1)}), bf16[32,72,128]{2,1,0:T(8,128)(2,1)S(1)}, u32[]{:S(2)}, u32[]{:S(2)}) async-start(bf16[32,72,128]{2,1,0:T(8,128)(2,1)} %shard_map.78), calls=%async_computation | async-start | bytes 1179648 | tf_op jit(solution)/shard_map/all_to_all | solution.py:330
  14.8 2.1 %copy-start.1 = (bf16[768,128]{1,0:T(8,128)(2,1)S(1)}, bf16[768,128]{1,0:T(8,128)(2,1)}, u32[]{:S(2)}) copy-start(bf16[768,128]{1,0:T(8,128)(2,1)} %proj_ref.3) | copy-start | bytes 589828
  17.0 20.2 %copy-start = (bf16[8,180,768]{2,1,0:T(8,128)(2,1)}, bf16[8,180,768]{2,1,0:T(8,128)(2,1)S(1)}, u32[]{:S(2)}) copy-start(bf16[8,180,768]{2,1,0:T(8,128)(2,1)S(1)} %copy.11.hidden_ref.refs_1_) | copy-start | bytes 6635524
  17.9 1.0 copy-start.4
  18.8 1.0 copy-start.5
  30.1 7.0 %collective-permute-start = (bf16[32,72,128]{2,1,0:T(8,128)(2,1)S(1)}, bf16[32,72,128]{2,1,0:T(8,128)(2,1)}, u32[]{:S(2)}, u32[]{:S(2)}) collective-permute-start(bf16[32,72,128]{2,1,0:T(8,128)(2,1)S(1)} %all-to-all-done.refs_1_.refs_4_), channel_id=1, source_target_pairs={{0,4},{4,0},{1,5},{5,1},{2,6},{6,2},{3,7},{7,3},{8,12},{12,8},{9,1... | collective-permute-start | bytes 1769480 | tf_op jit(solution)/shard_map/ppermute | solution.py:334
  37.1 20.4 %copy-start.9 = (f32[32,128]{1,0:T(8,128)}, f32[32,128]{1,0:T(8,128)S(1)}, u32[]{:S(2)}) copy-start(f32[32,128]{1,0:T(8,128)S(1)} %get-tuple-element.28.refs_3_.refs_6_) | copy-start | bytes 49156
  41.2 17.0 %copy-start.3 = (bf16[2,32,72,128]{3,2,1,0:T(8,128)(2,1)}, bf16[2,32,72,128]{3,2,1,0:T(8,128)(2,1)S(1)}, u32[]{:S(2)}) copy-start(bf16[2,32,72,128]{3,2,1,0:T(8,128)(2,1)S(1)} %get-tuple-element.34.refs_5_) | copy-start | bytes 3538948
  41.2 17.0 %copy-start.10 = (f32[32,128]{1,0:T(8,128)}, f32[32,128]{1,0:T(8,128)S(1)}, u32[]{:S(2)}) copy-start(f32[32,128]{1,0:T(8,128)S(1)} %get-tuple-element.31.refs_3_.refs_7_) | copy-start | bytes 49156
  56.0 2.2 %copy-start.6 = (f32[64,1,128]{2,1,0:T(1,128)}, f32[64,1,128]{2,1,0:T(1,128)S(1)}, u32[]{:S(2)}) copy-start(f32[64,1,128]{2,1,0:T(1,128)S(1)} %all_to_all.30.refs_1_.refs_4_) | copy-start | bytes 98308
  56.7 2.3 %collective-permute-start.1 = (bf16[32,64,128]{2,1,0:T(8,128)(2,1)S(1)}, bf16[32,64,128]{2,1,0:T(8,128)(2,1)S(1)}, u32[]{:S(2)}, u32[]{:S(2)}) collective-permute-start(bf16[32,64,128]{2,1,0:T(8,128)(2,1)S(1)} %shard_map.82), channel_id=1, source_target_pairs={{0,4},{4,0},{1,5},{5,1},{2,6},{6,2},{3,7},{7,3},{8,12},{12,8},{9,1... | collective-permute-start | bytes 1572872 | tf_op jit(solution)/shard_map/ppermute | solution.py:334
  60.0 18.8 %all-to-all-start.2 = ((bf16[32,64,128]{2,1,0:T(8,128)(2,1)}), bf16[32,64,128]{2,1,0:T(8,128)(2,1)S(1)}, u32[]{:S(2)}, u32[]{:S(2)}) async-start(bf16[32,64,128]{2,1,0:T(8,128)(2,1)} %shard_map.83), calls=%async_computation.2 | async-start | bytes 1048576 | tf_op jit(solution)/shard_map/all_to_all | solution.py:330
  64.0 14.7 %copy-start.2 = (bf16[768,128]{1,0:T(8,128)(2,1)S(1)}, bf16[768,128]{1,0:T(8,128)(2,1)}, u32[]{:S(2)}) copy-start(bf16[768,128]{1,0:T(8,128)(2,1)} %proj_ref.3) | copy-start | bytes 589828
  64.0 14.7 %copy-start.8 = (bf16[2,32,768]{2,1,0:T(8,128)(2,1)S(1)}, bf16[2,32,768]{2,1,0:T(8,128)(2,1)}, u32[]{:S(2)}) copy-start(bf16[2,32,768]{2,1,0:T(8,128)(2,1)} %param.6) | copy-start | bytes 294916
  74.9 1.0 copy-start.7
